TPU v7x, 512 devices: a whole 4x8x8 slice. The times are simulated.
512 devices in a mesh: wide: 64 (over y, z), narrow: 8 (over x, core).
Axes of the slice: x: 4, y: 8, z: 8, core: 2. Of those that a mesh axis runs over, the one named last changes fastest.
Arguments:
- right_side: float32 [8, 2048, 1024], P(None, 'wide', 'narrow'), may hold values from -6 to 6
- wet_mask: int32 [8, 2048, 1024], P(None, 'wide', 'narrow'), may hold values 0 or 1
- helmholtz: float32 [8, 2048, 1024], P(None, 'wide', 'narrow'), may hold values from 0.02 to 2
- eig_low: float32 [1], replicated, may hold values from 0.03 to 0.3
- eig_high: float32 [1], replicated, may hold values from 1.6 to 2
Outputs:
- pressure: float32 [8, 2048, 1024], P(None, 'wide', 'narrow')
- residual: float32 [8, 2048, 1024], P(None, 'wide', 'narrow')
All inputs are finite; a program needn't handle non-finite values. No bound on the sum of `wet_mask` on one device may be relied on, other than what follows from the above.
Results may differ from a plain program's by a relative error of at most 0.000044.
Values sent between devices are 32-bit elements; how exact they have to be, the bound alone decides.
No kernel may reach another device: no remote copies, remote signals or barrier semaphores. Data moves between devices by JAX's collectives and lax.ppermute only.
A program may use at most 64 MiB of HBM per device.

v0:
```python
import jax
import jax.numpy as jnp
from jax import lax
from jax.sharding import PartitionSpec as P

PRE = 2
POST = 2
CHEB = 4


def extended(array, sides, width):
    for axis, dim in sides:
        devices, length = (lax.axis_size(axis), array.shape[dim])
        up = [(i, (i + 1) % devices) for i in range(devices - 1)]
        down = [(j, i) for i, j in up]
        last = lax.slice_in_dim(array, length - width, length, axis=dim)
        initial = lax.slice_in_dim(array, 0, width, axis=dim)
        before = lax.ppermute(last, axis, up)
        after = lax.ppermute(initial, axis, down)
        array = jnp.concatenate([before, array, after], axis=dim)
    return array


def neighbours(padded):
    total = padded[2:, 1:-1, 1:-1] + padded[:-2, 1:-1, 1:-1]
    total = total + padded[1:-1, 2:, 1:-1] + padded[1:-1, :-2, 1:-1]
    total = total + padded[1:-1, 1:-1, 2:] + padded[1:-1, 1:-1, :-2]
    return total


def pad_vertical(field):
    return jnp.pad(field, ((1, 1), (0, 0), (0, 0)))


def coarsen(field):
    first, second, third = field.shape
    blocks = field.reshape(first // 2, 2, second // 2, 2, third // 2, 2)
    return jnp.sum(blocks, axis=(1, 3, 5)) * 0.125


def refine_axis(field, axis):
    length = field.shape[axis] - 2
    centre = lax.slice_in_dim(field, 1, length + 1, axis=axis)
    before = lax.slice_in_dim(field, 0, length, axis=axis)
    after = lax.slice_in_dim(field, 2, length + 2, axis=axis)
    low_half = 0.75 * centre + 0.25 * before
    high_half = 0.75 * centre + 0.25 * after
    stacked = jnp.stack((low_half, high_half), axis=axis + 1)
    shape = list(centre.shape)
    shape[axis] = 2 * length
    return stacked.reshape(shape)


def refine(padded):
    field = refine_axis(padded, 1)
    field = refine_axis(field, 2)
    return refine_axis(pad_vertical(field), 0)


def chebyshev(source, wet_c, shift_c, count_c, low_bound, high_bound, coarse_rim):
    centre_value = 0.5 * (high_bound + low_bound)
    half_width = 0.5 * (high_bound - low_bound)
    sigma_value = centre_value / half_width
    rho_value = 1.0 / sigma_value
    diag_c = wet_c * (shift_c + 0.25 * count_c) + (1.0 - wet_c)
    remain = source
    direction = remain / diag_c / centre_value
    error_c = jnp.zeros_like(source)
    for sweep in range(CHEB):
        error_c = error_c + direction
        if sweep + 1 < CHEB:
            near = neighbours(pad_vertical(coarse_rim(wet_c * direction)))
            image = (
                wet_c * ((shift_c + 0.25 * count_c) * direction - 0.25 * near)
                + (1.0 - wet_c) * direction
            )
            remain = remain - image
            rho_next = 1.0 / (2.0 * sigma_value - rho_value)
            direction = (
                rho_next * rho_value * direction + 2.0 * rho_next / half_width * remain / diag_c
            )
            rho_value = rho_next
    return error_c


def body(right_side, wet_mask, helmholtz, eig_low, eig_high):
    wet = wet_mask.astype(jnp.float32)
    wet_border = extended(wet_mask, (("wide", 1), ("narrow", 2)), 1)
    count = neighbours(pad_vertical(wet_border.astype(jnp.float32)))
    fine_diag = wet * (helmholtz + count) + (1.0 - wet)

    def fine_apply(field):
        border = extended(wet * field, (("wide", 1), ("narrow", 2)), 1)
        near = neighbours(pad_vertical(border))
        return wet * ((helmholtz + count) * field - near) + (1.0 - wet) * field

    pressure = jnp.zeros_like(right_side)
    for sweep in range(PRE):
        pressure = pressure + 0.8 * (right_side - fine_apply(pressure)) / fine_diag
    fine_res = right_side - fine_apply(pressure)
    coarse_src = coarsen(wet * fine_res)
    first, second, third = wet_mask.shape
    wet_sum = jnp.sum(
        wet_mask.reshape(first // 2, 2, second // 2, 2, third // 2, 2), axis=(1, 3, 5)
    )
    wet_c = (wet_sum >= 4).astype(jnp.float32)
    shift_c = wet_c * coarsen(helmholtz)
    low_bound = eig_low[0]
    high_bound = eig_high[0]

    def brick_rim(field):
        return extended(field, (("wide", 1), ("narrow", 2)), 1)

    count_c = neighbours(pad_vertical(brick_rim(wet_c)))
    error_c = chebyshev(coarse_src, wet_c, shift_c, count_c, low_bound, high_bound, brick_rim)
    padded = extended(error_c, (("wide", 1), ("narrow", 2)), 1)
    pressure = pressure + wet * refine(padded)
    for sweep in range(POST):
        pressure = pressure + 0.8 * (right_side - fine_apply(pressure)) / fine_diag
    residual = right_side - fine_apply(pressure)
    return (pressure, residual)


def solution(mesh):
    placed = (
        P(None, "wide", "narrow"),
        P(None, "wide", "narrow"),
        P(None, "wide", "narrow"),
        P(),
        P(),
    )
    return jax.shard_map(
        body,
        mesh=mesh,
        in_specs=placed,
        out_specs=(P(None, "wide", "narrow"), P(None, "wide", "narrow")),
        check_vma=False,
    )
```

profile of v0, /device:TPU:34, one launch (start us, length us, event | category | flops | bytes accessed | tf_op | source)
XLA Modules:
  0.0 270.7 jit_solution(12506861246588733464)
XLA Ops:
  1.4 4.3 %collective-permute-start = (s32[8,1,128]{2,1,0:T(1,128)S(1)}, s32[8,1,128]{2,1,0:T(1,128)S(1)}, u32[]{:S(2)}, u32[]{:S(2)}) collective-permute-start(s32[8,1,128]{2,1,0:T(1,128)S(1)} %get-tuple-element.45), channel_id=1, source_target_pairs={{0,8},{8,16},{16,24},{24,32},{32,40},{40,48},{48,56},{56,64},{64,7... | collective-permute-start | bytes 12296 | tf_op jit(solution)/shard_map/ppermute | solution.py:18
  5.7 8.5 %collective-permute-start.1 = (s32[8,1,128]{2,1,0:T(1,128)S(1)}, s32[8,1,128]{2,1,0:T(1,128)S(1)}, u32[]{:S(2)}, u32[]{:S(2)}) collective-permute-start(s32[8,1,128]{2,1,0:T(1,128)S(1)} %get-tuple-element.46), channel_id=1, source_target_pairs={{8,0},{16,8},{24,16},{32,24},{40,32},{48,40},{56,48},{64,56},{72,6... | collective-permute-start | bytes 12296 | tf_op jit(solution)/shard_map/ppermute | solution.py:19
  17.1 7.4 %collective-permute-start.5 = (f32[8,1,128]{2,1,0:T(1,128)S(1)}, f32[8,1,128]{2,1,0:T(1,128)S(1)}, u32[]{:S(2)}, u32[]{:S(2)}) collective-permute-start(f32[8,1,128]{2,1,0:T(1,128)S(1)} %get-tuple-element.48), channel_id=1, source_target_pairs={{8,0},{16,8},{24,16},{32,24},{40,32},{48,40},{56,48},{64,56},{72,6... | collective-permute-start | bytes 12296 | tf_op jit(solution)/shard_map/ppermute | solution.py:19
  24.5 10.5 %reshape.29 = s32[4,2,16,2,64,2]{5,4,3,2,1,0:T(8,128)} reshape(s32[8,32,128]{2,1,0:T(8,128)} %param.6) | data formatting | bytes 262144 | tf_op jit(solution)/shard_map/reshape | solution.py:104
  35.0 4.5 %reduce_sum.28 = s32[4,16,64]{2,1,0:T(8,128)S(1)} reduce(s32[4,2,16,2,64,2]{5,4,3,2,1,0:T(8,128)} %reshape.29, s32[]{:T(128)} %constant.15.clone.1), dimensions={1,3,5}, to_apply=%region_1.2 | reduce | flops 28672 | bytes 147460 | tf_op jit(solution)/shard_map/reduce_sum | solution.py:103
  50.2 3.8 %collective-permute-done.6 = f32[8,34,1]{2,1,0:T(8,128)S(1)} collective-permute-done((f32[8,34,1]{2,1,0:T(8,128)S(1)}, f32[8,34,1]{2,1,0:T(8,128)S(1)}, u32[]{:S(2)}, u32[]{:S(2)}) %collective-permute-start.6) | collective-permute-done | bytes 1120 | tf_op jit(solution)/shard_map/ppermute | solution.py:18
  56.7 7.2 %collective-permute-start.9 = (f32[8,1,128]{2,1,0:T(1,128)S(1)}, f32[8,1,128]{2,1,0:T(1,128)S(1)}, u32[]{:S(2)}, u32[]{:S(2)}) collective-permute-start(f32[8,1,128]{2,1,0:T(1,128)S(1)} %get-tuple-element.44), channel_id=1, source_target_pairs={{8,0},{16,8},{24,16},{32,24},{40,32},{48,40},{56,48},{64,56},{72,6... | collective-permute-start | bytes 12296 | tf_op jit(solution)/shard_map/ppermute | solution.py:19
  65.9 7.2 %collective-permute-start.17 = (f32[4,1,64]{2,1,0:T(1,128)S(1)}, f32[4,1,64]{2,1,0:T(1,128)S(1)}, u32[]{:S(2)}, u32[]{:S(2)}) collective-permute-start(f32[4,1,64]{2,1,0:T(1,128)S(1)} %get-tuple-element.72), channel_id=1, source_target_pairs={{8,0},{16,8},{24,16},{32,24},{40,32},{48,40},{56,48},{64,56},{72,6... | collective-permute-start | bytes 3080 | tf_op jit(solution)/shard_map/ppermute | solution.py:19
  73.1 9.8 %reshape.30 = f32[4,2,16,2,64,2]{5,4,3,2,1,0:T(8,128)} reshape(f32[8,32,128]{2,1,0:T(8,128)S(1)} %copy-done.2) | data formatting | bytes 262144 | tf_op jit(solution)/shard_map/reshape | solution.py:37
  84.2 4.0 %reduce_sum.29 = f32[4,16,64]{2,1,0:T(8,128)S(1)} reduce(f32[4,2,16,2,64,2]{5,4,3,2,1,0:T(8,128)} %reshape.30, f32[]{:T(128)} %constant.11.clone.1), dimensions={1,3,5}, to_apply=%region_2.3 | reduce | flops 28672 | bytes 147460 | tf_op jit(solution)/shard_map/reduce_sum | solution.py:38
  93.2 3.8 %collective-permute-done.10 = f32[8,34,1]{2,1,0:T(8,128)S(1)} collective-permute-done((f32[8,34,1]{2,1,0:T(8,128)S(1)}, f32[8,34,1]{2,1,0:T(8,128)S(1)}, u32[]{:S(2)}, u32[]{:S(2)}) %collective-permute-start.10) | collective-permute-done | bytes 1120 | tf_op jit(solution)/shard_map/ppermute | solution.py:18
  99.4 7.2 %collective-permute-start.13 = (f32[8,1,128]{2,1,0:T(1,128)S(1)}, f32[8,1,128]{2,1,0:T(1,128)S(1)}, u32[]{:S(2)}, u32[]{:S(2)}) collective-permute-start(f32[8,1,128]{2,1,0:T(1,128)S(1)} %get-tuple-element.42), channel_id=1, source_target_pairs={{8,0},{16,8},{24,16},{32,24},{40,32},{48,40},{56,48},{64,56},{72,6... | collective-permute-start | bytes 12296 | tf_op jit(solution)/shard_map/ppermute | solution.py:19
  121.6 9.8 %reshape.28 = f32[4,2,16,2,64,2]{5,4,3,2,1,0:T(8,128)} reshape(f32[8,32,128]{2,1,0:T(8,128)S(1)} %fusion.48) | data formatting | bytes 262144 | tf_op jit(solution)/shard_map/reshape | solution.py:37
  131.4 4.0 %reduce_sum.27 = f32[4,16,64]{2,1,0:T(8,128)S(1)} reduce(f32[4,2,16,2,64,2]{5,4,3,2,1,0:T(8,128)} %reshape.28, f32[]{:T(128)} %constant.11.clone.1), dimensions={1,3,5}, to_apply=%region_0.1 | reduce | flops 28672 | bytes 147460 | tf_op jit(solution)/shard_map/reduce_sum | solution.py:38
  137.5 7.2 %collective-permute-start.21 = (f32[4,1,64]{2,1,0:T(1,128)S(1)}, f32[4,1,64]{2,1,0:T(1,128)S(1)}, u32[]{:S(2)}, u32[]{:S(2)}) collective-permute-start(f32[4,1,64]{2,1,0:T(1,128)S(1)} %get-tuple-element.70), channel_id=1, source_target_pairs={{8,0},{16,8},{24,16},{32,24},{40,32},{48,40},{56,48},{64,56},{72,6... | collective-permute-start | bytes 3080 | tf_op jit(solution)/shard_map/ppermute | solution.py:19
  155.6 7.5 %collective-permute-start.25 = (f32[4,1,64]{2,1,0:T(1,128)S(1)}, f32[4,1,64]{2,1,0:T(1,128)S(1)}, u32[]{:S(2)}, u32[]{:S(2)}) collective-permute-start(f32[4,1,64]{2,1,0:T(1,128)S(1)} %get-tuple-element.68), channel_id=1, source_target_pairs={{8,0},{16,8},{24,16},{32,24},{40,32},{48,40},{56,48},{64,56},{72,6... | collective-permute-start | bytes 3080 | tf_op jit(solution)/shard_map/ppermute | solution.py:19
  174.0 7.5 %collective-permute-start.29 = (f32[4,1,64]{2,1,0:T(1,128)S(1)}, f32[4,1,64]{2,1,0:T(1,128)S(1)}, u32[]{:S(2)}, u32[]{:S(2)}) collective-permute-start(f32[4,1,64]{2,1,0:T(1,128)S(1)} %get-tuple-element.66), channel_id=1, source_target_pairs={{8,0},{16,8},{24,16},{32,24},{40,32},{48,40},{56,48},{64,56},{72,6... | collective-permute-start | bytes 3080 | tf_op jit(solution)/shard_map/ppermute | solution.py:19
  192.5 7.5 %collective-permute-start.33 = (f32[4,1,64]{2,1,0:T(1,128)S(1)}, f32[4,1,64]{2,1,0:T(1,128)S(1)}, u32[]{:S(2)}, u32[]{:S(2)}) collective-permute-start(f32[4,1,64]{2,1,0:T(1,128)S(1)} %get-tuple-element.64), channel_id=1, source_target_pairs={{8,0},{16,8},{24,16},{32,24},{40,32},{48,40},{56,48},{64,56},{72,6... | collective-permute-start | bytes 3080 | tf_op jit(solution)/shard_map/ppermute | solution.py:19
  203.3 3.8 %collective-permute-start.35 = (f32[4,18,1]{2,1,0:T(8,128)S(1)}, f32[4,18,1]{2,1,0:T(8,128)S(1)}, u32[]{:S(2)}, u32[]{:S(2)}) collective-permute-start(f32[4,18,1]{2,1,0:T(8,128)S(1)} %get-tuple-element.54), channel_id=1, source_target_pairs={{1,0},{2,1},{3,2},{4,3},{5,4},{6,5},{7,6},{9,8},{10,9},{11,10},{12... | collective-permute-start | bytes 872 | tf_op jit(solution)/shard_map/ppermute | solution.py:19
  211.4 7.5 %collective-permute-start.37 = (f32[8,1,128]{2,1,0:T(1,128)S(1)}, f32[8,1,128]{2,1,0:T(1,128)S(1)}, u32[]{:S(2)}, u32[]{:S(2)}) collective-permute-start(f32[8,1,128]{2,1,0:T(1,128)S(1)} %get-tuple-element.40), channel_id=1, source_target_pairs={{8,0},{16,8},{24,16},{32,24},{40,32},{48,40},{56,48},{64,56},{72,6... | collective-permute-start | bytes 12296 | tf_op jit(solution)/shard_map/ppermute | solution.py:19
  226.0 3.8 %collective-permute-done.38 = f32[8,34,1]{2,1,0:T(8,128)S(1)} collective-permute-done((f32[8,34,1]{2,1,0:T(8,128)S(1)}, f32[8,34,1]{2,1,0:T(8,128)S(1)}, u32[]{:S(2)}, u32[]{:S(2)}) %collective-permute-start.38) | collective-permute-done | bytes 1120 | tf_op jit(solution)/shard_map/ppermute | solution.py:18
  232.3 7.2 %collective-permute-start.41 = (f32[8,1,128]{2,1,0:T(1,128)S(1)}, f32[8,1,128]{2,1,0:T(1,128)S(1)}, u32[]{:S(2)}, u32[]{:S(2)}) collective-permute-start(f32[8,1,128]{2,1,0:T(1,128)S(1)} %get-tuple-element.38), channel_id=1, source_target_pairs={{8,0},{16,8},{24,16},{32,24},{40,32},{48,40},{56,48},{64,56},{72,6... | collective-permute-start | bytes 12296 | tf_op jit(solution)/shard_map/ppermute | solution.py:19
  245.7 3.8 %collective-permute-done.42 = f32[8,34,1]{2,1,0:T(8,128)S(1)} collective-permute-done((f32[8,34,1]{2,1,0:T(8,128)S(1)}, f32[8,34,1]{2,1,0:T(8,128)S(1)}, u32[]{:S(2)}, u32[]{:S(2)}) %collective-permute-start.42) | collective-permute-done | bytes 1120 | tf_op jit(solution)/shard_map/ppermute | solution.py:18
  252.0 7.5 %collective-permute-start.45 = (f32[8,1,128]{2,1,0:T(1,128)S(1)}, f32[8,1,128]{2,1,0:T(1,128)S(1)}, u32[]{:S(2)}, u32[]{:S(2)}) collective-permute-start(f32[8,1,128]{2,1,0:T(1,128)S(1)} %get-tuple-element.36), channel_id=1, source_target_pairs={{8,0},{16,8},{24,16},{32,24},{40,32},{48,40},{56,48},{64,56},{72,6... | collective-permute-start | bytes 12296 | tf_op jit(solution)/shard_map/ppermute | solution.py:19
  (156 shorter events, 111.7 us)
Async XLA Ops:
  1.4 38.2 %collective-permute-start = (s32[8,1,128]{2,1,0:T(1,128)S(1)}, s32[8,1,128]{2,1,0:T(1,128)S(1)}, u32[]{:S(2)}, u32[]{:S(2)}) collective-permute-start(s32[8,1,128]{2,1,0:T(1,128)S(1)} %get-tuple-element.45), channel_id=1, source_target_pairs={{0,8},{8,16},{16,24},{24,32},{32,40},{40,48},{48,56},{56,64},{64,7... | collective-permute-start | bytes 12296 | tf_op jit(solution)/shard_map/ppermute | solution.py:18
  5.7 33.9 %collective-permute-start.1 = (s32[8,1,128]{2,1,0:T(1,128)S(1)}, s32[8,1,128]{2,1,0:T(1,128)S(1)}, u32[]{:S(2)}, u32[]{:S(2)}) collective-permute-start(s32[8,1,128]{2,1,0:T(1,128)S(1)} %get-tuple-element.46), channel_id=1, source_target_pairs={{8,0},{16,8},{24,16},{32,24},{40,32},{48,40},{56,48},{64,56},{72,6... | collective-permute-start | bytes 12296 | tf_op jit(solution)/shard_map/ppermute | solution.py:19
  15.1 30.2 %collective-permute-start.4 = (f32[8,1,128]{2,1,0:T(1,128)S(1)}, f32[8,1,128]{2,1,0:T(1,128)S(1)}, u32[]{:S(2)}, u32[]{:S(2)}) collective-permute-start(f32[8,1,128]{2,1,0:T(1,128)S(1)} %get-tuple-element.47), channel_id=1, source_target_pairs={{0,8},{8,16},{16,24},{24,32},{32,40},{40,48},{48,56},{56,64},{64,7... | collective-permute-start | bytes 12296 | tf_op jit(solution)/shard_map/ppermute | solution.py:18
  17.1 28.3 %collective-permute-start.5 = (f32[8,1,128]{2,1,0:T(1,128)S(1)}, f32[8,1,128]{2,1,0:T(1,128)S(1)}, u32[]{:S(2)}, u32[]{:S(2)}) collective-permute-start(f32[8,1,128]{2,1,0:T(1,128)S(1)} %get-tuple-element.48), channel_id=1, source_target_pairs={{8,0},{16,8},{24,16},{32,24},{40,32},{48,40},{56,48},{64,56},{72,6... | collective-permute-start | bytes 12296 | tf_op jit(solution)/shard_map/ppermute | solution.py:19
  39.7 10.1 %collective-permute-start.2 = (s32[8,34,1]{2,1,0:T(8,128)S(1)}, s32[8,34,1]{2,1,0:T(8,128)S(1)}, u32[]{:S(2)}, u32[]{:S(2)}) collective-permute-start(s32[8,34,1]{2,1,0:T(8,128)S(1)} %get-tuple-element.31), channel_id=1, source_target_pairs={{0,1},{1,2},{2,3},{3,4},{4,5},{5,6},{6,7},{8,9},{9,10},{10,11},{11... | collective-permute-start | bytes 3272 | tf_op jit(solution)/shard_map/ppermute | solution.py:18
  54.8 33.5 %collective-permute-start.8 = (f32[8,1,128]{2,1,0:T(1,128)S(1)}, f32[8,1,128]{2,1,0:T(1,128)S(1)}, u32[]{:S(2)}, u32[]{:S(2)}) collective-permute-start(f32[8,1,128]{2,1,0:T(1,128)S(1)} %get-tuple-element.43), channel_id=1, source_target_pairs={{0,8},{8,16},{16,24},{24,32},{32,40},{40,48},{48,56},{56,64},{64,7... | collective-permute-start | bytes 12296 | tf_op jit(solution)/shard_map/ppermute | solution.py:18
  56.7 31.6 %collective-permute-start.9 = (f32[8,1,128]{2,1,0:T(1,128)S(1)}, f32[8,1,128]{2,1,0:T(1,128)S(1)}, u32[]{:S(2)}, u32[]{:S(2)}) collective-permute-start(f32[8,1,128]{2,1,0:T(1,128)S(1)} %get-tuple-element.44), channel_id=1, source_target_pairs={{8,0},{16,8},{24,16},{32,24},{40,32},{48,40},{56,48},{64,56},{72,6... | collective-permute-start | bytes 12296 | tf_op jit(solution)/shard_map/ppermute | solution.py:19
  64.0 28.8 %collective-permute-start.16 = (f32[4,1,64]{2,1,0:T(1,128)S(1)}, f32[4,1,64]{2,1,0:T(1,128)S(1)}, u32[]{:S(2)}, u32[]{:S(2)}) collective-permute-start(f32[4,1,64]{2,1,0:T(1,128)S(1)} %get-tuple-element.71), channel_id=1, source_target_pairs={{0,8},{8,16},{16,24},{24,32},{32,40},{40,48},{48,56},{56,64},{64,7... | collective-permute-start | bytes 3080 | tf_op jit(solution)/shard_map/ppermute | solution.py:18
  65.9 26.9 %collective-permute-start.17 = (f32[4,1,64]{2,1,0:T(1,128)S(1)}, f32[4,1,64]{2,1,0:T(1,128)S(1)}, u32[]{:S(2)}, u32[]{:S(2)}) collective-permute-start(f32[4,1,64]{2,1,0:T(1,128)S(1)} %get-tuple-element.72), channel_id=1, source_target_pairs={{8,0},{16,8},{24,16},{32,24},{40,32},{48,40},{56,48},{64,56},{72,6... | collective-permute-start | bytes 3080 | tf_op jit(solution)/shard_map/ppermute | solution.py:19
  97.5 13.6 %collective-permute-start.12 = (f32[8,1,128]{2,1,0:T(1,128)S(1)}, f32[8,1,128]{2,1,0:T(1,128)S(1)}, u32[]{:S(2)}, u32[]{:S(2)}) collective-permute-start(f32[8,1,128]{2,1,0:T(1,128)S(1)} %get-tuple-element.41), channel_id=1, source_target_pairs={{0,8},{8,16},{16,24},{24,32},{32,40},{40,48},{48,56},{56,64},{64,7... | collective-permute-start | bytes 12296 | tf_op jit(solution)/shard_map/ppermute | solution.py:18
  99.4 11.7 %collective-permute-start.13 = (f32[8,1,128]{2,1,0:T(1,128)S(1)}, f32[8,1,128]{2,1,0:T(1,128)S(1)}, u32[]{:S(2)}, u32[]{:S(2)}) collective-permute-start(f32[8,1,128]{2,1,0:T(1,128)S(1)} %get-tuple-element.42), channel_id=1, source_target_pairs={{8,0},{16,8},{24,16},{32,24},{40,32},{48,40},{56,48},{64,56},{72,6... | collective-permute-start | bytes 12296 | tf_op jit(solution)/shard_map/ppermute | solution.py:19
  106.8 9.6 %collective-permute-start.19 = (f32[4,18,1]{2,1,0:T(8,128)S(1)}, f32[4,18,1]{2,1,0:T(8,128)S(1)}, u32[]{:S(2)}, u32[]{:S(2)}) collective-permute-start(f32[4,18,1]{2,1,0:T(8,128)S(1)} %get-tuple-element.61), channel_id=1, source_target_pairs={{1,0},{2,1},{3,2},{4,3},{5,4},{6,5},{7,6},{9,8},{10,9},{11,10},{12... | collective-permute-start | bytes 872 | tf_op jit(solution)/shard_map/ppermute | solution.py:19
  135.5 9.3 %collective-permute-start.20 = (f32[4,1,64]{2,1,0:T(1,128)S(1)}, f32[4,1,64]{2,1,0:T(1,128)S(1)}, u32[]{:S(2)}, u32[]{:S(2)}) collective-permute-start(f32[4,1,64]{2,1,0:T(1,128)S(1)} %get-tuple-element.69), channel_id=1, source_target_pairs={{0,8},{8,16},{16,24},{24,32},{32,40},{40,48},{48,56},{56,64},{64,7... | collective-permute-start | bytes 3080 | tf_op jit(solution)/shard_map/ppermute | solution.py:18
  153.7 9.4 %collective-permute-start.24 = (f32[4,1,64]{2,1,0:T(1,128)S(1)}, f32[4,1,64]{2,1,0:T(1,128)S(1)}, u32[]{:S(2)}, u32[]{:S(2)}) collective-permute-start(f32[4,1,64]{2,1,0:T(1,128)S(1)} %get-tuple-element.67), channel_id=1, source_target_pairs={{0,8},{8,16},{16,24},{24,32},{32,40},{40,48},{48,56},{56,64},{64,7... | collective-permute-start | bytes 3080 | tf_op jit(solution)/shard_map/ppermute | solution.py:18
  155.6 8.8 %collective-permute-start.25 = (f32[4,1,64]{2,1,0:T(1,128)S(1)}, f32[4,1,64]{2,1,0:T(1,128)S(1)}, u32[]{:S(2)}, u32[]{:S(2)}) collective-permute-start(f32[4,1,64]{2,1,0:T(1,128)S(1)} %get-tuple-element.68), channel_id=1, source_target_pairs={{8,0},{16,8},{24,16},{32,24},{40,32},{48,40},{56,48},{64,56},{72,6... | collective-permute-start | bytes 3080 | tf_op jit(solution)/shard_map/ppermute | solution.py:19
  172.1 9.4 %collective-permute-start.28 = (f32[4,1,64]{2,1,0:T(1,128)S(1)}, f32[4,1,64]{2,1,0:T(1,128)S(1)}, u32[]{:S(2)}, u32[]{:S(2)}) collective-permute-start(f32[4,1,64]{2,1,0:T(1,128)S(1)} %get-tuple-element.65), channel_id=1, source_target_pairs={{0,8},{8,16},{16,24},{24,32},{32,40},{40,48},{48,56},{56,64},{64,7... | collective-permute-start | bytes 3080 | tf_op jit(solution)/shard_map/ppermute | solution.py:18
  174.0 8.8 %collective-permute-start.29 = (f32[4,1,64]{2,1,0:T(1,128)S(1)}, f32[4,1,64]{2,1,0:T(1,128)S(1)}, u32[]{:S(2)}, u32[]{:S(2)}) collective-permute-start(f32[4,1,64]{2,1,0:T(1,128)S(1)} %get-tuple-element.66), channel_id=1, source_target_pairs={{8,0},{16,8},{24,16},{32,24},{40,32},{48,40},{56,48},{64,56},{72,6... | collective-permute-start | bytes 3080 | tf_op jit(solution)/shard_map/ppermute | solution.py:19
  190.5 9.4 %collective-permute-start.32 = (f32[4,1,64]{2,1,0:T(1,128)S(1)}, f32[4,1,64]{2,1,0:T(1,128)S(1)}, u32[]{:S(2)}, u32[]{:S(2)}) collective-permute-start(f32[4,1,64]{2,1,0:T(1,128)S(1)} %get-tuple-element.63), channel_id=1, source_target_pairs={{0,8},{8,16},{16,24},{24,32},{32,40},{40,48},{48,56},{56,64},{64,7... | collective-permute-start | bytes 3080 | tf_op jit(solution)/shard_map/ppermute | solution.py:18
  192.5 8.8 %collective-permute-start.33 = (f32[4,1,64]{2,1,0:T(1,128)S(1)}, f32[4,1,64]{2,1,0:T(1,128)S(1)}, u32[]{:S(2)}, u32[]{:S(2)}) collective-permute-start(f32[4,1,64]{2,1,0:T(1,128)S(1)} %get-tuple-element.64), channel_id=1, source_target_pairs={{8,0},{16,8},{24,16},{32,24},{40,32},{48,40},{56,48},{64,56},{72,6... | collective-permute-start | bytes 3080 | tf_op jit(solution)/shard_map/ppermute | solution.py:19
  209.5 9.4 %collective-permute-start.36 = (f32[8,1,128]{2,1,0:T(1,128)S(1)}, f32[8,1,128]{2,1,0:T(1,128)S(1)}, u32[]{:S(2)}, u32[]{:S(2)}) collective-permute-start(f32[8,1,128]{2,1,0:T(1,128)S(1)} %get-tuple-element.39), channel_id=1, source_target_pairs={{0,8},{8,16},{16,24},{24,32},{32,40},{40,48},{48,56},{56,64},{64,7... | collective-permute-start | bytes 12296 | tf_op jit(solution)/shard_map/ppermute | solution.py:18
  211.4 8.8 %collective-permute-start.37 = (f32[8,1,128]{2,1,0:T(1,128)S(1)}, f32[8,1,128]{2,1,0:T(1,128)S(1)}, u32[]{:S(2)}, u32[]{:S(2)}) collective-permute-start(f32[8,1,128]{2,1,0:T(1,128)S(1)} %get-tuple-element.40), channel_id=1, source_target_pairs={{8,0},{16,8},{24,16},{32,24},{40,32},{48,40},{56,48},{64,56},{72,6... | collective-permute-start | bytes 12296 | tf_op jit(solution)/shard_map/ppermute | solution.py:19
  230.4 9.2 %collective-permute-start.40 = (f32[8,1,128]{2,1,0:T(1,128)S(1)}, f32[8,1,128]{2,1,0:T(1,128)S(1)}, u32[]{:S(2)}, u32[]{:S(2)}) collective-permute-start(f32[8,1,128]{2,1,0:T(1,128)S(1)} %get-tuple-element.37), channel_id=1, source_target_pairs={{0,8},{8,16},{16,24},{24,32},{32,40},{40,48},{48,56},{56,64},{64,7... | collective-permute-start | bytes 12296 | tf_op jit(solution)/shard_map/ppermute | solution.py:18
  250.1 9.4 %collective-permute-start.44 = (f32[8,1,128]{2,1,0:T(1,128)S(1)}, f32[8,1,128]{2,1,0:T(1,128)S(1)}, u32[]{:S(2)}, u32[]{:S(2)}) collective-permute-start(f32[8,1,128]{2,1,0:T(1,128)S(1)} %get-tuple-element.35), channel_id=1, source_target_pairs={{0,8},{8,16},{16,24},{24,32},{32,40},{40,48},{48,56},{56,64},{64,7... | collective-permute-start | bytes 12296 | tf_op jit(solution)/shard_map/ppermute | solution.py:18
  252.0 8.8 %collective-permute-start.45 = (f32[8,1,128]{2,1,0:T(1,128)S(1)}, f32[8,1,128]{2,1,0:T(1,128)S(1)}, u32[]{:S(2)}, u32[]{:S(2)}) collective-permute-start(f32[8,1,128]{2,1,0:T(1,128)S(1)} %get-tuple-element.36), channel_id=1, source_target_pairs={{8,0},{16,8},{24,16},{32,24},{40,32},{48,40},{56,48},{64,56},{72,6... | collective-permute-start | bytes 12296 | tf_op jit(solution)/shard_map/ppermute | solution.py:19
  (28 other events, 261.6 us)
where the time goes:
time: 272 us; the launch traced here: 271 us
  starting transfers between devices  171 us (63%)
  waiting for transfers between devices  45.1 us (17%)
  local copies, waits for them, and re-layouts  32.5 us (12%)
  other arithmetic  19.1 us (7%)
  between operations  3.35 us (1%)
    ppermute x24, starting transfers between devices, extended(): after = lax.ppermute(initial, axis, down)  118 us
    ppermute x24, starting transfers between devices, extended(): before = lax.ppermute(last, axis, up)  52.3 us
    ppermute x24, waiting for transfers between devices, extended(): before = lax.ppermute(last, axis, up)  31.7 us
    reshape x2, local copies, waits for them, and re-layouts, coarsen(): blocks = field.reshape(first // 2, 2, second // 2, 2, third // 2, 2)  19.6 us
    ppermute x24, waiting for transfers between devices, extended(): after = lax.ppermute(initial, axis, down)  13.4 us
    reshape x1, local copies, waits for them, and re-layouts, body(): wet_mask.reshape(first // 2, 2, second // 2, 2, third // 2, 2)  10.5 us
    reduce_sum x2, other arithmetic, coarsen(): return jnp.sum(blocks, axis=(1, 3, 5)) * 0.125  8.03 us
  transfers between devices with their start and end apart: 48, of which 23 were waited for; matrix products, arithmetic and copies ran while one was open for 11% of the time, Pallas kernels for 0%

commit v1 on v0

v1 whole, which is shorter than its diff:
```python
import functools

import jax
import jax.numpy as jnp
from jax import lax
from jax.experimental import pallas as pl
from jax.experimental.pallas import tpu as pltpu
from jax.sharding import PartitionSpec as P

CHEB = 4

CZ = 8
ROWS = 32
LANES = 128
RIM = 14
TALL = ROWS + 2 * RIM
MASK_RIM = 13
RIGHT_RIM = 12
STRIP = MASK_RIM + 2 * RIGHT_RIM
SIDE = 16
GROUP = LANES // SIDE
PACKED = 8
WIDE = 2 * LANES

VMEM = pl.BlockSpec(memory_space=pltpu.VMEM)
SMEM = pl.BlockSpec(memory_space=pltpu.SMEM)


def brick_row(ref, row):
    return ref[pl.ds(row, CZ, stride=ROWS), :]


def strips_kernel(right_ref, mask_ref, helm_ref, first_ref, last_ref):
    for out_ref, mask_from, other_from in (
        (first_ref, 0, 0),
        (last_ref, ROWS - MASK_RIM, ROWS - RIGHT_RIM),
    ):
        for row in range(MASK_RIM):
            out_ref[row] = brick_row(mask_ref, mask_from + row).astype(jnp.float32)
        for row in range(RIGHT_RIM):
            out_ref[MASK_RIM + row] = brick_row(helm_ref, other_from + row)
            out_ref[MASK_RIM + RIGHT_RIM + row] = brick_row(right_ref, other_from + row)


def sides_kernel(
    right_ref, mask_ref, helm_ref, before_ref, after_ref, tall_ref, first_ref, last_ref
):
    zero = jnp.zeros((CZ, LANES), jnp.float32)
    for field in range(3):
        for row in (0, 1, TALL - 2, TALL - 1):
            tall_ref[field, row] = zero
    for field, own_ref, offset, rim in (
        (0, mask_ref, 0, MASK_RIM),
        (1, helm_ref, MASK_RIM, RIGHT_RIM),
        (2, right_ref, MASK_RIM + RIGHT_RIM, RIGHT_RIM),
    ):
        for row in range(rim):
            tall_ref[field, RIM - rim + row] = before_ref[offset + row]
            tall_ref[field, RIM + ROWS + row] = after_ref[offset + row]
        for row in range(ROWS):
            tall_ref[field, RIM + row] = brick_row(own_ref, row).astype(jnp.float32)
    lane = lax.broadcasted_iota(jnp.int32, (CZ, LANES), 1)
    for field in range(3):

        def pack(group, carry):
            first, last = zero, zero
            for k in range(GROUP):
                line = tall_ref[field, jnp.minimum(group * GROUP + k, TALL - 1)]
                here = (lane >= SIDE * k) & (lane < SIDE * (k + 1))
                one = pltpu.roll(line, SIDE * k, 1) if k else line
                two = pltpu.roll(line, (SIDE * (k + 1)) % LANES, 1) if k + 1 < GROUP else line
                first = jnp.where(here, one, first)
                last = jnp.where(here, two, last)
            first_ref[field * PACKED + group] = first
            last_ref[field * PACKED + group] = last
            return carry

        lax.fori_loop(0, PACKED, pack, 0)


def rows_loop(start, stop, chunk, step):
    count = (stop - start) // chunk
    assert count * chunk == stop - start

    def body(index, carry):
        step(start + index * chunk)
        return carry

    lax.fori_loop(0, count, body, 0)


def cycle_kernel(
    eig_low_ref,
    eig_high_ref,
    tall_ref,
    left_ref,
    right_ref,
    pressure_ref,
    residual_ref,
    wet,
    helm,
    rhs,
    diag,
    base,
    gain,
    flow,
    flow_next,
    state,
    wet_c,
    diag_c,
    inverse_c,
    remain,
    error,
    direction,
    masked,
    masked_next,
):
    lane = lax.broadcasted_iota(jnp.int32, (CZ, LANES), 1)

    for field, dest in ((0, wet), (1, helm), (2, rhs)):

        def unpack(group, carry):
            after = right_ref[field * PACKED + group]
            ahead = pltpu.roll(left_ref[field * PACKED + group], LANES - SIDE, 1)
            for k in range(GROUP):
                row = jnp.minimum(group * GROUP + k, TALL - 1)
                low, high = SIDE * k, SIDE * (k + 1)
                beyond = (low - SIDE) % LANES
                both = jnp.where((lane >= beyond) & (lane < beyond + SIDE), ahead, 0.0)
                both = jnp.where((lane >= low) & (lane < high), after, both)
                if k:
                    both = pltpu.roll(both, LANES - low, 1)
                dest[row, :, :LANES] = tall_ref[field, row]
                dest[row, :, LANES:] = both
            return carry

        lax.fori_loop(0, PACKED, unpack, 0)

    def planes(count):
        level = lax.broadcasted_iota(jnp.int32, (count, CZ, WIDE), 1)
        column = lax.broadcasted_iota(jnp.int32, (count, CZ, WIDE), 2)
        return level, column

    def near_rows(ref, row, count, reach, ahead=1):
        level, _ = planes(count)
        here = ref[pl.ds(row, count)]
        total = ref[pl.ds(row - 1, count)] + ref[pl.ds(row + 1, count)]
        total = total + jnp.where(level >= reach, pltpu.roll(here, reach, 1), 0.0)
        total = total + jnp.where(level < CZ - reach, pltpu.roll(here, CZ - reach, 1), 0.0)
        return total + (pltpu.roll(here, reach, 2) + pltpu.roll(here, WIDE - reach, 2))

    def smooth_setup(row, chunk=4):
        rows = pl.ds(row, chunk)
        water = wet[rows]
        count = near_rows(wet, row, chunk, 1)
        scale = water * (helm[rows] + count) + (1.0 - water)
        inverse = 0.8 / scale
        start = inverse * rhs[rows]
        diag[rows] = scale
        base[rows] = start
        gain[rows] = inverse * water
        flow[rows] = water * start

    rows_loop(2, 58, 4, smooth_setup)

    def smooth_second(row, chunk=3):
        rows = pl.ds(row, chunk)
        value = 1.2 * base[rows] + gain[rows] * near_rows(flow, row, chunk, 1)
        state[rows] = value
        flow_next[rows] = wet[rows] * value

    rows_loop(3, 57, 3, smooth_second)

    def pair_sum(value):
        level, column = planes(value.shape[0])
        other = jnp.where(
            level % 2 == 0, pltpu.roll(value, CZ - 1, 1), pltpu.roll(value, 1, 1)
        )
        value = value + other
        other = jnp.where(
            column % 2 == 0, pltpu.roll(value, WIDE - 1, 2), pltpu.roll(value, 1, 2)
        )
        return value + other

    def coarse_mask(row, chunk=4):
        total = jnp.stack([wet[2 * (row + i)] + wet[2 * (row + i) + 1] for i in range(chunk)])
        wet_c[pl.ds(row, chunk)] = jnp.where(pair_sum(total) >= 3.5, 1.0, 0.0)

    rows_loop(1, 29, 4, coarse_mask)

    low = jnp.full((1, CZ, WIDE), eig_low_ref[0], jnp.float32)
    high = jnp.full((1, CZ, WIDE), eig_high_ref[0], jnp.float32)
    centre = 0.5 * (high + low)
    half = 0.5 * (high - low)
    sigma = centre / half
    rho = 1.0 / sigma
    start_scale = 1.0 / centre

    def coarse_setup(row, chunk=2):
        rows = pl.ds(row, chunk)
        fine = pl.ds(2 * row, 2 * chunk)
        water = wet[fine]
        left_over = water * (
            rhs[fine] - diag[fine] * state[fine] + near_rows(flow_next, 2 * row, 2 * chunk, 1)
        )
        lumps = helm[fine]
        source = jnp.stack([left_over[2 * i] + left_over[2 * i + 1] for i in range(chunk)])
        shift = jnp.stack([lumps[2 * i] + lumps[2 * i + 1] for i in range(chunk)])
        source = 0.125 * pair_sum(source)
        shift = 0.125 * pair_sum(shift)
        water_c = wet_c[rows]
        count_c = near_rows(wet_c, row, chunk, 2)
        scale = water_c * (shift + 0.25 * count_c) + (1.0 - water_c)
        inverse = 1.0 / scale
        first = source * inverse * start_scale
        diag_c[rows] = scale
        inverse_c[rows] = inverse
        remain[rows] = source
        error[rows] = first
        direction[rows] = first
        masked[rows] = water_c * first

    rows_loop(2, 28, 2, coarse_setup)

    source_ref, other_ref = masked, masked_next
    for sweep in range(1, CHEB):
        rho_next = 1.0 / (2.0 * sigma - rho)
        keep = rho_next * rho
        add = 2.0 * rho_next / half

        def chebyshev(row, chunk=2, keep=keep, add=add, now=source_ref, later=other_ref):
            rows = pl.ds(row, chunk)
            old = direction[rows]
            water_c = wet_c[rows]
            left_over = remain[rows] - (
                diag_c[rows] * old - 0.25 * water_c * near_rows(now, row, chunk, 2)
            )
            fresh = keep * old + add * (left_over * inverse_c[rows])
            remain[rows] = left_over
            direction[rows] = fresh
            error[rows] = error[rows] + fresh
            later[rows] = water_c * fresh

        rows_loop(2 + sweep, 28 - sweep, 2, chebyshev)
        rho = rho_next
        source_ref, other_ref = other_ref, source_ref

    def spread(row, chunk=2):
        level, column = planes(chunk)
        value = error[pl.ds(row, chunk)]
        other = jnp.where(
            column % 2 == 0, pltpu.roll(value, 1, 2), pltpu.roll(value, WIDE - 1, 2)
        )
        value = 0.75 * value + 0.25 * other
        other = jnp.where(
            level % 2 == 0, pltpu.roll(value, 1, 1), pltpu.roll(value, CZ - 1, 1)
        )
        other = jnp.where((level == 0) | (level == CZ - 1), 0.0, other)
        masked[pl.ds(row, chunk)] = 0.75 * value + 0.25 * other

    rows_loop(5, 25, 2, spread)

    def correct(row, chunk=2):
        for i in range(chunk):
            here = 0.75 * masked[row + i]
            for fine, side in (
                (2 * (row + i), masked[row + i - 1]),
                (2 * (row + i) + 1, masked[row + i + 1]),
            ):
                water = wet[fine]
                value = state[fine] + water * (here + 0.25 * side)
                state[fine] = value
                flow[fine] = water * value

    rows_loop(5, 25, 2, correct)

    def smooth_third(row, chunk=4):
        rows = pl.ds(row, chunk)
        value = 0.2 * state[rows] + base[rows] + gain[rows] * near_rows(flow, row, chunk, 1)
        state[rows] = value
        flow_next[rows] = wet[rows] * value

    rows_loop(12, 48, 4, smooth_third)

    def smooth_fourth(row, chunk=2):
        rows = pl.ds(row, chunk)
        value = 0.2 * state[rows] + base[rows] + gain[rows] * near_rows(flow_next, row, chunk, 1)
        state[rows] = value
        flow[rows] = wet[rows] * value

    rows_loop(13, 47, 2, smooth_fourth)

    def finish(row, chunk=4):
        rows = pl.ds(row, chunk)
        value = state[rows]
        left_over = rhs[rows] - diag[rows] * value + wet[rows] * near_rows(flow, row, chunk, 1)
        for i in range(chunk):
            place = pl.ds(row - RIM + i, CZ, stride=ROWS)
            pressure_ref[place, :] = value[i, :, :LANES]
            residual_ref[place, :] = left_over[i, :, :LANES]

    rows_loop(RIM, RIM + ROWS, 4, finish)


def shifted(array, axis, step):
    devices = lax.axis_size(axis)
    pairs = [(i, i + step) for i in range(devices) if 0 <= i + step < devices]
    return lax.ppermute(array, axis, pairs)


def f32(*shape):
    return jax.ShapeDtypeStruct(shape, jnp.float32)


def body(right_side, wet_mask, helmholtz, eig_low, eig_high):
    flat = (CZ * ROWS, LANES)
    right_flat = right_side.reshape(flat)
    mask_flat = wet_mask.reshape(flat)
    helm_flat = helmholtz.reshape(flat)
    limits = pltpu.CompilerParams(vmem_limit_bytes=16 * 1024 * 1024)

    first, last = pl.pallas_call(
        strips_kernel,
        out_shape=(f32(STRIP, CZ, LANES),) * 2,
        in_specs=[VMEM] * 3,
        out_specs=(VMEM,) * 2,
        compiler_params=limits,
        name="strips",
    )(right_flat, mask_flat, helm_flat)
    before = shifted(last, "wide", 1)
    after = shifted(first, "wide", -1)

    tall, first, last = pl.pallas_call(
        sides_kernel,
        out_shape=(
            f32(3, TALL, CZ, LANES),
            f32(3 * PACKED, CZ, LANES),
            f32(3 * PACKED, CZ, LANES),
        ),
        in_specs=[VMEM] * 5,
        out_specs=(VMEM,) * 3,
        compiler_params=limits,
        name="sides",
    )(right_flat, mask_flat, helm_flat, before, after)
    from_left = shifted(last, "narrow", 1)
    from_right = shifted(first, "narrow", -1)

    pressure, residual = pl.pallas_call(
        cycle_kernel,
        out_shape=(f32(*flat),) * 2,
        in_specs=[SMEM] * 2 + [VMEM] * 3,
        out_specs=(VMEM,) * 2,
        scratch_shapes=[pltpu.VMEM((TALL, CZ, WIDE), jnp.float32)] * 9
        + [pltpu.VMEM((TALL // 2, CZ, WIDE), jnp.float32)] * 8,
        compiler_params=limits,
        name="cycle",
    )(eig_low, eig_high, tall, from_left, from_right)
    shape = (CZ, ROWS, LANES)
    return pressure.reshape(shape), residual.reshape(shape)


def solution(mesh):
    field = P(None, "wide", "narrow")
    return jax.shard_map(
        body,
        mesh=mesh,
        in_specs=(field, field, field, P(), P()),
        out_specs=(field, field),
        check_vma=False,
    )
```

time: 272 us -> 49.3 us (0.18)
  the two profiles are of different devices: /device:TPU:34 before, /device:TPU:57 now
where the time goes in v1:
time: 49.3 us; the launch traced here: 49.1 us
  starting transfers between devices  19.8 us (40%)
  Pallas kernels  19.3 us (39%)
  waiting for transfers between devices  5.29 us (11%)
  local copies, waits for them, and re-layouts  2.7 us (5%)
  between operations  1.98 us (4%)
    ppermute x4, starting transfers between devices, shifted(): return lax.ppermute(array, axis, pairs)  19.8 us
    pallas_call x1, Pallas kernels, body(): pl.pallas_call(cycle_kernel, out_shape=(f32(*flat),) * 2, in_specs=[SMEM]...  16.8 us
    ppermute x4, waiting for transfers between devices, shifted(): return lax.ppermute(array, axis, pairs)  5.29 us
    unnamed x6, local copies, waits for them, and re-layouts  2.7 us
    pallas_call x1, Pallas kernels, body(): pl.pallas_call(sides_kernel, out_shape=(f32(3, TALL, CZ, LANES), f32(3 *...  2.25 us
  transfers between devices with their start and end apart: 4, of which 3 were waited for; matrix products, arithmetic and copies ran while one was open for 0% of the time, Pallas kernels for 0%

profile of v1, /device:TPU:57, one launch (start us, length us, event | category | flops | bytes accessed | tf_op | source)
XLA Modules:
  0.0 49.1 jit_solution(14831389896310743168)
XLA Ops:
  0.6 0.0 copy-start
  0.6 0.9 %copy-done = f32[8,32,128]{2,1,0:T(8,128)S(1)} copy-done((f32[8,32,128]{2,1,0:T(8,128)S(1)}, f32[8,32,128]{2,1,0:T(8,128)}, u32[]{:S(2)}) %copy-start) | copy-done | bytes 131096
  1.5 0.0 copy-start.1
  1.5 0.9 %copy-done.1 = s32[8,32,128]{2,1,0:T(8,128)S(1)} copy-done((s32[8,32,128]{2,1,0:T(8,128)S(1)}, s32[8,32,128]{2,1,0:T(8,128)}, u32[]{:S(2)}) %copy-start.1) | copy-done | bytes 131096
  2.4 0.0 copy-start.2
  2.4 0.9 %copy-done.2 = f32[8,32,128]{2,1,0:T(8,128)S(1)} copy-done((f32[8,32,128]{2,1,0:T(8,128)S(1)}, f32[8,32,128]{2,1,0:T(8,128)}, u32[]{:S(2)}) %copy-start.2) | copy-done | bytes 131096
  3.3 0.2 strips.1
  3.5 4.0 %collective-permute-start = (f32[37,8,128]{2,1,0:T(8,128)S(1)}, f32[37,8,128]{2,1,0:T(8,128)S(1)}, u32[]{:S(2)}, u32[]{:S(2)}) collective-permute-start(f32[37,8,128]{2,1,0:T(8,128)S(1)} %get-tuple-element.9), channel_id=1, source_target_pairs={{0,8},{8,16},{16,24},{24,32},{32,40},{40,48},{48,56},{56,64},{64,7... | collective-permute-start | bytes 454664 | tf_op jit(solution)/shard_map/ppermute | solution.py:308
  7.5 9.4 %collective-permute-start.1 = (f32[37,8,128]{2,1,0:T(8,128)S(1)}, f32[37,8,128]{2,1,0:T(8,128)S(1)}, u32[]{:S(2)}, u32[]{:S(2)}) collective-permute-start(f32[37,8,128]{2,1,0:T(8,128)S(1)} %get-tuple-element.10), channel_id=1, source_target_pairs={{8,0},{16,8},{24,16},{32,24},{40,32},{48,40},{56,48},{64,56},{72,6... | collective-permute-start | bytes 454664 | tf_op jit(solution)/shard_map/ppermute | solution.py:308
  16.9 1.7 %collective-permute-done.before_ref = f32[37,8,128]{2,1,0:T(8,128)S(1)} collective-permute-done((f32[37,8,128]{2,1,0:T(8,128)S(1)}, f32[37,8,128]{2,1,0:T(8,128)S(1)}, u32[]{:S(2)}, u32[]{:S(2)}) %collective-permute-start) | collective-permute-done | bytes 151584 | tf_op jit(solution)/shard_map/ppermute | solution.py:308
  18.6 0.9 %collective-permute-done.1.after_ref = f32[37,8,128]{2,1,0:T(8,128)S(1)} collective-permute-done((f32[37,8,128]{2,1,0:T(8,128)S(1)}, f32[37,8,128]{2,1,0:T(8,128)S(1)}, u32[]{:S(2)}, u32[]{:S(2)}) %collective-permute-start.1) | collective-permute-done | bytes 151584 | tf_op jit(solution)/shard_map/ppermute | solution.py:308
  19.5 2.2 %sides.1 = (f32[3,60,8,128]{3,2,1,0:T(8,128)S(1)}, f32[24,8,128]{2,1,0:T(8,128)S(1)}, f32[24,8,128]{2,1,0:T(8,128)S(1)}) custom-call(f32[256,128]{1,0:T(8,128)S(1)} %bitcast.6, s32[256,128]{1,0:T(8,128)S(1)} %bitcast.8, f32[256,128]{1,0:T(8,128)S(1)} %bitcast.10, f32[37,8,128]{2,1,0:T(8,128)S(1)} %collective-permute-done.before_ref, ...), custom_call_target="tpu_custom_call" | custom-call | tf_op jit(solution)/shard_map/sides/pallas_call | solution.py:333
  21.8 4.6 %collective-permute-start.2 = (f32[24,8,128]{2,1,0:T(8,128)S(1)}, f32[24,8,128]{2,1,0:T(8,128)S(1)}, u32[]{:S(2)}, u32[]{:S(2)}) collective-permute-start(f32[24,8,128]{2,1,0:T(8,128)S(1)} %get-tuple-element.12), channel_id=1, source_target_pairs={{0,1},{1,2},{2,3},{3,4},{4,5},{5,6},{6,7},{8,9},{9,10},{10,11},{11... | collective-permute-start | bytes 294920 | tf_op jit(solution)/shard_map/ppermute | solution.py:308
  26.3 1.9 %collective-permute-start.3 = (f32[24,8,128]{2,1,0:T(8,128)S(1)}, f32[24,8,128]{2,1,0:T(8,128)S(1)}, u32[]{:S(2)}, u32[]{:S(2)}) collective-permute-start(f32[24,8,128]{2,1,0:T(8,128)S(1)} %get-tuple-element.13), channel_id=1, source_target_pairs={{1,0},{2,1},{3,2},{4,3},{5,4},{6,5},{7,6},{9,8},{10,9},{11,10},{12... | collective-permute-start | bytes 294920 | tf_op jit(solution)/shard_map/ppermute | solution.py:308
  29.5 0.0 collective-permute-done.2.left_ref
  29.5 2.7 %collective-permute-done.3.right_ref = f32[24,8,128]{2,1,0:T(8,128)S(1)} collective-permute-done((f32[24,8,128]{2,1,0:T(8,128)S(1)}, f32[24,8,128]{2,1,0:T(8,128)S(1)}, u32[]{:S(2)}, u32[]{:S(2)}) %collective-permute-start.3) | collective-permute-done | bytes 98336 | tf_op jit(solution)/shard_map/ppermute | solution.py:308
  32.2 16.8 %cycle.1 = (f32[256,128]{1,0:T(8,128)}, f32[256,128]{1,0:T(8,128)}) custom-call(f32[1]{0:T(128)S(6)} %copy.7.eig_low_ref, f32[1]{0:T(128)S(6)} %copy.8.eig_high_ref, f32[3,60,8,128]{3,2,1,0:T(8,128)S(1)} %get-tuple-element.11.tall_ref, f32[24,8,128]{2,1,0:T(8,128)S(1)} %collective-permute-done.2.left_ref, f32[24,8,128]{2,1,0:T(8,128)S(1)} %collective-permute-done.3.right_ref), custom_call_target="tpu_custom_call" | custom-call | tf_op jit(solution)/shard_map/cycle/pallas_call | solution.py:348
Async XLA Ops:
  0.6 0.9 %copy-start = (f32[8,32,128]{2,1,0:T(8,128)S(1)}, f32[8,32,128]{2,1,0:T(8,128)}, u32[]{:S(2)}) copy-start(f32[8,32,128]{2,1,0:T(8,128)} %param.5) | copy-start | bytes 393220
  1.5 0.9 %copy-start.1 = (s32[8,32,128]{2,1,0:T(8,128)S(1)}, s32[8,32,128]{2,1,0:T(8,128)}, u32[]{:S(2)}) copy-start(s32[8,32,128]{2,1,0:T(8,128)} %param.6) | copy-start | bytes 393220
  2.4 0.9 %copy-start.2 = (f32[8,32,128]{2,1,0:T(8,128)S(1)}, f32[8,32,128]{2,1,0:T(8,128)}, u32[]{:S(2)}) copy-start(f32[8,32,128]{2,1,0:T(8,128)} %param.7) | copy-start | bytes 393220
  3.5 15.1 %collective-permute-start = (f32[37,8,128]{2,1,0:T(8,128)S(1)}, f32[37,8,128]{2,1,0:T(8,128)S(1)}, u32[]{:S(2)}, u32[]{:S(2)}) collective-permute-start(f32[37,8,128]{2,1,0:T(8,128)S(1)} %get-tuple-element.9), channel_id=1, source_target_pairs={{0,8},{8,16},{16,24},{24,32},{32,40},{40,48},{48,56},{56,64},{64,7... | collective-permute-start | bytes 454664 | tf_op jit(solution)/shard_map/ppermute | solution.py:308
  7.5 12.0 %collective-permute-start.1 = (f32[37,8,128]{2,1,0:T(8,128)S(1)}, f32[37,8,128]{2,1,0:T(8,128)S(1)}, u32[]{:S(2)}, u32[]{:S(2)}) collective-permute-start(f32[37,8,128]{2,1,0:T(8,128)S(1)} %get-tuple-element.10), channel_id=1, source_target_pairs={{8,0},{16,8},{24,16},{32,24},{40,32},{48,40},{56,48},{64,56},{72,6... | collective-permute-start | bytes 454664 | tf_op jit(solution)/shard_map/ppermute | solution.py:308
  21.8 7.8 %collective-permute-start.2 = (f32[24,8,128]{2,1,0:T(8,128)S(1)}, f32[24,8,128]{2,1,0:T(8,128)S(1)}, u32[]{:S(2)}, u32[]{:S(2)}) collective-permute-start(f32[24,8,128]{2,1,0:T(8,128)S(1)} %get-tuple-element.12), channel_id=1, source_target_pairs={{0,1},{1,2},{2,3},{3,4},{4,5},{5,6},{6,7},{8,9},{9,10},{10,11},{11... | collective-permute-start | bytes 294920 | tf_op jit(solution)/shard_map/ppermute | solution.py:308
  26.3 5.9 %collective-permute-start.3 = (f32[24,8,128]{2,1,0:T(8,128)S(1)}, f32[24,8,128]{2,1,0:T(8,128)S(1)}, u32[]{:S(2)}, u32[]{:S(2)}) collective-permute-start(f32[24,8,128]{2,1,0:T(8,128)S(1)} %get-tuple-element.13), channel_id=1, source_target_pairs={{1,0},{2,1},{3,2},{4,3},{5,4},{6,5},{7,6},{9,8},{10,9},{11,10},{12... | collective-permute-start | bytes 294920 | tf_op jit(solution)/shard_map/ppermute | solution.py:308

commit v2 on v1

v2 whole, which is shorter than its diff:
```python
import functools

import jax
import jax.numpy as jnp
from jax import lax
from jax.experimental import pallas as pl
from jax.experimental.pallas import tpu as pltpu
from jax.sharding import PartitionSpec as P

CHEB = 4

CZ = 8
ROWS = 32
LANES = 128
RIM = 14
TALL = ROWS + 2 * RIM
MASK_RIM = 13
RIGHT_RIM = 12
STRIP = MASK_RIM + 2 * RIGHT_RIM
SIDE = 16
GROUP = LANES // SIDE
PACKED = 8
PITCH = 2 * CZ

VMEM = pl.BlockSpec(memory_space=pltpu.VMEM)
ANY = pl.BlockSpec(memory_space=pl.ANY)
SMEM = pl.BlockSpec(memory_space=pltpu.SMEM)


def brick_row(ref, row):
    return ref[pl.ds(row, CZ, stride=ROWS), :]


def strips_kernel(right_ref, mask_ref, helm_ref, first_ref, last_ref):
    for out_ref, mask_from, other_from in (
        (first_ref, 0, 0),
        (last_ref, ROWS - MASK_RIM, ROWS - RIGHT_RIM),
    ):
        for row in range(MASK_RIM):
            out_ref[row] = brick_row(mask_ref, mask_from + row).astype(jnp.float32)
        for row in range(RIGHT_RIM):
            out_ref[MASK_RIM + row] = brick_row(helm_ref, other_from + row)
            out_ref[MASK_RIM + RIGHT_RIM + row] = brick_row(right_ref, other_from + row)


def sides_kernel(
    right_ref, mask_ref, helm_ref, before_ref, after_ref, tall_ref, first_ref, last_ref
):
    zero = jnp.zeros((CZ, LANES), jnp.float32)
    for field in range(3):
        for row in (0, 1, TALL - 2, TALL - 1):
            tall_ref[field, row] = zero
    for field, own_ref, offset, rim in (
        (0, mask_ref, 0, MASK_RIM),
        (1, helm_ref, MASK_RIM, RIGHT_RIM),
        (2, right_ref, MASK_RIM + RIGHT_RIM, RIGHT_RIM),
    ):
        for row in range(rim):
            tall_ref[field, RIM - rim + row] = before_ref[offset + row]
            tall_ref[field, RIM + ROWS + row] = after_ref[offset + row]
        for row in range(ROWS):
            tall_ref[field, RIM + row] = brick_row(own_ref, row).astype(jnp.float32)
    lane = lax.broadcasted_iota(jnp.int32, (CZ, LANES), 1)
    for field in range(3):

        def pack(group, carry):
            first, last = zero, zero
            for k in range(GROUP):
                line = tall_ref[field, jnp.minimum(group * GROUP + k, TALL - 1)]
                here = (lane >= SIDE * k) & (lane < SIDE * (k + 1))
                one = pltpu.roll(line, SIDE * k, 1) if k else line
                two = pltpu.roll(line, (SIDE * (k + 1)) % LANES, 1) if k + 1 < GROUP else line
                first = jnp.where(here, one, first)
                last = jnp.where(here, two, last)
            first_ref[field * PACKED + group] = first
            last_ref[field * PACKED + group] = last
            return carry

        lax.fori_loop(0, PACKED, pack, 0)


def rows_loop(start, stop, chunk, step):
    count = (stop - start) // chunk
    assert count * chunk == stop - start

    def body(index, carry):
        step(start + index * chunk, chunk)
        return carry

    lax.fori_loop(0, count, body, 0)


def cycle_kernel(
    eig_low_ref,
    eig_high_ref,
    tall_ref,
    left_ref,
    right_ref,
    pressure_out,
    residual_out,
    wet,
    flow,
    flow_next,
    helm,
    rhs,
    diag,
    base,
    gain,
    state,
    wet_c,
    masked,
    masked_next,
    diag_c,
    inverse_c,
    remain,
    error,
    direction,
    pressure_ref,
    residual_ref,
    out_sem,
):
    lane = lax.broadcasted_iota(jnp.int32, (CZ, LANES), 1)
    level = lax.broadcasted_iota(jnp.int32, (CZ, LANES), 0)
    zero = jnp.zeros((CZ, LANES), jnp.float32)
    tiles = (0, 1)

    def put(ref, tile, row, value):
        ref[tile, pl.ds(row * PITCH + CZ, CZ), :] = value

    def get(ref, tile, row, shift=0):
        return ref[tile, pl.ds(row * PITCH + (CZ + shift), CZ), :]

    def clear(ref, first, last):
        def body(row, carry):
            for tile in tiles:
                ref[tile, pl.ds(row * PITCH, CZ), :] = zero
            return carry

        lax.fori_loop(first, last + 1, body, 0, unroll=8)

    for ref in (wet, flow, flow_next):
        clear(ref, 0, TALL)
    for ref in (wet_c, masked, masked_next):
        clear(ref, 0, TALL // 2)

    def beside(main, side, reach):
        low, high = lane < reach, lane >= LANES - reach
        main_up, side_up = pltpu.roll(main, reach, 1), pltpu.roll(side, reach, 1)
        main_down = pltpu.roll(main, LANES - reach, 1)
        side_down = pltpu.roll(side, LANES - reach, 1)
        return (
            (jnp.where(low, side_up, main_up), jnp.where(high, side_down, main_down)),
            (jnp.where(low, main_up, side_up), jnp.where(high, main_down, side_down)),
        )

    def near_rows(ref, row, count, reach):
        lines = [[get(ref, tile, row + k - 1) for tile in tiles] for k in range(2)]
        for k in range(count):
            lines.append([get(ref, tile, row + k + 1) for tile in tiles])
            here = lines[k + 1]
            sides = beside(here[0], here[1], reach)
            yield [
                (lines[k][tile] + lines[k + 2][tile])
                + (get(ref, tile, row + k, -reach) + get(ref, tile, row + k, reach))
                + (sides[tile][0] + sides[tile][1])
                for tile in tiles
            ]

    def unpack(first_group, groups):
        for i in range(groups):
            group = first_group + i
            for field in range(3):
                after = right_ref[field * PACKED + group]
                ahead = pltpu.roll(left_ref[field * PACKED + group], LANES - SIDE, 1)
                for k in range(GROUP):
                    row = jnp.minimum(group * GROUP + k, TALL - 1)
                    low, high = SIDE * k, SIDE * (k + 1)
                    beyond = (low - SIDE) % LANES
                    both = jnp.where((lane >= beyond) & (lane < beyond + SIDE), ahead, 0.0)
                    both = jnp.where((lane >= low) & (lane < high), after, both)
                    if k:
                        both = pltpu.roll(both, LANES - low, 1)
                    main = tall_ref[field, row]
                    if field == 0:
                        put(wet, 0, row, main)
                        put(wet, 1, row, both)
                    else:
                        dest = (helm, rhs)[field - 1]
                        dest[0, row] = main
                        dest[1, row] = both

    rows_loop(0, PACKED, 2, unpack)

    def smooth_setup(row, chunk):
        for k, count in enumerate(near_rows(wet, row, chunk, 1)):
            for tile in tiles:
                water = get(wet, tile, row + k)
                scale = water * (helm[tile, row + k] + count[tile]) + (1.0 - water)
                inverse = 0.8 / scale
                start = inverse * rhs[tile, row + k]
                diag[tile, row + k] = scale
                base[tile, row + k] = start
                gain[tile, row + k] = inverse * water
                put(flow, tile, row + k, water * start)

    rows_loop(2, 58, 14, smooth_setup)

    def smooth_second(row, chunk):
        for k, near in enumerate(near_rows(flow, row, chunk, 1)):
            for tile in tiles:
                value = 1.2 * base[tile, row + k] + gain[tile, row + k] * near[tile]
                state[tile, row + k] = value
                put(flow_next, tile, row + k, get(wet, tile, row + k) * value)

    rows_loop(3, 57, 18, smooth_second)

    def pair_sum(value):
        value = value + jnp.where(
            level % 2 == 0, pltpu.roll(value, CZ - 1, 0), pltpu.roll(value, 1, 0)
        )
        return value + jnp.where(
            lane % 2 == 0, pltpu.roll(value, LANES - 1, 1), pltpu.roll(value, 1, 1)
        )

    def coarse_mask(row, chunk):
        for k in range(chunk):
            for tile in tiles:
                fine = 2 * (row + k)
                total = pair_sum(get(wet, tile, fine) + get(wet, tile, fine + 1))
                put(wet_c, tile, row + k, jnp.where(total >= 3.5, 1.0, 0.0))

    rows_loop(1, 29, 14, coarse_mask)

    low = jnp.full((CZ, LANES), eig_low_ref[0], jnp.float32)
    high = jnp.full((CZ, LANES), eig_high_ref[0], jnp.float32)
    centre = 0.5 * (high + low)
    half = 0.5 * (high - low)
    sigma = centre / half
    rho = 1.0 / sigma
    start_scale = 1.0 / centre

    def coarse_setup(row, chunk):
        fine_near = near_rows(flow_next, 2 * row, 2 * chunk, 1)
        for k, count_c in enumerate(near_rows(wet_c, row, chunk, 2)):
            source, shift = [zero, zero], [zero, zero]
            for fine in (2 * (row + k), 2 * (row + k) + 1):
                near = next(fine_near)
                for tile in tiles:
                    left_over = rhs[tile, fine] - diag[tile, fine] * state[tile, fine]
                    source[tile] += get(wet, tile, fine) * (left_over + near[tile])
                    shift[tile] += helm[tile, fine]
            for tile in tiles:
                first_sum = 0.125 * pair_sum(source[tile])
                water_c = get(wet_c, tile, row + k)
                scale = water_c * (0.125 * pair_sum(shift[tile]) + 0.25 * count_c[tile])
                scale = scale + (1.0 - water_c)
                inverse = 1.0 / scale
                first = first_sum * inverse * start_scale
                diag_c[tile, row + k] = scale
                inverse_c[tile, row + k] = inverse
                remain[tile, row + k] = first_sum
                error[tile, row + k] = first
                direction[tile, row + k] = first
                put(masked, tile, row + k, water_c * first)

    rows_loop(2, 28, 13, coarse_setup)

    now, later = masked, masked_next
    for sweep in range(1, CHEB):
        rho_next = 1.0 / (2.0 * sigma - rho)
        keep = rho_next * rho
        add = 2.0 * rho_next / half

        def chebyshev(row, chunk, keep=keep, add=add, now=now, later=later):
            for k, near in enumerate(near_rows(now, row, chunk, 2)):
                for tile in tiles:
                    old = direction[tile, row + k]
                    water_c = get(wet_c, tile, row + k)
                    image = diag_c[tile, row + k] * old - 0.25 * water_c * near[tile]
                    left_over = remain[tile, row + k] - image
                    fresh = keep * old + add * (left_over * inverse_c[tile, row + k])
                    remain[tile, row + k] = left_over
                    direction[tile, row + k] = fresh
                    error[tile, row + k] = error[tile, row + k] + fresh
                    put(later, tile, row + k, water_c * fresh)

        rows_loop(2 + sweep, 28 - sweep, 13 - sweep, chebyshev)
        rho = rho_next
        now, later = later, now

    def spread(row, chunk):
        for k in range(chunk):
            value = [error[tile, row + k] for tile in tiles]
            sides = beside(value[0], value[1], 1)
            for tile in tiles:
                line = 0.75 * value[tile] + 0.25 * jnp.where(
                    lane % 2 == 0, sides[tile][0], sides[tile][1]
                )
                other = jnp.where(level % 2 == 0, pltpu.roll(line, 1, 0), pltpu.roll(line, CZ - 1, 0))
                other = jnp.where((level == 0) | (level == CZ - 1), 0.0, other)
                direction[tile, row + k] = 0.75 * line + 0.25 * other

    rows_loop(5, 25, 10, spread)

    def correct(row, chunk):
        for k in range(chunk):
            for tile in tiles:
                here = 0.75 * direction[tile, row + k]
                for fine, side in ((2 * (row + k), row + k - 1), (2 * (row + k) + 1, row + k + 1)):
                    water = get(wet, tile, fine)
                    value = state[tile, fine] + water * (here + 0.25 * direction[tile, side])
                    state[tile, fine] = value
                    put(flow, tile, fine, water * value)

    rows_loop(5, 25, 10, correct)

    def smooth(now, later):
        def step(row, chunk):
            for k, near in enumerate(near_rows(now, row, chunk, 1)):
                for tile in tiles:
                    value = 0.2 * state[tile, row + k] + base[tile, row + k]
                    value = value + gain[tile, row + k] * near[tile]
                    state[tile, row + k] = value
                    put(later, tile, row + k, get(wet, tile, row + k) * value)

        return step

    rows_loop(12, 48, 12, smooth(flow, flow_next))
    rows_loop(13, 47, 17, smooth(flow_next, flow))

    def finish_pressure(row, chunk):
        for k in range(chunk):
            pressure_ref[pl.ds(row + k - RIM, CZ, stride=ROWS), :] = state[0, row + k]

    rows_loop(RIM, RIM + ROWS, 16, finish_pressure)
    pressure_copy = pltpu.make_async_copy(pressure_ref, pressure_out, out_sem.at[0])
    pressure_copy.start()

    def finish(row, chunk):
        for k, near in enumerate(near_rows(flow, row, chunk, 1)):
            left_over = rhs[0, row + k] - diag[0, row + k] * state[0, row + k]
            left_over = left_over + get(wet, 0, row + k) * near[0]
            residual_ref[pl.ds(row + k - RIM, CZ, stride=ROWS), :] = left_over

    rows_loop(RIM, RIM + ROWS, 16, finish)
    residual_copy = pltpu.make_async_copy(residual_ref, residual_out, out_sem.at[1])
    residual_copy.start()
    pressure_copy.wait()
    residual_copy.wait()


def shifted(array, axis, step):
    devices = lax.axis_size(axis)
    pairs = [(i, i + step) for i in range(devices) if 0 <= i + step < devices]
    return lax.ppermute(array, axis, pairs)


def f32(*shape):
    return jax.ShapeDtypeStruct(shape, jnp.float32)


def body(right_side, wet_mask, helmholtz, eig_low, eig_high):
    flat = (CZ * ROWS, LANES)
    right_flat = right_side.reshape(flat)
    mask_flat = wet_mask.reshape(flat)
    helm_flat = helmholtz.reshape(flat)
    limits = pltpu.CompilerParams(vmem_limit_bytes=24 * 1024 * 1024)

    first, last = pl.pallas_call(
        strips_kernel,
        out_shape=(f32(STRIP, CZ, LANES),) * 2,
        in_specs=[VMEM] * 3,
        out_specs=(VMEM,) * 2,
        compiler_params=limits,
        name="strips",
    )(right_flat, mask_flat, helm_flat)
    before = shifted(last, "wide", 1)
    after = shifted(first, "wide", -1)

    tall, first, last = pl.pallas_call(
        sides_kernel,
        out_shape=(
            f32(3, TALL, CZ, LANES),
            f32(3 * PACKED, CZ, LANES),
            f32(3 * PACKED, CZ, LANES),
        ),
        in_specs=[VMEM] * 5,
        out_specs=(VMEM,) * 3,
        compiler_params=limits,
        name="sides",
    )(right_flat, mask_flat, helm_flat, before, after)
    from_left = shifted(last, "narrow", 1)
    from_right = shifted(first, "narrow", -1)

    pressure, residual = pl.pallas_call(
        cycle_kernel,
        out_shape=(f32(*flat),) * 2,
        in_specs=[SMEM] * 2 + [VMEM] * 3,
        out_specs=(ANY,) * 2,
        scratch_shapes=[pltpu.VMEM((2, TALL * PITCH + CZ, LANES), jnp.float32)] * 3
        + [pltpu.VMEM((2, TALL, CZ, LANES), jnp.float32)] * 6
        + [pltpu.VMEM((2, TALL // 2 * PITCH + CZ, LANES), jnp.float32)] * 3
        + [pltpu.VMEM((2, TALL // 2, CZ, LANES), jnp.float32)] * 5
        + [pltpu.VMEM(flat, jnp.float32)] * 2
        + [pltpu.SemaphoreType.DMA((2,))],
        compiler_params=limits,
        name="cycle",
    )(eig_low, eig_high, tall, from_left, from_right)
    shape = (CZ, ROWS, LANES)
    return pressure.reshape(shape), residual.reshape(shape)


def solution(mesh):
    field = P(None, "wide", "narrow")
    return jax.shard_map(
        body,
        mesh=mesh,
        in_specs=(field, field, field, P(), P()),
        out_specs=(field, field),
        check_vma=False,
    )
```

time: 49.3 us -> 39.4 us (0.80)
  Pallas kernels: 19.3 us -> 9.31 us
    pallas_call x1, Pallas kernels: 16.8 us -> 6.88 us  [body(): pl.pallas_call(cycle_kernel, out_shape=(f32(*flat),) * 2, in_specs=[SMEM]...]
where the time goes in v2:
time: 39.4 us; the launch traced here: 39.1 us
  starting transfers between devices  19.8 us (50%)
  Pallas kernels  9.31 us (24%)
  waiting for transfers between devices  5.29 us (13%)
  local copies, waits for them, and re-layouts  2.7 us (7%)
  between operations  1.98 us (5%)
    ppermute x4, starting transfers between devices, shifted(): return lax.ppermute(array, axis, pairs)  19.8 us
    pallas_call x1, Pallas kernels, body(): pl.pallas_call(cycle_kernel, out_shape=(f32(*flat),) * 2, in_specs=[SMEM]...  6.88 us
    ppermute x4, waiting for transfers between devices, shifted(): return lax.ppermute(array, axis, pairs)  5.29 us
    unnamed x6, local copies, waits for them, and re-layouts  2.7 us
    pallas_call x1, Pallas kernels, body(): pl.pallas_call(sides_kernel, out_shape=(f32(3, TALL, CZ, LANES), f32(3 *...  2.25 us
  transfers between devices with their start and end apart: 4, of which 3 were waited for; matrix products, arithmetic and copies ran while one was open for 0% of the time, Pallas kernels for 0%

profile of v2, /device:TPU:57, one launch (start us, length us, event | category | flops | bytes accessed | tf_op | source)
XLA Modules:
  0.0 39.1 jit_solution(512946080231214755)
XLA Ops:
  0.6 0.0 copy-start
  0.6 0.9 %copy-done = f32[8,32,128]{2,1,0:T(8,128)S(1)} copy-done((f32[8,32,128]{2,1,0:T(8,128)S(1)}, f32[8,32,128]{2,1,0:T(8,128)}, u32[]{:S(2)}) %copy-start) | copy-done | bytes 131096
  1.5 0.0 copy-start.1
  1.5 0.9 %copy-done.1 = s32[8,32,128]{2,1,0:T(8,128)S(1)} copy-done((s32[8,32,128]{2,1,0:T(8,128)S(1)}, s32[8,32,128]{2,1,0:T(8,128)}, u32[]{:S(2)}) %copy-start.1) | copy-done | bytes 131096
  2.4 0.0 copy-start.2
  2.4 0.9 %copy-done.2 = f32[8,32,128]{2,1,0:T(8,128)S(1)} copy-done((f32[8,32,128]{2,1,0:T(8,128)S(1)}, f32[8,32,128]{2,1,0:T(8,128)}, u32[]{:S(2)}) %copy-start.2) | copy-done | bytes 131096
  3.3 0.2 strips.1
  3.5 4.0 %collective-permute-start = (f32[37,8,128]{2,1,0:T(8,128)S(1)}, f32[37,8,128]{2,1,0:T(8,128)S(1)}, u32[]{:S(2)}, u32[]{:S(2)}) collective-permute-start(f32[37,8,128]{2,1,0:T(8,128)S(1)} %get-tuple-element.9), channel_id=1, source_target_pairs={{0,8},{8,16},{16,24},{24,32},{32,40},{40,48},{48,56},{56,64},{64,7... | collective-permute-start | bytes 454664 | tf_op jit(solution)/shard_map/ppermute | solution.py:355
  7.5 9.4 %collective-permute-start.1 = (f32[37,8,128]{2,1,0:T(8,128)S(1)}, f32[37,8,128]{2,1,0:T(8,128)S(1)}, u32[]{:S(2)}, u32[]{:S(2)}) collective-permute-start(f32[37,8,128]{2,1,0:T(8,128)S(1)} %get-tuple-element.10), channel_id=1, source_target_pairs={{8,0},{16,8},{24,16},{32,24},{40,32},{48,40},{56,48},{64,56},{72,6... | collective-permute-start | bytes 454664 | tf_op jit(solution)/shard_map/ppermute | solution.py:355
  16.9 1.7 %collective-permute-done.before_ref = f32[37,8,128]{2,1,0:T(8,128)S(1)} collective-permute-done((f32[37,8,128]{2,1,0:T(8,128)S(1)}, f32[37,8,128]{2,1,0:T(8,128)S(1)}, u32[]{:S(2)}, u32[]{:S(2)}) %collective-permute-start) | collective-permute-done | bytes 151584 | tf_op jit(solution)/shard_map/ppermute | solution.py:355
  18.6 0.9 %collective-permute-done.1.after_ref = f32[37,8,128]{2,1,0:T(8,128)S(1)} collective-permute-done((f32[37,8,128]{2,1,0:T(8,128)S(1)}, f32[37,8,128]{2,1,0:T(8,128)S(1)}, u32[]{:S(2)}, u32[]{:S(2)}) %collective-permute-start.1) | collective-permute-done | bytes 151584 | tf_op jit(solution)/shard_map/ppermute | solution.py:355
  19.5 2.2 %sides.1 = (f32[3,60,8,128]{3,2,1,0:T(8,128)S(1)}, f32[24,8,128]{2,1,0:T(8,128)S(1)}, f32[24,8,128]{2,1,0:T(8,128)S(1)}) custom-call(f32[256,128]{1,0:T(8,128)S(1)} %bitcast.6, s32[256,128]{1,0:T(8,128)S(1)} %bitcast.8, f32[256,128]{1,0:T(8,128)S(1)} %bitcast.10, f32[37,8,128]{2,1,0:T(8,128)S(1)} %collective-permute-done.before_ref, ...), custom_call_target="tpu_custom_call" | custom-call | tf_op jit(solution)/shard_map/sides/pallas_call | solution.py:380
  21.8 4.6 %collective-permute-start.2 = (f32[24,8,128]{2,1,0:T(8,128)S(1)}, f32[24,8,128]{2,1,0:T(8,128)S(1)}, u32[]{:S(2)}, u32[]{:S(2)}) collective-permute-start(f32[24,8,128]{2,1,0:T(8,128)S(1)} %get-tuple-element.12), channel_id=1, source_target_pairs={{0,1},{1,2},{2,3},{3,4},{4,5},{5,6},{6,7},{8,9},{9,10},{10,11},{11... | collective-permute-start | bytes 294920 | tf_op jit(solution)/shard_map/ppermute | solution.py:355
  26.3 1.9 %collective-permute-start.3 = (f32[24,8,128]{2,1,0:T(8,128)S(1)}, f32[24,8,128]{2,1,0:T(8,128)S(1)}, u32[]{:S(2)}, u32[]{:S(2)}) collective-permute-start(f32[24,8,128]{2,1,0:T(8,128)S(1)} %get-tuple-element.13), channel_id=1, source_target_pairs={{1,0},{2,1},{3,2},{4,3},{5,4},{6,5},{7,6},{9,8},{10,9},{11,10},{12... | collective-permute-start | bytes 294920 | tf_op jit(solution)/shard_map/ppermute | solution.py:355
  29.5 0.0 collective-permute-done.2.left_ref
  29.5 2.7 %collective-permute-done.3.right_ref = f32[24,8,128]{2,1,0:T(8,128)S(1)} collective-permute-done((f32[24,8,128]{2,1,0:T(8,128)S(1)}, f32[24,8,128]{2,1,0:T(8,128)S(1)}, u32[]{:S(2)}, u32[]{:S(2)}) %collective-permute-start.3) | collective-permute-done | bytes 98336 | tf_op jit(solution)/shard_map/ppermute | solution.py:355
  32.2 6.9 %cycle.1 = (f32[256,128]{1,0:T(8,128)}, f32[256,128]{1,0:T(8,128)}) custom-call(f32[1]{0:T(128)S(6)} %copy.7.eig_low_ref, f32[1]{0:T(128)S(6)} %copy.8.eig_high_ref, f32[3,60,8,128]{3,2,1,0:T(8,128)S(1)} %get-tuple-element.11.tall_ref, f32[24,8,128]{2,1,0:T(8,128)S(1)} %collective-permute-done.2.left_ref, f32[24,8,128]{2,1,0:T(8,128)S(1)} %collective-permute-done.3.right_ref), custom_call_target="tpu_custom_call" | custom-call | tf_op jit(solution)/shard_map/cycle/pallas_call | solution.py:395
Async XLA Ops:
  0.6 0.9 %copy-start = (f32[8,32,128]{2,1,0:T(8,128)S(1)}, f32[8,32,128]{2,1,0:T(8,128)}, u32[]{:S(2)}) copy-start(f32[8,32,128]{2,1,0:T(8,128)} %param.5) | copy-start | bytes 393220
  1.5 0.9 %copy-start.1 = (s32[8,32,128]{2,1,0:T(8,128)S(1)}, s32[8,32,128]{2,1,0:T(8,128)}, u32[]{:S(2)}) copy-start(s32[8,32,128]{2,1,0:T(8,128)} %param.6) | copy-start | bytes 393220
  2.4 0.9 %copy-start.2 = (f32[8,32,128]{2,1,0:T(8,128)S(1)}, f32[8,32,128]{2,1,0:T(8,128)}, u32[]{:S(2)}) copy-start(f32[8,32,128]{2,1,0:T(8,128)} %param.7) | copy-start | bytes 393220
  3.5 15.1 %collective-permute-start = (f32[37,8,128]{2,1,0:T(8,128)S(1)}, f32[37,8,128]{2,1,0:T(8,128)S(1)}, u32[]{:S(2)}, u32[]{:S(2)}) collective-permute-start(f32[37,8,128]{2,1,0:T(8,128)S(1)} %get-tuple-element.9), channel_id=1, source_target_pairs={{0,8},{8,16},{16,24},{24,32},{32,40},{40,48},{48,56},{56,64},{64,7... | collective-permute-start | bytes 454664 | tf_op jit(solution)/shard_map/ppermute | solution.py:355
  7.5 12.0 %collective-permute-start.1 = (f32[37,8,128]{2,1,0:T(8,128)S(1)}, f32[37,8,128]{2,1,0:T(8,128)S(1)}, u32[]{:S(2)}, u32[]{:S(2)}) collective-permute-start(f32[37,8,128]{2,1,0:T(8,128)S(1)} %get-tuple-element.10), channel_id=1, source_target_pairs={{8,0},{16,8},{24,16},{32,24},{40,32},{48,40},{56,48},{64,56},{72,6... | collective-permute-start | bytes 454664 | tf_op jit(solution)/shard_map/ppermute | solution.py:355
  21.8 7.8 %collective-permute-start.2 = (f32[24,8,128]{2,1,0:T(8,128)S(1)}, f32[24,8,128]{2,1,0:T(8,128)S(1)}, u32[]{:S(2)}, u32[]{:S(2)}) collective-permute-start(f32[24,8,128]{2,1,0:T(8,128)S(1)} %get-tuple-element.12), channel_id=1, source_target_pairs={{0,1},{1,2},{2,3},{3,4},{4,5},{5,6},{6,7},{8,9},{9,10},{10,11},{11... | collective-permute-start | bytes 294920 | tf_op jit(solution)/shard_map/ppermute | solution.py:355
  26.3 5.9 %collective-permute-start.3 = (f32[24,8,128]{2,1,0:T(8,128)S(1)}, f32[24,8,128]{2,1,0:T(8,128)S(1)}, u32[]{:S(2)}, u32[]{:S(2)}) collective-permute-start(f32[24,8,128]{2,1,0:T(8,128)S(1)} %get-tuple-element.13), channel_id=1, source_target_pairs={{1,0},{2,1},{3,2},{4,3},{5,4},{6,5},{7,6},{9,8},{10,9},{11,10},{12... | collective-permute-start | bytes 294920 | tf_op jit(solution)/shard_map/ppermute | solution.py:355

commit v3 on v2

--- a/solution.py
+++ b/solution.py
@@ -23,60 +23,80 @@
 PITCH = 2 * CZ
 
 VMEM = pl.BlockSpec(memory_space=pltpu.VMEM)
-ANY = pl.BlockSpec(memory_space=pl.ANY)
 SMEM = pl.BlockSpec(memory_space=pltpu.SMEM)
+HBM = pl.BlockSpec(memory_space=pltpu.HBM)
 
 
 def brick_row(ref, row):
     return ref[pl.ds(row, CZ, stride=ROWS), :]
 
 
-def strips_kernel(right_ref, mask_ref, helm_ref, first_ref, last_ref):
-    for out_ref, mask_from, other_from in (
-        (first_ref, 0, 0),
-        (last_ref, ROWS - MASK_RIM, ROWS - RIGHT_RIM),
+def strips_kernel(
+    right_hbm, mask_hbm, helm_hbm, first_ref, last_ref, own_ref, mask_ref, helm_ref, right_ref, sem
+):
+    copies = [
+        pltpu.make_async_copy(source, dest, sem.at[k])
+        for k, (source, dest) in enumerate(
+            ((mask_hbm, mask_ref), (helm_hbm, helm_ref), (right_hbm, right_ref))
+        )
+    ]
+    for copy in copies:
+        copy.start()
+    for field, (ref, rim, offset) in enumerate(
+        (
+            (mask_ref, MASK_RIM, 0),
+            (helm_ref, RIGHT_RIM, MASK_RIM),
+            (right_ref, RIGHT_RIM, MASK_RIM + RIGHT_RIM),
+        )
     ):
-        for row in range(MASK_RIM):
-            out_ref[row] = brick_row(mask_ref, mask_from + row).astype(jnp.float32)
-        for row in range(RIGHT_RIM):
-            out_ref[MASK_RIM + row] = brick_row(helm_ref, other_from + row)
-            out_ref[MASK_RIM + RIGHT_RIM + row] = brick_row(right_ref, other_from + row)
+        copies[field].wait()
+        for row in range(ROWS):
+            line = brick_row(ref, row).astype(jnp.float32)
+            own_ref[field, row] = line
+            if row < rim:
+                first_ref[offset + row] = line
+            if row >= ROWS - rim:
+                last_ref[offset + row - (ROWS - rim)] = line
 
 
 def sides_kernel(
-    right_ref, mask_ref, helm_ref, before_ref, after_ref, tall_ref, first_ref, last_ref
+    low_ref, high_ref, own_ref, before_ref, after_ref, tall_ref, first_ref, last_ref, eig_ref
 ):
+    eig_ref[0] = jnp.full((CZ, LANES), low_ref[0], jnp.float32)
+    eig_ref[1] = jnp.full((CZ, LANES), high_ref[0], jnp.float32)
     zero = jnp.zeros((CZ, LANES), jnp.float32)
-    for field in range(3):
+    lane = lax.broadcasted_iota(jnp.int32, (CZ, LANES), 1)
+    for field, offset, rim in (
+        (0, 0, MASK_RIM),
+        (1, MASK_RIM, RIGHT_RIM),
+        (2, MASK_RIM + RIGHT_RIM, RIGHT_RIM),
+    ):
         for row in (0, 1, TALL - 2, TALL - 1):
             tall_ref[field, row] = zero
-    for field, own_ref, offset, rim in (
-        (0, mask_ref, 0, MASK_RIM),
-        (1, helm_ref, MASK_RIM, RIGHT_RIM),
-        (2, right_ref, MASK_RIM + RIGHT_RIM, RIGHT_RIM),
-    ):
         for row in range(rim):
             tall_ref[field, RIM - rim + row] = before_ref[offset + row]
             tall_ref[field, RIM + ROWS + row] = after_ref[offset + row]
         for row in range(ROWS):
-            tall_ref[field, RIM + row] = brick_row(own_ref, row).astype(jnp.float32)
-    lane = lax.broadcasted_iota(jnp.int32, (CZ, LANES), 1)
-    for field in range(3):
-
-        def pack(group, carry):
-            first, last = zero, zero
-            for k in range(GROUP):
-                line = tall_ref[field, jnp.minimum(group * GROUP + k, TALL - 1)]
-                here = (lane >= SIDE * k) & (lane < SIDE * (k + 1))
-                one = pltpu.roll(line, SIDE * k, 1) if k else line
-                two = pltpu.roll(line, (SIDE * (k + 1)) % LANES, 1) if k + 1 < GROUP else line
-                first = jnp.where(here, one, first)
-                last = jnp.where(here, two, last)
-            first_ref[field * PACKED + group] = first
-            last_ref[field * PACKED + group] = last
-            return carry
-
-        lax.fori_loop(0, PACKED, pack, 0)
+            tall_ref[field, RIM + row] = own_ref[field, row]
+
+    def pack(first_group, groups):
+        for i in range(groups):
+            group = first_group + i
+            for field in range(3):
+                first, last = [], []
+                for k in range(GROUP):
+                    line = tall_ref[field, jnp.minimum(group * GROUP + k, TALL - 1)]
+                    here = (lane >= SIDE * k) & (lane < SIDE * (k + 1))
+                    one = pltpu.roll(line, SIDE * k, 1) if k else line
+                    two = pltpu.roll(line, SIDE * (k + 1), 1) if k + 1 < GROUP else line
+                    first.append(jnp.where(here, one, 0.0))
+                    last.append(jnp.where(here, two, 0.0))
+                for ref, parts in ((first_ref, first), (last_ref, last)):
+                    while len(parts) > 1:
+                        parts = [x + y for x, y in zip(parts[::2], parts[1::2])]
+                    ref[field * PACKED + group] = parts[0]
+
+    rows_loop(0, PACKED, 2, pack)
 
 
 def rows_loop(start, stop, chunk, step):
@@ -91,8 +111,7 @@
 
 
 def cycle_kernel(
-    eig_low_ref,
-    eig_high_ref,
+    eig_ref,
     tall_ref,
     left_ref,
     right_ref,
@@ -231,8 +250,7 @@
 
     rows_loop(1, 29, 14, coarse_mask)
 
-    low = jnp.full((CZ, LANES), eig_low_ref[0], jnp.float32)
-    high = jnp.full((CZ, LANES), eig_high_ref[0], jnp.float32)
+    low, high = eig_ref[0], eig_ref[1]
     centre = 0.5 * (high + low)
     half = 0.5 * (high - low)
     sigma = centre / half
@@ -355,6 +373,10 @@
     return lax.ppermute(array, axis, pairs)
 
 
+def in_hbm(array):
+    return pltpu.with_memory_space_constraint(array, pltpu.HBM)
+
+
 def f32(*shape):
     return jax.ShapeDtypeStruct(shape, jnp.float32)
 
@@ -366,37 +388,44 @@
     helm_flat = helmholtz.reshape(flat)
     limits = pltpu.CompilerParams(vmem_limit_bytes=24 * 1024 * 1024)
 
-    first, last = pl.pallas_call(
+    first, last, own = pl.pallas_call(
         strips_kernel,
-        out_shape=(f32(STRIP, CZ, LANES),) * 2,
-        in_specs=[VMEM] * 3,
-        out_specs=(VMEM,) * 2,
+        out_shape=(f32(STRIP, CZ, LANES), f32(STRIP, CZ, LANES), f32(3, ROWS, CZ, LANES)),
+        in_specs=[HBM] * 3,
+        out_specs=(VMEM,) * 3,
+        scratch_shapes=[
+            pltpu.VMEM(flat, jnp.int32),
+            pltpu.VMEM(flat, jnp.float32),
+            pltpu.VMEM(flat, jnp.float32),
+            pltpu.SemaphoreType.DMA((3,)),
+        ],
         compiler_params=limits,
         name="strips",
-    )(right_flat, mask_flat, helm_flat)
+    )(in_hbm(right_flat), in_hbm(mask_flat), in_hbm(helm_flat))
     before = shifted(last, "wide", 1)
     after = shifted(first, "wide", -1)
 
-    tall, first, last = pl.pallas_call(
+    tall, first, last, eigs = pl.pallas_call(
         sides_kernel,
         out_shape=(
             f32(3, TALL, CZ, LANES),
             f32(3 * PACKED, CZ, LANES),
             f32(3 * PACKED, CZ, LANES),
+            f32(2, CZ, LANES),
         ),
-        in_specs=[VMEM] * 5,
-        out_specs=(VMEM,) * 3,
+        in_specs=[SMEM] * 2 + [VMEM] * 3,
+        out_specs=(VMEM,) * 4,
         compiler_params=limits,
         name="sides",
-    )(right_flat, mask_flat, helm_flat, before, after)
+    )(eig_low, eig_high, own, before, after)
     from_left = shifted(last, "narrow", 1)
     from_right = shifted(first, "narrow", -1)
 
     pressure, residual = pl.pallas_call(
         cycle_kernel,
         out_shape=(f32(*flat),) * 2,
-        in_specs=[SMEM] * 2 + [VMEM] * 3,
-        out_specs=(ANY,) * 2,
+        in_specs=[VMEM] * 4,
+        out_specs=(HBM,) * 2,
         scratch_shapes=[pltpu.VMEM((2, TALL * PITCH + CZ, LANES), jnp.float32)] * 3
         + [pltpu.VMEM((2, TALL, CZ, LANES), jnp.float32)] * 6
         + [pltpu.VMEM((2, TALL // 2 * PITCH + CZ, LANES), jnp.float32)] * 3
@@ -405,7 +434,7 @@
         + [pltpu.SemaphoreType.DMA((2,))],
         compiler_params=limits,
         name="cycle",
-    )(eig_low, eig_high, tall, from_left, from_right)
+    )(eigs, tall, from_left, from_right)
     shape = (CZ, ROWS, LANES)
     return pressure.reshape(shape), residual.reshape(shape)
 

time: 39.4 us -> 36.1 us (0.916)
  local copies, waits for them, and re-layouts: 2.7 us -> 0 us
  Pallas kernels: 9.31 us -> 8.75 us
    unnamed x6 -> x0, local copies, waits for them, and re-layouts: 2.7 us -> none
    pallas_call x1, Pallas kernels: 2.25 us -> 0.69 us  [body(): pl.pallas_call(sides_kernel, out_shape=(f32(3, TALL, CZ, LANES), f32(3 *...]
    pallas_call x2, Pallas kernels: 7.06 us -> 8.06 us  [the longest x1 6.88 us: body(): pl.pallas_call(cycle_kernel, out_shape=(f32(*flat),) * 2, in_specs=[VMEM]...]
where the time goes in v3:
time: 36.1 us; the launch traced here: 35.9 us
  starting transfers between devices  19.8 us (55%)
  Pallas kernels  8.75 us (24%)
  waiting for transfers between devices  5.29 us (15%)
  between operations  1.98 us (5%)
    ppermute x4, starting transfers between devices, shifted(): return lax.ppermute(array, axis, pairs)  19.8 us
    pallas_call x1, Pallas kernels, body(): pl.pallas_call(cycle_kernel, out_shape=(f32(*flat),) * 2, in_specs=[VMEM]...  6.88 us
    ppermute x4, waiting for transfers between devices, shifted(): return lax.ppermute(array, axis, pairs)  5.29 us
    pallas_call x1, Pallas kernels, body(): pl.pallas_call(strips_kernel, out_shape=(f32(STRIP, CZ, LANES), f32(STRIP...  1.18 us
  transfers between devices with their start and end apart: 4, of which 3 were waited for; matrix products, arithmetic and copies ran while one was open for 0% of the time, Pallas kernels for 0%

profile of v3, /device:TPU:57, one launch (start us, length us, event | category | flops | bytes accessed | tf_op | source)
XLA Modules:
  0.0 35.9 jit_solution(10957311978738883507)
XLA Ops:
  0.6 1.2 %strips.1 = (f32[37,8,128]{2,1,0:T(8,128)S(1)}, f32[37,8,128]{2,1,0:T(8,128)S(1)}, f32[3,32,8,128]{3,2,1,0:T(8,128)S(1)}) custom-call(f32[256,128]{1,0:T(8,128)} %bitcast.5, s32[256,128]{1,0:T(8,128)} %bitcast.6, f32[256,128]{1,0:T(8,128)} %bitcast.7), custom_call_target="tpu_custom_call" | custom-call | tf_op jit(solution)/shard_map/strips/pallas_call | solution.py:391
  1.8 4.0 %collective-permute-start = (f32[37,8,128]{2,1,0:T(8,128)S(1)}, f32[37,8,128]{2,1,0:T(8,128)S(1)}, u32[]{:S(2)}, u32[]{:S(2)}) collective-permute-start(f32[37,8,128]{2,1,0:T(8,128)S(1)} %get-tuple-element.12), channel_id=1, source_target_pairs={{0,8},{8,16},{16,24},{24,32},{32,40},{40,48},{48,56},{56,64},{64,7... | collective-permute-start | bytes 454664 | tf_op jit(solution)/shard_map/ppermute | solution.py:373
  5.8 9.4 %collective-permute-start.1 = (f32[37,8,128]{2,1,0:T(8,128)S(1)}, f32[37,8,128]{2,1,0:T(8,128)S(1)}, u32[]{:S(2)}, u32[]{:S(2)}) collective-permute-start(f32[37,8,128]{2,1,0:T(8,128)S(1)} %get-tuple-element.13), channel_id=1, source_target_pairs={{8,0},{16,8},{24,16},{32,24},{40,32},{48,40},{56,48},{64,56},{72,6... | collective-permute-start | bytes 454664 | tf_op jit(solution)/shard_map/ppermute | solution.py:373
  16.5 0.4 %collective-permute-done.before_ref = f32[37,8,128]{2,1,0:T(8,128)S(1)} collective-permute-done((f32[37,8,128]{2,1,0:T(8,128)S(1)}, f32[37,8,128]{2,1,0:T(8,128)S(1)}, u32[]{:S(2)}, u32[]{:S(2)}) %collective-permute-start) | collective-permute-done | bytes 151584 | tf_op jit(solution)/shard_map/ppermute | solution.py:373
  16.9 0.9 %collective-permute-done.1.after_ref = f32[37,8,128]{2,1,0:T(8,128)S(1)} collective-permute-done((f32[37,8,128]{2,1,0:T(8,128)S(1)}, f32[37,8,128]{2,1,0:T(8,128)S(1)}, u32[]{:S(2)}, u32[]{:S(2)}) %collective-permute-start.1) | collective-permute-done | bytes 151584 | tf_op jit(solution)/shard_map/ppermute | solution.py:373
  17.8 0.7 %sides.1 = (f32[3,60,8,128]{3,2,1,0:T(8,128)S(1)}, f32[24,8,128]{2,1,0:T(8,128)S(1)}, f32[24,8,128]{2,1,0:T(8,128)S(1)}, f32[2,8,128]{2,1,0:T(8,128)S(1)}) custom-call(f32[1]{0:T(128)S(6)} %copy.7.low_ref, f32[1]{0:T(128)S(6)} %copy.8.high_ref, f32[3,32,8,128]{3,2,1,0:T(8,128)S(1)} %get-tuple-element.11.own_ref, ...), custom_call_target="tpu_custom_call" | custom-call | tf_op jit(solution)/shard_map/sides/pallas_call | solution.py:408
  18.5 4.6 %collective-permute-start.2 = (f32[24,8,128]{2,1,0:T(8,128)S(1)}, f32[24,8,128]{2,1,0:T(8,128)S(1)}, u32[]{:S(2)}, u32[]{:S(2)}) collective-permute-start(f32[24,8,128]{2,1,0:T(8,128)S(1)} %get-tuple-element.16), channel_id=1, source_target_pairs={{0,1},{1,2},{2,3},{3,4},{4,5},{5,6},{6,7},{8,9},{9,10},{10,11},{11... | collective-permute-start | bytes 294920 | tf_op jit(solution)/shard_map/ppermute | solution.py:373
  23.0 1.9 %collective-permute-start.3 = (f32[24,8,128]{2,1,0:T(8,128)S(1)}, f32[24,8,128]{2,1,0:T(8,128)S(1)}, u32[]{:S(2)}, u32[]{:S(2)}) collective-permute-start(f32[24,8,128]{2,1,0:T(8,128)S(1)} %get-tuple-element.17), channel_id=1, source_target_pairs={{1,0},{2,1},{3,2},{4,3},{5,4},{6,5},{7,6},{9,8},{10,9},{11,10},{12... | collective-permute-start | bytes 294920 | tf_op jit(solution)/shard_map/ppermute | solution.py:373
  25.0 0.0 collective-permute-done.2.left_ref
  25.0 4.0 %collective-permute-done.3.right_ref = f32[24,8,128]{2,1,0:T(8,128)S(1)} collective-permute-done((f32[24,8,128]{2,1,0:T(8,128)S(1)}, f32[24,8,128]{2,1,0:T(8,128)S(1)}, u32[]{:S(2)}, u32[]{:S(2)}) %collective-permute-start.3) | collective-permute-done | bytes 98336 | tf_op jit(solution)/shard_map/ppermute | solution.py:373
  29.0 6.9 %cycle.1 = (f32[256,128]{1,0:T(8,128)}, f32[256,128]{1,0:T(8,128)}) custom-call(f32[2,8,128]{2,1,0:T(8,128)S(1)} %get-tuple-element.14.eig_ref, f32[3,60,8,128]{3,2,1,0:T(8,128)S(1)} %get-tuple-element.15.tall_ref, f32[24,8,128]{2,1,0:T(8,128)S(1)} %collective-permute-done.2.left_ref, f32[24,8,128]{2,1,0:T(8,128)S(1)} %collective-permute-done.3.right_ref), custom_call_target="tpu_custom_call" | custom-call | tf_op jit(solution)/shard_map/cycle/pallas_call | solution.py:424
Async XLA Ops:
  1.8 15.1 %collective-permute-start = (f32[37,8,128]{2,1,0:T(8,128)S(1)}, f32[37,8,128]{2,1,0:T(8,128)S(1)}, u32[]{:S(2)}, u32[]{:S(2)}) collective-permute-start(f32[37,8,128]{2,1,0:T(8,128)S(1)} %get-tuple-element.12), channel_id=1, source_target_pairs={{0,8},{8,16},{16,24},{24,32},{32,40},{40,48},{48,56},{56,64},{64,7... | collective-permute-start | bytes 454664 | tf_op jit(solution)/shard_map/ppermute | solution.py:373
  5.8 12.0 %collective-permute-start.1 = (f32[37,8,128]{2,1,0:T(8,128)S(1)}, f32[37,8,128]{2,1,0:T(8,128)S(1)}, u32[]{:S(2)}, u32[]{:S(2)}) collective-permute-start(f32[37,8,128]{2,1,0:T(8,128)S(1)} %get-tuple-element.13), channel_id=1, source_target_pairs={{8,0},{16,8},{24,16},{32,24},{40,32},{48,40},{56,48},{64,56},{72,6... | collective-permute-start | bytes 454664 | tf_op jit(solution)/shard_map/ppermute | solution.py:373
  18.5 6.5 %collective-permute-start.2 = (f32[24,8,128]{2,1,0:T(8,128)S(1)}, f32[24,8,128]{2,1,0:T(8,128)S(1)}, u32[]{:S(2)}, u32[]{:S(2)}) collective-permute-start(f32[24,8,128]{2,1,0:T(8,128)S(1)} %get-tuple-element.16), channel_id=1, source_target_pairs={{0,1},{1,2},{2,3},{3,4},{4,5},{5,6},{6,7},{8,9},{9,10},{10,11},{11... | collective-permute-start | bytes 294920 | tf_op jit(solution)/shard_map/ppermute | solution.py:373
  23.0 5.9 %collective-permute-start.3 = (f32[24,8,128]{2,1,0:T(8,128)S(1)}, f32[24,8,128]{2,1,0:T(8,128)S(1)}, u32[]{:S(2)}, u32[]{:S(2)}) collective-permute-start(f32[24,8,128]{2,1,0:T(8,128)S(1)} %get-tuple-element.17), channel_id=1, source_target_pairs={{1,0},{2,1},{3,2},{4,3},{5,4},{6,5},{7,6},{9,8},{10,9},{11,10},{12... | collective-permute-start | bytes 294920 | tf_op jit(solution)/shard_map/ppermute | solution.py:373

commit v4 on v3

--- a/solution.py
+++ b/solution.py
@@ -32,8 +32,9 @@
 
 
 def strips_kernel(
-    right_hbm, mask_hbm, helm_hbm, first_ref, last_ref, own_ref, mask_ref, helm_ref, right_ref, sem
+    right_hbm, mask_hbm, helm_hbm, far_ref, near_ref, own_ref, mask_ref, helm_ref, right_ref, sem
 ):
+    odd = lax.rem(lax.axis_index("wide"), 2)
     copies = [
         pltpu.make_async_copy(source, dest, sem.at[k])
         for k, (source, dest) in enumerate(
@@ -53,15 +54,17 @@
         for row in range(ROWS):
             line = brick_row(ref, row).astype(jnp.float32)
             own_ref[field, row] = line
-            if row < rim:
-                first_ref[offset + row] = line
-            if row >= ROWS - rim:
-                last_ref[offset + row - (ROWS - rim)] = line
+        to_far, to_near = (ROWS - rim) * odd, (ROWS - rim) * (1 - odd)
+        for row in range(rim):
+            far_ref[offset + row] = own_ref[field, to_far + row]
+            near_ref[offset + row] = own_ref[field, to_near + row]
 
 
 def sides_kernel(
-    low_ref, high_ref, own_ref, before_ref, after_ref, tall_ref, first_ref, last_ref, eig_ref
+    low_ref, high_ref, own_ref, far_ref, near_ref, tall_ref, far_out, near_out, eig_ref
 ):
+    odd = lax.rem(lax.axis_index("wide"), 2)
+    odd_column = lax.rem(lax.axis_index("narrow"), 2) == 1
     eig_ref[0] = jnp.full((CZ, LANES), low_ref[0], jnp.float32)
     eig_ref[1] = jnp.full((CZ, LANES), high_ref[0], jnp.float32)
     zero = jnp.zeros((CZ, LANES), jnp.float32)
@@ -73,9 +76,11 @@
     ):
         for row in (0, 1, TALL - 2, TALL - 1):
             tall_ref[field, row] = zero
+        from_far = RIM - rim + (ROWS + rim) * odd
+        from_near = RIM - rim + (ROWS + rim) * (1 - odd)
         for row in range(rim):
-            tall_ref[field, RIM - rim + row] = before_ref[offset + row]
-            tall_ref[field, RIM + ROWS + row] = after_ref[offset + row]
+            tall_ref[field, from_far + row] = far_ref[offset + row]
+            tall_ref[field, from_near + row] = near_ref[offset + row]
         for row in range(ROWS):
             tall_ref[field, RIM + row] = own_ref[field, row]
 
@@ -91,10 +96,12 @@
                     two = pltpu.roll(line, SIDE * (k + 1), 1) if k + 1 < GROUP else line
                     first.append(jnp.where(here, one, 0.0))
                     last.append(jnp.where(here, two, 0.0))
-                for ref, parts in ((first_ref, first), (last_ref, last)):
-                    while len(parts) > 1:
-                        parts = [x + y for x, y in zip(parts[::2], parts[1::2])]
-                    ref[field * PACKED + group] = parts[0]
+                while len(first) > 1:
+                    first = [x + y for x, y in zip(first[::2], first[1::2])]
+                    last = [x + y for x, y in zip(last[::2], last[1::2])]
+                place = field * PACKED + group
+                far_out[place] = jnp.where(odd_column, last[0], first[0])
+                near_out[place] = jnp.where(odd_column, first[0], last[0])
 
     rows_loop(0, PACKED, 2, pack)
 
@@ -113,8 +120,8 @@
 def cycle_kernel(
     eig_ref,
     tall_ref,
-    left_ref,
-    right_ref,
+    far_ref,
+    near_ref,
     pressure_out,
     residual_out,
     wet,
@@ -185,12 +192,15 @@
                 for tile in tiles
             ]
 
+    odd_column = lax.rem(lax.axis_index("narrow"), 2) == 1
+
     def unpack(first_group, groups):
         for i in range(groups):
             group = first_group + i
             for field in range(3):
-                after = right_ref[field * PACKED + group]
-                ahead = pltpu.roll(left_ref[field * PACKED + group], LANES - SIDE, 1)
+                far, near = far_ref[field * PACKED + group], near_ref[field * PACKED + group]
+                after = jnp.where(odd_column, far, near)
+                ahead = pltpu.roll(jnp.where(odd_column, near, far), LANES - SIDE, 1)
                 for k in range(GROUP):
                     row = jnp.minimum(group * GROUP + k, TALL - 1)
                     low, high = SIDE * k, SIDE * (k + 1)
@@ -367,10 +377,9 @@
     residual_copy.wait()
 
 
-def shifted(array, axis, step):
-    devices = lax.axis_size(axis)
-    pairs = [(i, i + step) for i in range(devices) if 0 <= i + step < devices]
-    return lax.ppermute(array, axis, pairs)
+def swapped(array, axis, first):
+    pairs = [(i, i + 1) for i in range(first, lax.axis_size(axis) - 1, 2)]
+    return lax.ppermute(array, axis, pairs + [(j, i) for i, j in pairs])
 
 
 def in_hbm(array):
@@ -388,7 +397,7 @@
     helm_flat = helmholtz.reshape(flat)
     limits = pltpu.CompilerParams(vmem_limit_bytes=24 * 1024 * 1024)
 
-    first, last, own = pl.pallas_call(
+    far, near, own = pl.pallas_call(
         strips_kernel,
         out_shape=(f32(STRIP, CZ, LANES), f32(STRIP, CZ, LANES), f32(3, ROWS, CZ, LANES)),
         in_specs=[HBM] * 3,
@@ -402,10 +411,10 @@
         compiler_params=limits,
         name="strips",
     )(in_hbm(right_flat), in_hbm(mask_flat), in_hbm(helm_flat))
-    before = shifted(last, "wide", 1)
-    after = shifted(first, "wide", -1)
-
-    tall, first, last, eigs = pl.pallas_call(
+    far = swapped(far, "wide", 1)
+    near = swapped(near, "wide", 0)
+
+    tall, far, near, eigs = pl.pallas_call(
         sides_kernel,
         out_shape=(
             f32(3, TALL, CZ, LANES),
@@ -417,9 +426,9 @@
         out_specs=(VMEM,) * 4,
         compiler_params=limits,
         name="sides",
-    )(eig_low, eig_high, own, before, after)
-    from_left = shifted(last, "narrow", 1)
-    from_right = shifted(first, "narrow", -1)
+    )(eig_low, eig_high, own, far, near)
+    far = swapped(far, "narrow", 1)
+    near = swapped(near, "narrow", 0)
 
     pressure, residual = pl.pallas_call(
         cycle_kernel,
@@ -434,7 +443,7 @@
         + [pltpu.SemaphoreType.DMA((2,))],
         compiler_params=limits,
         name="cycle",
-    )(eigs, tall, from_left, from_right)
+    )(eigs, tall, far, near)
     shape = (CZ, ROWS, LANES)
     return pressure.reshape(shape), residual.reshape(shape)
 

time: 36.1 us -> 35.6 us (0.986)
  waiting for transfers between devices: 5.29 us -> 4.42 us
  starting transfers between devices: 19.8 us -> 20.2 us
    ppermute x4, waiting for transfers between devices: 5.29 us -> 4.42 us  [swapped(): return lax.ppermute(array, axis, pairs + [(j, i) for i, j in pairs])]
  transfers between devices with their start and end apart: 4 -> 4, of which waited for: 3 -> 4; matrix products, arithmetic and copies ran while one was open for 0% -> 0% of each run, Pallas kernels for 0% -> 0%
where the time goes in v4:
time: 35.6 us; the launch traced here: 35.4 us
  starting transfers between devices  20.2 us (57%)
  Pallas kernels  8.81 us (25%)
  waiting for transfers between devices  4.42 us (12%)
  between operations  1.97 us (6%)
    ppermute x4, starting transfers between devices, swapped(): return lax.ppermute(array, axis, pairs + [(j, i) for i, j in pairs])  20.2 us
    pallas_call x1, Pallas kernels, body(): pl.pallas_call(cycle_kernel, out_shape=(f32(*flat),) * 2, in_specs=[VMEM]...  6.9 us
    ppermute x4, waiting for transfers between devices, swapped(): return lax.ppermute(array, axis, pairs + [(j, i) for i, j in pairs])  4.42 us
    pallas_call x1, Pallas kernels, body(): pl.pallas_call(strips_kernel, out_shape=(f32(STRIP, CZ, LANES), f32(STRIP...  1.21 us
  transfers between devices with their start and end apart: 4, of which 4 were waited for; matrix products, arithmetic and copies ran while one was open for 0% of the time, Pallas kernels for 0%

profile of v4, /device:TPU:57, one launch (start us, length us, event | category | flops | bytes accessed | tf_op | source)
XLA Modules:
  0.0 35.4 jit_solution(12977958981000684951)
XLA Ops:
  0.6 1.2 %strips.1 = (f32[37,8,128]{2,1,0:T(8,128)S(1)}, f32[37,8,128]{2,1,0:T(8,128)S(1)}, f32[3,32,8,128]{3,2,1,0:T(8,128)S(1)}) custom-call(f32[256,128]{1,0:T(8,128)} %bitcast.5, s32[256,128]{1,0:T(8,128)} %bitcast.6, f32[256,128]{1,0:T(8,128)} %bitcast.7), custom_call_target="tpu_custom_call" | custom-call | tf_op jit(solution)/shard_map/strips/pallas_call | solution.py:400
  1.8 11.5 %collective-permute-start = (f32[37,8,128]{2,1,0:T(8,128)S(1)}, f32[37,8,128]{2,1,0:T(8,128)S(1)}, u32[]{:S(2)}, u32[]{:S(2)}) collective-permute-start(f32[37,8,128]{2,1,0:T(8,128)S(1)} %get-tuple-element.12), channel_id=1, source_target_pairs={{8,16},{24,32},{40,48},{56,64},{72,80},{88,96},{104,112},{120,128}... | collective-permute-start | bytes 454664 | tf_op jit(solution)/shard_map/ppermute | solution.py:382
  13.3 1.9 %collective-permute-start.1 = (f32[37,8,128]{2,1,0:T(8,128)S(1)}, f32[37,8,128]{2,1,0:T(8,128)S(1)}, u32[]{:S(2)}, u32[]{:S(2)}) collective-permute-start(f32[37,8,128]{2,1,0:T(8,128)S(1)} %get-tuple-element.13), channel_id=1, source_target_pairs={{0,8},{16,24},{32,40},{48,56},{64,72},{80,88},{96,104},{112,120},{... | collective-permute-start | bytes 454664 | tf_op jit(solution)/shard_map/ppermute | solution.py:382
  16.5 0.4 %collective-permute-done.far_ref = f32[37,8,128]{2,1,0:T(8,128)S(1)} collective-permute-done((f32[37,8,128]{2,1,0:T(8,128)S(1)}, f32[37,8,128]{2,1,0:T(8,128)S(1)}, u32[]{:S(2)}, u32[]{:S(2)}) %collective-permute-start) | collective-permute-done | bytes 151584 | tf_op jit(solution)/shard_map/ppermute | solution.py:382
  17.0 2.7 %collective-permute-done.1.near_ref = f32[37,8,128]{2,1,0:T(8,128)S(1)} collective-permute-done((f32[37,8,128]{2,1,0:T(8,128)S(1)}, f32[37,8,128]{2,1,0:T(8,128)S(1)}, u32[]{:S(2)}, u32[]{:S(2)}) %collective-permute-start.1) | collective-permute-done | bytes 151584 | tf_op jit(solution)/shard_map/ppermute | solution.py:382
  19.7 0.7 %sides.1 = (f32[3,60,8,128]{3,2,1,0:T(8,128)S(1)}, f32[24,8,128]{2,1,0:T(8,128)S(1)}, f32[24,8,128]{2,1,0:T(8,128)S(1)}, f32[2,8,128]{2,1,0:T(8,128)S(1)}) custom-call(f32[1]{0:T(128)S(6)} %copy.7.low_ref, f32[1]{0:T(128)S(6)} %copy.8.high_ref, f32[3,32,8,128]{3,2,1,0:T(8,128)S(1)} %get-tuple-element.11.own_ref, ...), custom_call_target="tpu_custom_call" | custom-call | tf_op jit(solution)/shard_map/sides/pallas_call | solution.py:417
  20.4 4.9 %collective-permute-start.2 = (f32[24,8,128]{2,1,0:T(8,128)S(1)}, f32[24,8,128]{2,1,0:T(8,128)S(1)}, u32[]{:S(2)}, u32[]{:S(2)}) collective-permute-start(f32[24,8,128]{2,1,0:T(8,128)S(1)} %get-tuple-element.16), channel_id=1, source_target_pairs={{1,2},{3,4},{5,6},{2,1},{4,3},{6,5},{9,10},{11,12},{13,14},{10,9},... | collective-permute-start | bytes 294920 | tf_op jit(solution)/shard_map/ppermute | solution.py:382
  25.3 1.9 %collective-permute-start.3 = (f32[24,8,128]{2,1,0:T(8,128)S(1)}, f32[24,8,128]{2,1,0:T(8,128)S(1)}, u32[]{:S(2)}, u32[]{:S(2)}) collective-permute-start(f32[24,8,128]{2,1,0:T(8,128)S(1)} %get-tuple-element.17), channel_id=1, source_target_pairs={{0,1},{2,3},{4,5},{6,7},{1,0},{3,2},{5,4},{7,6},{8,9},{10,11},{12,... | collective-permute-start | bytes 294920 | tf_op jit(solution)/shard_map/ppermute | solution.py:382
  27.2 0.4 %collective-permute-done.2.far_ref = f32[24,8,128]{2,1,0:T(8,128)S(1)} collective-permute-done((f32[24,8,128]{2,1,0:T(8,128)S(1)}, f32[24,8,128]{2,1,0:T(8,128)S(1)}, u32[]{:S(2)}, u32[]{:S(2)}) %collective-permute-start.2) | collective-permute-done | bytes 98336 | tf_op jit(solution)/shard_map/ppermute | solution.py:382
  27.6 0.9 %collective-permute-done.3.near_ref = f32[24,8,128]{2,1,0:T(8,128)S(1)} collective-permute-done((f32[24,8,128]{2,1,0:T(8,128)S(1)}, f32[24,8,128]{2,1,0:T(8,128)S(1)}, u32[]{:S(2)}, u32[]{:S(2)}) %collective-permute-start.3) | collective-permute-done | bytes 98336 | tf_op jit(solution)/shard_map/ppermute | solution.py:382
  28.5 6.9 %cycle.1 = (f32[256,128]{1,0:T(8,128)}, f32[256,128]{1,0:T(8,128)}) custom-call(f32[2,8,128]{2,1,0:T(8,128)S(1)} %get-tuple-element.14.eig_ref, f32[3,60,8,128]{3,2,1,0:T(8,128)S(1)} %get-tuple-element.15.tall_ref, f32[24,8,128]{2,1,0:T(8,128)S(1)} %collective-permute-done.2.far_ref, f32[24,8,128]{2,1,0:T(8,128)S(1)} %collective-permute-done.3.near_ref), custom_call_target="tpu_custom_call" | custom-call | tf_op jit(solution)/shard_map/cycle/pallas_call | solution.py:433
Async XLA Ops:
  1.8 15.1 %collective-permute-start = (f32[37,8,128]{2,1,0:T(8,128)S(1)}, f32[37,8,128]{2,1,0:T(8,128)S(1)}, u32[]{:S(2)}, u32[]{:S(2)}) collective-permute-start(f32[37,8,128]{2,1,0:T(8,128)S(1)} %get-tuple-element.12), channel_id=1, source_target_pairs={{8,16},{24,32},{40,48},{56,64},{72,80},{88,96},{104,112},{120,128}... | collective-permute-start | bytes 454664 | tf_op jit(solution)/shard_map/ppermute | solution.py:382
  13.3 6.4 %collective-permute-start.1 = (f32[37,8,128]{2,1,0:T(8,128)S(1)}, f32[37,8,128]{2,1,0:T(8,128)S(1)}, u32[]{:S(2)}, u32[]{:S(2)}) collective-permute-start(f32[37,8,128]{2,1,0:T(8,128)S(1)} %get-tuple-element.13), channel_id=1, source_target_pairs={{0,8},{16,24},{32,40},{48,56},{64,72},{80,88},{96,104},{112,120},{... | collective-permute-start | bytes 454664 | tf_op jit(solution)/shard_map/ppermute | solution.py:382
  20.4 7.2 %collective-permute-start.2 = (f32[24,8,128]{2,1,0:T(8,128)S(1)}, f32[24,8,128]{2,1,0:T(8,128)S(1)}, u32[]{:S(2)}, u32[]{:S(2)}) collective-permute-start(f32[24,8,128]{2,1,0:T(8,128)S(1)} %get-tuple-element.16), channel_id=1, source_target_pairs={{1,2},{3,4},{5,6},{2,1},{4,3},{6,5},{9,10},{11,12},{13,14},{10,9},... | collective-permute-start | bytes 294920 | tf_op jit(solution)/shard_map/ppermute | solution.py:382
  25.3 3.2 %collective-permute-start.3 = (f32[24,8,128]{2,1,0:T(8,128)S(1)}, f32[24,8,128]{2,1,0:T(8,128)S(1)}, u32[]{:S(2)}, u32[]{:S(2)}) collective-permute-start(f32[24,8,128]{2,1,0:T(8,128)S(1)} %get-tuple-element.17), channel_id=1, source_target_pairs={{0,1},{2,3},{4,5},{6,7},{1,0},{3,2},{5,4},{7,6},{8,9},{10,11},{12,... | collective-permute-start | bytes 294920 | tf_op jit(solution)/shard_map/ppermute | solution.py:382

commit v5 on v4

--- a/solution.py
+++ b/solution.py
@@ -110,6 +110,10 @@
     count = (stop - start) // chunk
     assert count * chunk == stop - start
 
+    if count == 1:
+        step(start, chunk)
+        return
+
     def body(index, carry):
         step(start + index * chunk, chunk)
         return carry
@@ -127,8 +131,8 @@
     wet,
     flow,
     flow_next,
-    helm,
-    rhs,
+    helm_side,
+    rhs_side,
     diag,
     base,
     gain,
@@ -156,18 +160,17 @@
     def get(ref, tile, row, shift=0):
         return ref[tile, pl.ds(row * PITCH + (CZ + shift), CZ), :]
 
-    def clear(ref, first, last):
-        def body(row, carry):
-            for tile in tiles:
-                ref[tile, pl.ds(row * PITCH, CZ), :] = zero
-            return carry
-
-        lax.fori_loop(first, last + 1, body, 0, unroll=8)
+    def clear(ref, count, reach):
+        for place in [CZ - 1 - k for k in range(reach)] + [2 * CZ + k for k in range(reach)]:
+            for first in range(0, count, CZ):
+                first = min(first, count - CZ)
+                for tile in tiles:
+                    ref[tile, pl.ds(first * PITCH + place, CZ, stride=PITCH), :] = zero
 
     for ref in (wet, flow, flow_next):
-        clear(ref, 0, TALL)
+        clear(ref, TALL, 1)
     for ref in (wet_c, masked, masked_next):
-        clear(ref, 0, TALL // 2)
+        clear(ref, TALL // 2, 2)
 
     def beside(main, side, reach):
         low, high = lane < reach, lane >= LANES - reach
@@ -209,30 +212,33 @@
                     both = jnp.where((lane >= low) & (lane < high), after, both)
                     if k:
                         both = pltpu.roll(both, LANES - low, 1)
-                    main = tall_ref[field, row]
                     if field == 0:
-                        put(wet, 0, row, main)
+                        put(wet, 0, row, tall_ref[0, row])
                         put(wet, 1, row, both)
                     else:
-                        dest = (helm, rhs)[field - 1]
-                        dest[0, row] = main
-                        dest[1, row] = both
-
-    rows_loop(0, PACKED, 2, unpack)
+                        (helm_side, rhs_side)[field - 1][row] = both
+
+    rows_loop(0, PACKED, 4, unpack)
+
+    def helm(tile, row):
+        return helm_side[row] if tile else tall_ref[1, row]
+
+    def rhs(tile, row):
+        return rhs_side[row] if tile else tall_ref[2, row]
 
     def smooth_setup(row, chunk):
         for k, count in enumerate(near_rows(wet, row, chunk, 1)):
             for tile in tiles:
                 water = get(wet, tile, row + k)
-                scale = water * (helm[tile, row + k] + count[tile]) + (1.0 - water)
+                scale = water * (helm(tile, row + k) + count[tile]) + (1.0 - water)
                 inverse = 0.8 / scale
-                start = inverse * rhs[tile, row + k]
+                start = inverse * rhs(tile, row + k)
                 diag[tile, row + k] = scale
                 base[tile, row + k] = start
                 gain[tile, row + k] = inverse * water
                 put(flow, tile, row + k, water * start)
 
-    rows_loop(2, 58, 14, smooth_setup)
+    rows_loop(2, 58, 28, smooth_setup)
 
     def smooth_second(row, chunk):
         for k, near in enumerate(near_rows(flow, row, chunk, 1)):
@@ -241,7 +247,7 @@
                 state[tile, row + k] = value
                 put(flow_next, tile, row + k, get(wet, tile, row + k) * value)
 
-    rows_loop(3, 57, 18, smooth_second)
+    rows_loop(3, 57, 27, smooth_second)
 
     def pair_sum(value):
         value = value + jnp.where(
@@ -258,7 +264,7 @@
                 total = pair_sum(get(wet, tile, fine) + get(wet, tile, fine + 1))
                 put(wet_c, tile, row + k, jnp.where(total >= 3.5, 1.0, 0.0))
 
-    rows_loop(1, 29, 14, coarse_mask)
+    rows_loop(1, 29, 28, coarse_mask)
 
     low, high = eig_ref[0], eig_ref[1]
     centre = 0.5 * (high + low)
@@ -274,9 +280,9 @@
             for fine in (2 * (row + k), 2 * (row + k) + 1):
                 near = next(fine_near)
                 for tile in tiles:
-                    left_over = rhs[tile, fine] - diag[tile, fine] * state[tile, fine]
+                    left_over = rhs(tile, fine) - diag[tile, fine] * state[tile, fine]
                     source[tile] += get(wet, tile, fine) * (left_over + near[tile])
-                    shift[tile] += helm[tile, fine]
+                    shift[tile] += helm(tile, fine)
             for tile in tiles:
                 first_sum = 0.125 * pair_sum(source[tile])
                 water_c = get(wet_c, tile, row + k)
@@ -312,7 +318,7 @@
                     error[tile, row + k] = error[tile, row + k] + fresh
                     put(later, tile, row + k, water_c * fresh)
 
-        rows_loop(2 + sweep, 28 - sweep, 13 - sweep, chebyshev)
+        rows_loop(2 + sweep, 28 - sweep, 26 - 2 * sweep, chebyshev)
         rho = rho_next
         now, later = later, now
 
@@ -328,7 +334,7 @@
                 other = jnp.where((level == 0) | (level == CZ - 1), 0.0, other)
                 direction[tile, row + k] = 0.75 * line + 0.25 * other
 
-    rows_loop(5, 25, 10, spread)
+    rows_loop(5, 25, 20, spread)
 
     def correct(row, chunk):
         for k in range(chunk):
@@ -340,9 +346,9 @@
                     state[tile, fine] = value
                     put(flow, tile, fine, water * value)
 
-    rows_loop(5, 25, 10, correct)
-
-    def smooth(now, later):
+    rows_loop(5, 25, 20, correct)
+
+    def smooth(now, later, last=False):
         def step(row, chunk):
             for k, near in enumerate(near_rows(now, row, chunk, 1)):
                 for tile in tiles:
@@ -350,27 +356,24 @@
                     value = value + gain[tile, row + k] * near[tile]
                     state[tile, row + k] = value
                     put(later, tile, row + k, get(wet, tile, row + k) * value)
+                    if last and tile == 0 and RIM <= row + k < RIM + ROWS:
+                        pressure_ref[pl.ds(row + k - RIM, CZ, stride=ROWS), :] = value
 
         return step
 
-    rows_loop(12, 48, 12, smooth(flow, flow_next))
-    rows_loop(13, 47, 17, smooth(flow_next, flow))
-
-    def finish_pressure(row, chunk):
-        for k in range(chunk):
-            pressure_ref[pl.ds(row + k - RIM, CZ, stride=ROWS), :] = state[0, row + k]
-
-    rows_loop(RIM, RIM + ROWS, 16, finish_pressure)
+    rows_loop(12, 48, 18, smooth(flow, flow_next))
+    rows_loop(13, 47, 34, smooth(flow_next, flow, True))
+
     pressure_copy = pltpu.make_async_copy(pressure_ref, pressure_out, out_sem.at[0])
     pressure_copy.start()
 
     def finish(row, chunk):
         for k, near in enumerate(near_rows(flow, row, chunk, 1)):
-            left_over = rhs[0, row + k] - diag[0, row + k] * state[0, row + k]
+            left_over = rhs(0, row + k) - diag[0, row + k] * state[0, row + k]
             left_over = left_over + get(wet, 0, row + k) * near[0]
             residual_ref[pl.ds(row + k - RIM, CZ, stride=ROWS), :] = left_over
 
-    rows_loop(RIM, RIM + ROWS, 16, finish)
+    rows_loop(RIM, RIM + ROWS, 32, finish)
     residual_copy = pltpu.make_async_copy(residual_ref, residual_out, out_sem.at[1])
     residual_copy.start()
     pressure_copy.wait()
@@ -435,9 +438,10 @@
         out_shape=(f32(*flat),) * 2,
         in_specs=[VMEM] * 4,
         out_specs=(HBM,) * 2,
-        scratch_shapes=[pltpu.VMEM((2, TALL * PITCH + CZ, LANES), jnp.float32)] * 3
-        + [pltpu.VMEM((2, TALL, CZ, LANES), jnp.float32)] * 6
-        + [pltpu.VMEM((2, TALL // 2 * PITCH + CZ, LANES), jnp.float32)] * 3
+        scratch_shapes=[pltpu.VMEM((2, TALL * PITCH + 2 * CZ, LANES), jnp.float32)] * 3
+        + [pltpu.VMEM((TALL, CZ, LANES), jnp.float32)] * 2
+        + [pltpu.VMEM((2, TALL, CZ, LANES), jnp.float32)] * 4
+        + [pltpu.VMEM((2, TALL // 2 * PITCH + 2 * CZ, LANES), jnp.float32)] * 3
         + [pltpu.VMEM((2, TALL // 2, CZ, LANES), jnp.float32)] * 5
         + [pltpu.VMEM(flat, jnp.float32)] * 2
         + [pltpu.SemaphoreType.DMA((2,))],

time: 35.6 us -> 34 us (0.955)
  Pallas kernels: 8.81 us -> 7.25 us
    pallas_call x1, Pallas kernels: 6.9 us -> 5.34 us  [body(): pl.pallas_call(cycle_kernel, out_shape=(f32(*flat),) * 2, in_specs=[VMEM]...]
where the time goes in v5:
time: 34 us; the launch traced here: 33.8 us
  starting transfers between devices  20.2 us (59%)
  Pallas kernels  7.25 us (21%)
  waiting for transfers between devices  4.42 us (13%)
  between operations  1.97 us (6%)
    ppermute x4, starting transfers between devices, swapped(): return lax.ppermute(array, axis, pairs + [(j, i) for i, j in pairs])  20.2 us
    pallas_call x1, Pallas kernels, body(): pl.pallas_call(cycle_kernel, out_shape=(f32(*flat),) * 2, in_specs=[VMEM]...  5.34 us
    ppermute x4, waiting for transfers between devices, swapped(): return lax.ppermute(array, axis, pairs + [(j, i) for i, j in pairs])  4.42 us
    pallas_call x1, Pallas kernels, body(): pl.pallas_call(strips_kernel, out_shape=(f32(STRIP, CZ, LANES), f32(STRIP...  1.21 us
    pallas_call x1, Pallas kernels, body(): pl.pallas_call(sides_kernel, out_shape=(f32(3, TALL, CZ, LANES), f32(3 *...  0.7 us
  transfers between devices with their start and end apart: 4, of which 4 were waited for; matrix products, arithmetic and copies ran while one was open for 0% of the time, Pallas kernels for 0%

profile of v5, /device:TPU:57, one launch (start us, length us, event | category | flops | bytes accessed | tf_op | source)
XLA Modules:
  0.0 33.8 jit_solution(1407130329384199827)
XLA Ops:
  0.6 1.2 %strips.1 = (f32[37,8,128]{2,1,0:T(8,128)S(1)}, f32[37,8,128]{2,1,0:T(8,128)S(1)}, f32[3,32,8,128]{3,2,1,0:T(8,128)S(1)}) custom-call(f32[256,128]{1,0:T(8,128)} %bitcast.5, s32[256,128]{1,0:T(8,128)} %bitcast.6, f32[256,128]{1,0:T(8,128)} %bitcast.7), custom_call_target="tpu_custom_call" | custom-call | tf_op jit(solution)/shard_map/strips/pallas_call | solution.py:403
  1.8 11.5 %collective-permute-start = (f32[37,8,128]{2,1,0:T(8,128)S(1)}, f32[37,8,128]{2,1,0:T(8,128)S(1)}, u32[]{:S(2)}, u32[]{:S(2)}) collective-permute-start(f32[37,8,128]{2,1,0:T(8,128)S(1)} %get-tuple-element.12), channel_id=1, source_target_pairs={{8,16},{24,32},{40,48},{56,64},{72,80},{88,96},{104,112},{120,128}... | collective-permute-start | bytes 454664 | tf_op jit(solution)/shard_map/ppermute | solution.py:385
  13.3 1.9 %collective-permute-start.1 = (f32[37,8,128]{2,1,0:T(8,128)S(1)}, f32[37,8,128]{2,1,0:T(8,128)S(1)}, u32[]{:S(2)}, u32[]{:S(2)}) collective-permute-start(f32[37,8,128]{2,1,0:T(8,128)S(1)} %get-tuple-element.13), channel_id=1, source_target_pairs={{0,8},{16,24},{32,40},{48,56},{64,72},{80,88},{96,104},{112,120},{... | collective-permute-start | bytes 454664 | tf_op jit(solution)/shard_map/ppermute | solution.py:385
  16.5 0.4 %collective-permute-done.far_ref = f32[37,8,128]{2,1,0:T(8,128)S(1)} collective-permute-done((f32[37,8,128]{2,1,0:T(8,128)S(1)}, f32[37,8,128]{2,1,0:T(8,128)S(1)}, u32[]{:S(2)}, u32[]{:S(2)}) %collective-permute-start) | collective-permute-done | bytes 151584 | tf_op jit(solution)/shard_map/ppermute | solution.py:385
  17.0 2.7 %collective-permute-done.1.near_ref = f32[37,8,128]{2,1,0:T(8,128)S(1)} collective-permute-done((f32[37,8,128]{2,1,0:T(8,128)S(1)}, f32[37,8,128]{2,1,0:T(8,128)S(1)}, u32[]{:S(2)}, u32[]{:S(2)}) %collective-permute-start.1) | collective-permute-done | bytes 151584 | tf_op jit(solution)/shard_map/ppermute | solution.py:385
  19.7 0.7 %sides.1 = (f32[3,60,8,128]{3,2,1,0:T(8,128)S(1)}, f32[24,8,128]{2,1,0:T(8,128)S(1)}, f32[24,8,128]{2,1,0:T(8,128)S(1)}, f32[2,8,128]{2,1,0:T(8,128)S(1)}) custom-call(f32[1]{0:T(128)S(6)} %copy.7.low_ref, f32[1]{0:T(128)S(6)} %copy.8.high_ref, f32[3,32,8,128]{3,2,1,0:T(8,128)S(1)} %get-tuple-element.11.own_ref, ...), custom_call_target="tpu_custom_call" | custom-call | tf_op jit(solution)/shard_map/sides/pallas_call | solution.py:420
  20.4 4.9 %collective-permute-start.2 = (f32[24,8,128]{2,1,0:T(8,128)S(1)}, f32[24,8,128]{2,1,0:T(8,128)S(1)}, u32[]{:S(2)}, u32[]{:S(2)}) collective-permute-start(f32[24,8,128]{2,1,0:T(8,128)S(1)} %get-tuple-element.16), channel_id=1, source_target_pairs={{1,2},{3,4},{5,6},{2,1},{4,3},{6,5},{9,10},{11,12},{13,14},{10,9},... | collective-permute-start | bytes 294920 | tf_op jit(solution)/shard_map/ppermute | solution.py:385
  25.3 1.9 %collective-permute-start.3 = (f32[24,8,128]{2,1,0:T(8,128)S(1)}, f32[24,8,128]{2,1,0:T(8,128)S(1)}, u32[]{:S(2)}, u32[]{:S(2)}) collective-permute-start(f32[24,8,128]{2,1,0:T(8,128)S(1)} %get-tuple-element.17), channel_id=1, source_target_pairs={{0,1},{2,3},{4,5},{6,7},{1,0},{3,2},{5,4},{7,6},{8,9},{10,11},{12,... | collective-permute-start | bytes 294920 | tf_op jit(solution)/shard_map/ppermute | solution.py:385
  27.2 0.4 %collective-permute-done.2.far_ref = f32[24,8,128]{2,1,0:T(8,128)S(1)} collective-permute-done((f32[24,8,128]{2,1,0:T(8,128)S(1)}, f32[24,8,128]{2,1,0:T(8,128)S(1)}, u32[]{:S(2)}, u32[]{:S(2)}) %collective-permute-start.2) | collective-permute-done | bytes 98336 | tf_op jit(solution)/shard_map/ppermute | solution.py:385
  27.6 0.9 %collective-permute-done.3.near_ref = f32[24,8,128]{2,1,0:T(8,128)S(1)} collective-permute-done((f32[24,8,128]{2,1,0:T(8,128)S(1)}, f32[24,8,128]{2,1,0:T(8,128)S(1)}, u32[]{:S(2)}, u32[]{:S(2)}) %collective-permute-start.3) | collective-permute-done | bytes 98336 | tf_op jit(solution)/shard_map/ppermute | solution.py:385
  28.5 5.3 %cycle.1 = (f32[256,128]{1,0:T(8,128)}, f32[256,128]{1,0:T(8,128)}) custom-call(f32[2,8,128]{2,1,0:T(8,128)S(1)} %get-tuple-element.14.eig_ref, f32[3,60,8,128]{3,2,1,0:T(8,128)S(1)} %get-tuple-element.15.tall_ref, f32[24,8,128]{2,1,0:T(8,128)S(1)} %collective-permute-done.2.far_ref, f32[24,8,128]{2,1,0:T(8,128)S(1)} %collective-permute-done.3.near_ref), custom_call_target="tpu_custom_call" | custom-call | tf_op jit(solution)/shard_map/cycle/pallas_call | solution.py:436
Async XLA Ops:
  1.8 15.1 %collective-permute-start = (f32[37,8,128]{2,1,0:T(8,128)S(1)}, f32[37,8,128]{2,1,0:T(8,128)S(1)}, u32[]{:S(2)}, u32[]{:S(2)}) collective-permute-start(f32[37,8,128]{2,1,0:T(8,128)S(1)} %get-tuple-element.12), channel_id=1, source_target_pairs={{8,16},{24,32},{40,48},{56,64},{72,80},{88,96},{104,112},{120,128}... | collective-permute-start | bytes 454664 | tf_op jit(solution)/shard_map/ppermute | solution.py:385
  13.3 6.4 %collective-permute-start.1 = (f32[37,8,128]{2,1,0:T(8,128)S(1)}, f32[37,8,128]{2,1,0:T(8,128)S(1)}, u32[]{:S(2)}, u32[]{:S(2)}) collective-permute-start(f32[37,8,128]{2,1,0:T(8,128)S(1)} %get-tuple-element.13), channel_id=1, source_target_pairs={{0,8},{16,24},{32,40},{48,56},{64,72},{80,88},{96,104},{112,120},{... | collective-permute-start | bytes 454664 | tf_op jit(solution)/shard_map/ppermute | solution.py:385
  20.4 7.2 %collective-permute-start.2 = (f32[24,8,128]{2,1,0:T(8,128)S(1)}, f32[24,8,128]{2,1,0:T(8,128)S(1)}, u32[]{:S(2)}, u32[]{:S(2)}) collective-permute-start(f32[24,8,128]{2,1,0:T(8,128)S(1)} %get-tuple-element.16), channel_id=1, source_target_pairs={{1,2},{3,4},{5,6},{2,1},{4,3},{6,5},{9,10},{11,12},{13,14},{10,9},... | collective-permute-start | bytes 294920 | tf_op jit(solution)/shard_map/ppermute | solution.py:385
  25.3 3.2 %collective-permute-start.3 = (f32[24,8,128]{2,1,0:T(8,128)S(1)}, f32[24,8,128]{2,1,0:T(8,128)S(1)}, u32[]{:S(2)}, u32[]{:S(2)}) collective-permute-start(f32[24,8,128]{2,1,0:T(8,128)S(1)} %get-tuple-element.17), channel_id=1, source_target_pairs={{0,1},{2,3},{4,5},{6,7},{1,0},{3,2},{5,4},{7,6},{8,9},{10,11},{12,... | collective-permute-start | bytes 294920 | tf_op jit(solution)/shard_map/ppermute | solution.py:385

commit v6 on v4

v6 whole, which is shorter than its diff:
```python
import functools

import jax
import jax.numpy as jnp
from jax import lax
from jax.experimental import pallas as pl
from jax.experimental.pallas import tpu as pltpu
from jax.sharding import PartitionSpec as P

CHEB = 4

CZ = 8
ROWS = 32
LANES = 128
RIM = 14
TALL = ROWS + 2 * RIM + 4
MASK_RIM = 13
RIGHT_RIM = 12
STRIP = MASK_RIM + 2 * RIGHT_RIM
SIDE = 16
SPAN = 2 * SIDE
BLOCK = TALL * SPAN // LANES
PACKED = BLOCK // 2
PITCH = 2 * CZ

VMEM = pl.BlockSpec(memory_space=pltpu.VMEM)
SMEM = pl.BlockSpec(memory_space=pltpu.SMEM)
HBM = pl.BlockSpec(memory_space=pltpu.HBM)


def brick_row(ref, row):
    return ref[pl.ds(row, CZ, stride=ROWS), :]


def strips_kernel(
    right_hbm, mask_hbm, helm_hbm, far_ref, near_ref, own_ref, mask_ref, helm_ref, right_ref, sem
):
    odd = lax.rem(lax.axis_index("wide"), 2)
    copies = [
        pltpu.make_async_copy(source, dest, sem.at[k])
        for k, (source, dest) in enumerate(
            ((mask_hbm, mask_ref), (helm_hbm, helm_ref), (right_hbm, right_ref))
        )
    ]
    for copy in copies:
        copy.start()
    for field, (ref, rim, offset) in enumerate(
        (
            (mask_ref, MASK_RIM, 0),
            (helm_ref, RIGHT_RIM, MASK_RIM),
            (right_ref, RIGHT_RIM, MASK_RIM + RIGHT_RIM),
        )
    ):
        copies[field].wait()
        for row in range(ROWS):
            line = brick_row(ref, row).astype(jnp.float32)
            own_ref[field, row] = line
        to_far, to_near = (ROWS - rim) * odd, (ROWS - rim) * (1 - odd)
        for row in range(rim):
            far_ref[offset + row] = own_ref[field, to_far + row]
            near_ref[offset + row] = own_ref[field, to_near + row]


def sides_kernel(
    low_ref, high_ref, own_ref, far_ref, near_ref, tall_ref, far_out, near_out, eig_ref
):
    odd = lax.rem(lax.axis_index("wide"), 2)
    odd_column = lax.rem(lax.axis_index("narrow"), 2) == 1
    eig_ref[0] = jnp.full((CZ, LANES), low_ref[0], jnp.float32)
    eig_ref[1] = jnp.full((CZ, LANES), high_ref[0], jnp.float32)
    zero = jnp.zeros((CZ, LANES), jnp.float32)
    lane = lax.broadcasted_iota(jnp.int32, (CZ, LANES), 1)
    for field, offset, rim in (
        (0, 0, MASK_RIM),
        (1, MASK_RIM, RIGHT_RIM),
        (2, MASK_RIM + RIGHT_RIM, RIGHT_RIM),
    ):
        for row in (0, 1) + tuple(range(TALL - 6, TALL)):
            tall_ref[field, row] = zero
        from_far = RIM - rim + (ROWS + rim) * odd
        from_near = RIM - rim + (ROWS + rim) * (1 - odd)
        for row in range(rim):
            tall_ref[field, from_far + row] = far_ref[offset + row]
            tall_ref[field, from_near + row] = near_ref[offset + row]
        for row in range(ROWS):
            tall_ref[field, RIM + row] = own_ref[field, row]

    block, half = lane // SPAN, lane % SPAN < SIDE
    for field in range(3):
        for i in range(BLOCK // 2):
            first, last = zero, zero
            for b in range(LANES // SPAN):
                low = tall_ref[field, BLOCK * b + i]
                low = pltpu.roll(low, SPAN * b + SIDE, 1)
                high = tall_ref[field, BLOCK * b + i + BLOCK // 2]
                high = pltpu.roll(high, SPAN * (b + 1), 1) if SPAN * (b + 1) < LANES else high
                here, after = block == b, block == (b + 1) % (LANES // SPAN)
                last = jnp.where(here, jnp.where(half, low, high), last)
                first = jnp.where(here & ~half, low, jnp.where(after & half, high, first))
            place = field * PACKED + i
            far_out[place] = jnp.where(odd_column, last, first)
            near_out[place] = jnp.where(odd_column, first, last)


class Field:
    def __init__(self, main, side, height):
        self.refs, self.height = (main, side), height

    def get(self, kind, row, shift=0):
        return self.refs[kind][row]

    def put(self, kind, row, value):
        self.refs[kind][row] = value

    def line(self, kind, row):
        if kind and row < 0:
            return pltpu.roll(self.get(1, self.height - 1), SPAN, 1)
        if kind and row == self.height:
            return pltpu.roll(self.get(1, 0), LANES - SPAN, 1)
        return self.get(kind, row)


class Padded(Field):
    def get(self, kind, row, shift=0):
        return self.refs[kind][pl.ds(row * PITCH + CZ + shift, CZ), :]

    def put(self, kind, row, value):
        self.refs[kind][pl.ds(row * PITCH + CZ, CZ), :] = value

    def clear(self, reach):
        zero = jnp.zeros((CZ, LANES), jnp.float32)
        for ref, count in zip(self.refs, (self.height * (LANES // SPAN), self.height)):
            for place in [CZ - 1 - k for k in range(reach)] + [2 * CZ + k for k in range(reach)]:
                for first in range(0, count, CZ):
                    ref[pl.ds(first * PITCH + place, CZ, stride=PITCH), :] = zero


def cycle_kernel(eig_ref, tall_ref, far_ref, near_ref, pressure_out, residual_out, *scratch):
    scratch = list(scratch)
    out_sem = scratch.pop()
    residual_ref, pressure_ref = scratch.pop(), scratch.pop()

    def fields(kind, height, count):
        return [kind(scratch.pop(0), scratch.pop(0), height) for _ in range(count)]

    wet, flow, flow_next = fields(Padded, BLOCK, 3)
    diag, base, gain, state = fields(Field, BLOCK, 4)
    wet_c, masked, masked_next = fields(Padded, BLOCK // 2, 3)
    diag_c, inverse_c, remain, error, spread = fields(Field, BLOCK // 2, 5)
    helm = Field(tall_ref.at[1], scratch.pop(0), BLOCK)
    rhs = Field(tall_ref.at[2], scratch.pop(0), BLOCK)

    lane = lax.broadcasted_iota(jnp.int32, (CZ, LANES), 1)
    level = lax.broadcasted_iota(jnp.int32, (CZ, LANES), 0)
    place = lane % SPAN
    blocks = [lane // SPAN == b for b in range(LANES // SPAN)]

    wet.clear(1)
    flow.clear(1)
    flow_next.clear(1)
    wet_c.clear(2)
    masked.clear(2)
    masked_next.clear(2)

    odd_column = lax.rem(lax.axis_index("narrow"), 2) == 1
    for row in range(1, TALL - 5):
        wet.put(0, row, tall_ref[0, row])
    for index, field in enumerate((wet, helm, rhs)):
        for i in range(BLOCK // 2):
            far, near = far_ref[index * PACKED + i], near_ref[index * PACKED + i]
            right = jnp.where(odd_column, far, near)
            left = jnp.where(odd_column, near, far)
            field.put(1, i, jnp.where(place < SIDE, left, right))
            late = jnp.where(place < SIDE, right, left)
            field.put(1, i + BLOCK // 2, pltpu.roll(late, LANES - SIDE, 1))

    def cells(start, stop, height):
        for i in range(height):
            rows = [(b, height * b + i) for b in range(LANES // SPAN)]
            yield i, [(b, row) for b, row in rows if start <= row < stop]

    def beside(mains, side, reach):
        edge = side
        found = []
        for b, main in mains:
            inner = pltpu.roll(side, (LANES - SIDE - SPAN * b) % LANES, 1)
            before = jnp.where(lane >= LANES - reach, inner, main)
            after = jnp.where(lane < reach, inner, main)
            found.append((pltpu.roll(before, reach, 1), pltpu.roll(after, LANES - reach, 1)))
            edge = jnp.where(blocks[b], pltpu.roll(main, SIDE + SPAN * b, 1), edge)
        before = jnp.where((place < SIDE) & (place >= SIDE - reach), edge, side)
        after = jnp.where((place >= SIDE) & (place < SIDE + reach), edge, side)
        found.append((pltpu.roll(before, reach, 1), pltpu.roll(after, LANES - reach, 1)))
        return found

    def near_rows(field, start, stop, reach):
        for i, rows in cells(start, stop, field.height):
            side = field.get(1, i)
            sides = beside([(b, field.get(0, row)) for b, row in rows], side, reach)
            out = []
            for (kind, row), (before, after) in zip([(0, r) for _, r in rows] + [(1, i)], sides):
                total = field.line(kind, row - 1) + field.line(kind, row + 1)
                total = total + (field.get(kind, row, -reach) + field.get(kind, row, reach))
                out.append((kind, row, total + (before + after)))
            yield out

    def flat_rows(start, stop, height):
        for i, rows in cells(start, stop, height):
            yield from [(0, row) for _, row in rows] + [(1, i)]

    for group in near_rows(wet, 2, 58, 1):
        for kind, row, count in group:
            water = wet.get(kind, row)
            scale = water * (helm.get(kind, row) + count) + (1.0 - water)
            inverse = 0.8 / scale
            start = inverse * rhs.get(kind, row)
            diag.put(kind, row, scale)
            base.put(kind, row, start)
            gain.put(kind, row, inverse * water)
            flow.put(kind, row, water * start)

    for group in near_rows(flow, 3, 57, 1):
        for kind, row, near in group:
            value = 1.2 * base.get(kind, row) + gain.get(kind, row) * near
            state.put(kind, row, value)
            flow_next.put(kind, row, wet.get(kind, row) * value)

    def pair_sum(value):
        value = value + jnp.where(
            level % 2 == 0, pltpu.roll(value, CZ - 1, 0), pltpu.roll(value, 1, 0)
        )
        return value + jnp.where(
            lane % 2 == 0, pltpu.roll(value, LANES - 1, 1), pltpu.roll(value, 1, 1)
        )

    for kind, row in flat_rows(1, 29, BLOCK // 2):
        total = pair_sum(wet.get(kind, 2 * row) + wet.get(kind, 2 * row + 1))
        wet_c.put(kind, row, jnp.where(total >= 3.5, 1.0, 0.0))

    low, high = eig_ref[0], eig_ref[1]
    centre = 0.5 * (high + low)
    half = 0.5 * (high - low)
    sigma = centre / half
    rho = 1.0 / sigma
    start_scale = 1.0 / centre

    fine_near = near_rows(flow_next, 4, 56, 1)
    for group in near_rows(wet_c, 2, 28, 2):
        parts = {}
        for _ in range(2):
            for kind, row, near in next(fine_near):
                left_over = rhs.get(kind, row) - diag.get(kind, row) * state.get(kind, row)
                left_over = wet.get(kind, row) * (left_over + near)
                lump = helm.get(kind, row)
                if (kind, row // 2) in parts:
                    left_over = left_over + parts[kind, row // 2][0]
                    lump = lump + parts[kind, row // 2][1]
                parts[kind, row // 2] = (left_over, lump)
        for kind, row, count_c in group:
            source, shift = (0.125 * pair_sum(part) for part in parts[kind, row])
            water_c = wet_c.get(kind, row)
            scale = water_c * (shift + 0.25 * count_c) + (1.0 - water_c)
            inverse = 1.0 / scale
            first = source * inverse * start_scale
            diag_c.put(kind, row, scale)
            inverse_c.put(kind, row, inverse)
            remain.put(kind, row, source)
            error.put(kind, row, first)
            spread.put(kind, row, first)
            masked.put(kind, row, water_c * first)

    direction, now, later = spread, masked, masked_next
    for sweep in range(1, CHEB):
        rho_next = 1.0 / (2.0 * sigma - rho)
        keep = rho_next * rho
        add = 2.0 * rho_next / half
        for group in near_rows(now, 2 + sweep, 28 - sweep, 2):
            for kind, row, near in group:
                old = direction.get(kind, row)
                water_c = wet_c.get(kind, row)
                image = diag_c.get(kind, row) * old - 0.25 * water_c * near
                left_over = remain.get(kind, row) - image
                fresh = keep * old + add * (left_over * inverse_c.get(kind, row))
                error.put(kind, row, error.get(kind, row) + fresh)
                if sweep + 1 < CHEB:
                    remain.put(kind, row, left_over)
                    direction.put(kind, row, fresh)
                    later.put(kind, row, water_c * fresh)
        rho = rho_next
        now, later = later, now

    for i, rows in cells(5, 25, BLOCK // 2):
        values = [error.get(0, row) for _, row in rows] + [error.get(1, i)]
        sides = beside([(b, error.get(0, row)) for b, row in rows], values[-1], 1)
        for k, (kind, row) in enumerate([(0, row) for _, row in rows] + [(1, i)]):
            line = 0.75 * values[k] + 0.25 * jnp.where(lane % 2 == 0, *sides[k])
            other = jnp.where(level % 2 == 0, pltpu.roll(line, 1, 0), pltpu.roll(line, CZ - 1, 0))
            other = jnp.where((level == 0) | (level == CZ - 1), 0.0, other)
            spread.put(kind, row, 0.75 * line + 0.25 * other)

    for kind, row in flat_rows(5, 25, BLOCK // 2):
        here = 0.75 * spread.get(kind, row)
        for fine, beyond in ((2 * row, row - 1), (2 * row + 1, row + 1)):
            if kind == 0 and not 11 <= fine < 49:
                continue
            water = wet.get(kind, fine)
            value = state.get(kind, fine) + water * (here + 0.25 * spread.line(kind, beyond))
            state.put(kind, fine, value)
            flow.put(kind, fine, water * value)

    for start, stop, now, later in ((12, 48, flow, flow_next), (13, 47, flow_next, flow)):
        for group in near_rows(now, start, stop, 1):
            for kind, row, near in group:
                value = 0.2 * state.get(kind, row) + base.get(kind, row)
                value = value + gain.get(kind, row) * near
                state.put(kind, row, value)
                later.put(kind, row, wet.get(kind, row) * value)
                if later is flow and kind == 0 and RIM <= row < RIM + ROWS:
                    pressure_ref[pl.ds(row - RIM, CZ, stride=ROWS), :] = value

    pressure_copy = pltpu.make_async_copy(pressure_ref, pressure_out, out_sem.at[0])
    pressure_copy.start()
    for group in near_rows(flow, RIM, RIM + ROWS, 1):
        for kind, row, near in group[:-1]:
            left_over = rhs.get(0, row) - diag.get(0, row) * state.get(0, row)
            left_over = left_over + wet.get(0, row) * near
            residual_ref[pl.ds(row - RIM, CZ, stride=ROWS), :] = left_over
    residual_copy = pltpu.make_async_copy(residual_ref, residual_out, out_sem.at[1])
    residual_copy.start()
    pressure_copy.wait()
    residual_copy.wait()


def swapped(array, axis, first):
    pairs = [(i, i + 1) for i in range(first, lax.axis_size(axis) - 1, 2)]
    return lax.ppermute(array, axis, pairs + [(j, i) for i, j in pairs])


def in_hbm(array):
    return pltpu.with_memory_space_constraint(array, pltpu.HBM)


def f32(*shape):
    return jax.ShapeDtypeStruct(shape, jnp.float32)


def body(right_side, wet_mask, helmholtz, eig_low, eig_high):
    flat = (CZ * ROWS, LANES)
    right_flat = right_side.reshape(flat)
    mask_flat = wet_mask.reshape(flat)
    helm_flat = helmholtz.reshape(flat)
    limits = pltpu.CompilerParams(vmem_limit_bytes=24 * 1024 * 1024)

    far, near, own = pl.pallas_call(
        strips_kernel,
        out_shape=(f32(STRIP, CZ, LANES), f32(STRIP, CZ, LANES), f32(3, ROWS, CZ, LANES)),
        in_specs=[HBM] * 3,
        out_specs=(VMEM,) * 3,
        scratch_shapes=[
            pltpu.VMEM(flat, jnp.int32),
            pltpu.VMEM(flat, jnp.float32),
            pltpu.VMEM(flat, jnp.float32),
            pltpu.SemaphoreType.DMA((3,)),
        ],
        compiler_params=limits,
        name="strips",
    )(in_hbm(right_flat), in_hbm(mask_flat), in_hbm(helm_flat))
    far = swapped(far, "wide", 1)
    near = swapped(near, "wide", 0)

    tall, far, near, eigs = pl.pallas_call(
        sides_kernel,
        out_shape=(
            f32(3, TALL, CZ, LANES),
            f32(3 * PACKED, CZ, LANES),
            f32(3 * PACKED, CZ, LANES),
            f32(2, CZ, LANES),
        ),
        in_specs=[SMEM] * 2 + [VMEM] * 3,
        out_specs=(VMEM,) * 4,
        compiler_params=limits,
        name="sides",
    )(eig_low, eig_high, own, far, near)
    far = swapped(far, "narrow", 1)
    near = swapped(near, "narrow", 0)

    padded = [((rows + 1) * PITCH, LANES) for rows in (TALL, BLOCK)]
    plain = [(rows, CZ, LANES) for rows in (TALL, BLOCK)]
    padded_c = [((rows // 2 + 1) * PITCH, LANES) for rows in (TALL, BLOCK)]
    plain_c = [(rows // 2, CZ, LANES) for rows in (TALL, BLOCK)]
    shapes = padded * 3 + plain * 4 + padded_c * 3 + plain_c * 5 + [plain[1]] * 2 + [flat] * 2
    pressure, residual = pl.pallas_call(
        cycle_kernel,
        out_shape=(f32(*flat),) * 2,
        in_specs=[VMEM] * 4,
        out_specs=(HBM,) * 2,
        scratch_shapes=[pltpu.VMEM(shape, jnp.float32) for shape in shapes]
        + [pltpu.SemaphoreType.DMA((2,))],
        compiler_params=limits,
        name="cycle",
    )(eigs, tall, far, near)
    shape = (CZ, ROWS, LANES)
    return pressure.reshape(shape), residual.reshape(shape)


def solution(mesh):
    field = P(None, "wide", "narrow")
    return jax.shard_map(
        body,
        mesh=mesh,
        in_specs=(field, field, field, P(), P()),
        out_specs=(field, field),
        check_vma=False,
    )
```

time: 35.6 us -> 61.1 us (1.72)
  Pallas kernels: 8.81 us -> 34.3 us
    pallas_call x1, Pallas kernels: 6.9 us -> 32.8 us  [body(): pl.pallas_call(cycle_kernel, out_shape=(f32(*flat),) * 2, in_specs=[VMEM]...]
where the time goes in v6:
time: 61.1 us; the launch traced here: 60.9 us
  Pallas kernels  34.3 us (56%)
  starting transfers between devices  20.2 us (33%)
  waiting for transfers between devices  4.42 us (7%)
  between operations  1.97 us (3%)
    pallas_call x1, Pallas kernels, body(): pl.pallas_call(cycle_kernel, out_shape=(f32(*flat),) * 2, in_specs=[VMEM]...  32.8 us
    ppermute x4, starting transfers between devices, swapped(): return lax.ppermute(array, axis, pairs + [(j, i) for i, j in pairs])  20.2 us
    ppermute x4, waiting for transfers between devices, swapped(): return lax.ppermute(array, axis, pairs + [(j, i) for i, j in pairs])  4.42 us
  transfers between devices with their start and end apart: 4, of which 4 were waited for; matrix products, arithmetic and copies ran while one was open for 0% of the time, Pallas kernels for 0%

profile of v6, /device:TPU:57, one launch (start us, length us, event | category | flops | bytes accessed | tf_op | source)
XLA Modules:
  0.0 60.9 jit_solution(2679900033948870624)
XLA Ops:
  0.6 1.2 %strips.1 = (f32[37,8,128]{2,1,0:T(8,128)S(1)}, f32[37,8,128]{2,1,0:T(8,128)S(1)}, f32[3,32,8,128]{3,2,1,0:T(8,128)S(1)}) custom-call(f32[256,128]{1,0:T(8,128)} %bitcast.5, s32[256,128]{1,0:T(8,128)} %bitcast.6, f32[256,128]{1,0:T(8,128)} %bitcast.7), custom_call_target="tpu_custom_call" | custom-call | tf_op jit(solution)/shard_map/strips/pallas_call | solution.py:354
  1.8 11.5 %collective-permute-start = (f32[37,8,128]{2,1,0:T(8,128)S(1)}, f32[37,8,128]{2,1,0:T(8,128)S(1)}, u32[]{:S(2)}, u32[]{:S(2)}) collective-permute-start(f32[37,8,128]{2,1,0:T(8,128)S(1)} %get-tuple-element.12), channel_id=1, source_target_pairs={{8,16},{24,32},{40,48},{56,64},{72,80},{88,96},{104,112},{120,128}... | collective-permute-start | bytes 454664 | tf_op jit(solution)/shard_map/ppermute | solution.py:336
  13.3 1.9 %collective-permute-start.1 = (f32[37,8,128]{2,1,0:T(8,128)S(1)}, f32[37,8,128]{2,1,0:T(8,128)S(1)}, u32[]{:S(2)}, u32[]{:S(2)}) collective-permute-start(f32[37,8,128]{2,1,0:T(8,128)S(1)} %get-tuple-element.13), channel_id=1, source_target_pairs={{0,8},{16,24},{32,40},{48,56},{64,72},{80,88},{96,104},{112,120},{... | collective-permute-start | bytes 454664 | tf_op jit(solution)/shard_map/ppermute | solution.py:336
  16.5 0.4 collective-permute-done.far_ref
  17.0 2.7 %collective-permute-done.1.near_ref = f32[37,8,128]{2,1,0:T(8,128)S(1)} collective-permute-done((f32[37,8,128]{2,1,0:T(8,128)S(1)}, f32[37,8,128]{2,1,0:T(8,128)S(1)}, u32[]{:S(2)}, u32[]{:S(2)}) %collective-permute-start.1) | collective-permute-done | bytes 151584 | tf_op jit(solution)/shard_map/ppermute | solution.py:336
  19.7 0.3 sides.1
  20.0 4.9 %collective-permute-start.2 = (f32[24,8,128]{2,1,0:T(8,128)S(1)}, f32[24,8,128]{2,1,0:T(8,128)S(1)}, u32[]{:S(2)}, u32[]{:S(2)}) collective-permute-start(f32[24,8,128]{2,1,0:T(8,128)S(1)} %get-tuple-element.16), channel_id=1, source_target_pairs={{1,2},{3,4},{5,6},{2,1},{4,3},{6,5},{9,10},{11,12},{13,14},{10,9},... | collective-permute-start | bytes 294920 | tf_op jit(solution)/shard_map/ppermute | solution.py:336
  24.9 1.9 %collective-permute-start.3 = (f32[24,8,128]{2,1,0:T(8,128)S(1)}, f32[24,8,128]{2,1,0:T(8,128)S(1)}, u32[]{:S(2)}, u32[]{:S(2)}) collective-permute-start(f32[24,8,128]{2,1,0:T(8,128)S(1)} %get-tuple-element.17), channel_id=1, source_target_pairs={{0,1},{2,3},{4,5},{6,7},{1,0},{3,2},{5,4},{7,6},{8,9},{10,11},{12,... | collective-permute-start | bytes 294920 | tf_op jit(solution)/shard_map/ppermute | solution.py:336
  26.8 0.4 collective-permute-done.2.far_ref
  27.2 0.9 %collective-permute-done.3.near_ref = f32[24,8,128]{2,1,0:T(8,128)S(1)} collective-permute-done((f32[24,8,128]{2,1,0:T(8,128)S(1)}, f32[24,8,128]{2,1,0:T(8,128)S(1)}, u32[]{:S(2)}, u32[]{:S(2)}) %collective-permute-start.3) | collective-permute-done | bytes 98336 | tf_op jit(solution)/shard_map/ppermute | solution.py:336
  28.1 32.8 %cycle.1 = (f32[256,128]{1,0:T(8,128)}, f32[256,128]{1,0:T(8,128)}) custom-call(f32[2,8,128]{2,1,0:T(8,128)S(1)} %get-tuple-element.14.eig_ref, f32[3,64,8,128]{3,2,1,0:T(8,128)S(1)} %get-tuple-element.15.tall_ref, f32[24,8,128]{2,1,0:T(8,128)S(1)} %collective-permute-done.2.far_ref, f32[24,8,128]{2,1,0:T(8,128)S(1)} %collective-permute-done.3.near_ref), custom_call_target="tpu_custom_call" | custom-call | tf_op jit(solution)/shard_map/cycle/pallas_call | solution.py:392
Async XLA Ops:
  1.8 15.1 %collective-permute-start = (f32[37,8,128]{2,1,0:T(8,128)S(1)}, f32[37,8,128]{2,1,0:T(8,128)S(1)}, u32[]{:S(2)}, u32[]{:S(2)}) collective-permute-start(f32[37,8,128]{2,1,0:T(8,128)S(1)} %get-tuple-element.12), channel_id=1, source_target_pairs={{8,16},{24,32},{40,48},{56,64},{72,80},{88,96},{104,112},{120,128}... | collective-permute-start | bytes 454664 | tf_op jit(solution)/shard_map/ppermute | solution.py:336
  13.3 6.4 %collective-permute-start.1 = (f32[37,8,128]{2,1,0:T(8,128)S(1)}, f32[37,8,128]{2,1,0:T(8,128)S(1)}, u32[]{:S(2)}, u32[]{:S(2)}) collective-permute-start(f32[37,8,128]{2,1,0:T(8,128)S(1)} %get-tuple-element.13), channel_id=1, source_target_pairs={{0,8},{16,24},{32,40},{48,56},{64,72},{80,88},{96,104},{112,120},{... | collective-permute-start | bytes 454664 | tf_op jit(solution)/shard_map/ppermute | solution.py:336
  20.0 7.2 %collective-permute-start.2 = (f32[24,8,128]{2,1,0:T(8,128)S(1)}, f32[24,8,128]{2,1,0:T(8,128)S(1)}, u32[]{:S(2)}, u32[]{:S(2)}) collective-permute-start(f32[24,8,128]{2,1,0:T(8,128)S(1)} %get-tuple-element.16), channel_id=1, source_target_pairs={{1,2},{3,4},{5,6},{2,1},{4,3},{6,5},{9,10},{11,12},{13,14},{10,9},... | collective-permute-start | bytes 294920 | tf_op jit(solution)/shard_map/ppermute | solution.py:336
  24.9 3.2 %collective-permute-start.3 = (f32[24,8,128]{2,1,0:T(8,128)S(1)}, f32[24,8,128]{2,1,0:T(8,128)S(1)}, u32[]{:S(2)}, u32[]{:S(2)}) collective-permute-start(f32[24,8,128]{2,1,0:T(8,128)S(1)} %get-tuple-element.17), channel_id=1, source_target_pairs={{0,1},{2,3},{4,5},{6,7},{1,0},{3,2},{5,4},{7,6},{8,9},{10,11},{12,... | collective-permute-start | bytes 294920 | tf_op jit(solution)/shard_map/ppermute | solution.py:336

commit v7 on v6

v7 whole, which is shorter than its diff:
```python
import functools

import jax
import jax.numpy as jnp
from jax import lax
from jax.experimental import pallas as pl
from jax.experimental.pallas import tpu as pltpu
from jax.sharding import PartitionSpec as P

CHEB = 4

CZ = 8
ROWS = 32
LANES = 128
RIM = 14
TALL = ROWS + 2 * RIM + 4
MASK_RIM = 13
RIGHT_RIM = 12
STRIP = MASK_RIM + 2 * RIGHT_RIM
SIDE = 16
SPAN = 2 * SIDE
BLOCK = TALL * SPAN // LANES
BLOCKS = LANES // SPAN
ALL = tuple(range(BLOCKS))
PACKED = BLOCK // 2
PITCH = 2 * CZ

VMEM = pl.BlockSpec(memory_space=pltpu.VMEM)
SMEM = pl.BlockSpec(memory_space=pltpu.SMEM)
HBM = pl.BlockSpec(memory_space=pltpu.HBM)


def brick_row(ref, row):
    return ref[pl.ds(row, CZ, stride=ROWS), :]


def strips_kernel(
    right_hbm, mask_hbm, helm_hbm, far_ref, near_ref, own_ref, mask_ref, helm_ref, right_ref, sem
):
    odd = lax.rem(lax.axis_index("wide"), 2)
    copies = [
        pltpu.make_async_copy(source, dest, sem.at[k])
        for k, (source, dest) in enumerate(
            ((mask_hbm, mask_ref), (helm_hbm, helm_ref), (right_hbm, right_ref))
        )
    ]
    for copy in copies:
        copy.start()
    for field, (ref, rim, offset) in enumerate(
        (
            (mask_ref, MASK_RIM, 0),
            (helm_ref, RIGHT_RIM, MASK_RIM),
            (right_ref, RIGHT_RIM, MASK_RIM + RIGHT_RIM),
        )
    ):
        copies[field].wait()
        for row in range(ROWS):
            line = brick_row(ref, row).astype(jnp.float32)
            own_ref[field, row] = line
        to_far, to_near = (ROWS - rim) * odd, (ROWS - rim) * (1 - odd)
        for row in range(rim):
            far_ref[offset + row] = own_ref[field, to_far + row]
            near_ref[offset + row] = own_ref[field, to_near + row]


def sides_kernel(
    low_ref, high_ref, own_ref, far_ref, near_ref, tall_ref, far_out, near_out, eig_ref
):
    odd = lax.rem(lax.axis_index("wide"), 2)
    odd_column = lax.rem(lax.axis_index("narrow"), 2) == 1
    eig_ref[0] = jnp.full((CZ, LANES), low_ref[0], jnp.float32)
    eig_ref[1] = jnp.full((CZ, LANES), high_ref[0], jnp.float32)
    zero = jnp.zeros((CZ, LANES), jnp.float32)
    lane = lax.broadcasted_iota(jnp.int32, (CZ, LANES), 1)
    for field, offset, rim in (
        (0, 0, MASK_RIM),
        (1, MASK_RIM, RIGHT_RIM),
        (2, MASK_RIM + RIGHT_RIM, RIGHT_RIM),
    ):
        for row in (0, 1) + tuple(range(TALL - 6, TALL)):
            tall_ref[field, row] = zero
        from_far = RIM - rim + (ROWS + rim) * odd
        from_near = RIM - rim + (ROWS + rim) * (1 - odd)
        for row in range(rim):
            tall_ref[field, from_far + row] = far_ref[offset + row]
            tall_ref[field, from_near + row] = near_ref[offset + row]
        for row in range(ROWS):
            tall_ref[field, RIM + row] = own_ref[field, row]

    block, half = lane // SPAN, lane % SPAN < SIDE
    for field in range(3):
        for i in range(BLOCK // 2):
            first, last = zero, zero
            for b in range(LANES // SPAN):
                low = tall_ref[field, BLOCK * b + i]
                low = pltpu.roll(low, SPAN * b + SIDE, 1)
                high = tall_ref[field, BLOCK * b + i + BLOCK // 2]
                high = pltpu.roll(high, SPAN * (b + 1), 1) if SPAN * (b + 1) < LANES else high
                here, after = block == b, block == (b + 1) % (LANES // SPAN)
                last = jnp.where(here, jnp.where(half, low, high), last)
                first = jnp.where(here & ~half, low, jnp.where(after & half, high, first))
            place = field * PACKED + i
            far_out[place] = jnp.where(odd_column, last, first)
            near_out[place] = jnp.where(odd_column, first, last)


def rows_loop(start, stop, chunk, step):
    count = (stop - start) // chunk
    assert count * chunk == stop - start
    if count == 1:
        step(start, chunk)
        return

    def body(index, carry):
        step(start + index * chunk, chunk)
        return carry

    lax.fori_loop(0, count, body, 0)


class Field:
    def __init__(self, main, side, height, ahead=(1, 1)):
        self.refs, self.height, self.ahead = (main, side), height, ahead

    def get(self, kind, row, shift=0):
        return self.refs[kind][row + self.ahead[kind]]

    def put(self, kind, row, value):
        self.refs[kind][row + self.ahead[kind]] = value

    def wrap(self):
        self.put(1, -1, pltpu.roll(self.get(1, self.height - 1), SPAN, 1))
        self.put(1, self.height, pltpu.roll(self.get(1, 0), LANES - SPAN, 1))


class Padded(Field):
    def get(self, kind, row, shift=0):
        return self.refs[kind][pl.ds(row * PITCH + (PITCH + CZ + shift), CZ), :]

    def put(self, kind, row, value):
        self.refs[kind][pl.ds(row * PITCH + (PITCH + CZ), CZ), :] = value

    def clear(self, reach):
        zero = jnp.zeros((CZ, LANES), jnp.float32)
        for ref, count in zip(self.refs, (self.height * BLOCKS, self.height)):
            for place in [CZ - 1 - k for k in range(reach)] + [2 * CZ + k for k in range(reach)]:
                for first in range(0, count, CZ):
                    ref[pl.ds((first + 1) * PITCH + place, CZ, stride=PITCH), :] = zero


def cycle_kernel(eig_ref, tall_ref, far_ref, near_ref, pressure_out, residual_out, *scratch):
    scratch = list(scratch)
    out_sem = scratch.pop()
    residual_ref, pressure_ref = scratch.pop(), scratch.pop()

    def fields(kind, height, count):
        return [kind(scratch.pop(0), scratch.pop(0), height) for _ in range(count)]

    wet, flow, flow_next = fields(Padded, BLOCK, 3)
    diag, base, gain, state = fields(Field, BLOCK, 4)
    wet_c, masked, masked_next = fields(Padded, BLOCK // 2, 3)
    diag_c, inverse_c, remain, error, spread = fields(Field, BLOCK // 2, 5)
    helm = Field(tall_ref.at[1], scratch.pop(0), BLOCK, (0, 1))
    rhs = Field(tall_ref.at[2], scratch.pop(0), BLOCK, (0, 1))

    lane = lax.broadcasted_iota(jnp.int32, (CZ, LANES), 1)
    level = lax.broadcasted_iota(jnp.int32, (CZ, LANES), 0)
    place = lane % SPAN
    blocks = [lane // SPAN == b for b in range(BLOCKS)]

    wet.clear(1)
    flow.clear(1)
    flow_next.clear(1)
    wet_c.clear(2)
    masked.clear(2)
    masked_next.clear(2)

    odd_column = lax.rem(lax.axis_index("narrow"), 2) == 1

    def copy_wet(row, count):
        for k in range(count):
            wet.put(0, row + k, tall_ref[0, row + k])

    rows_loop(0, TALL, 16, copy_wet)

    def unpack(i, count):
        for k in range(count):
            for index, field in enumerate((wet, helm, rhs)):
                far, near = far_ref[index * PACKED + i + k], near_ref[index * PACKED + i + k]
                right = jnp.where(odd_column, far, near)
                left = jnp.where(odd_column, near, far)
                field.put(1, i + k, jnp.where(place < SIDE, left, right))
                late = jnp.where(place < SIDE, right, left)
                field.put(1, i + k + PACKED, pltpu.roll(late, LANES - SIDE, 1))

    rows_loop(0, PACKED, 4, unpack)
    wet.wrap()

    def cells(i, chosen, height):
        return [(0, height * b + i) for b in chosen] + [(1, i)]

    def beside(mains, side, reach):
        edge = side
        found = []
        for b, main in mains:
            inner = pltpu.roll(side, (LANES - SIDE - SPAN * b) % LANES, 1)
            before = jnp.where(lane >= LANES - reach, inner, main)
            after = jnp.where(lane < reach, inner, main)
            found.append((pltpu.roll(before, reach, 1), pltpu.roll(after, LANES - reach, 1)))
            edge = jnp.where(blocks[b], pltpu.roll(main, SIDE + SPAN * b, 1), edge)
        before = jnp.where((place < SIDE) & (place >= SIDE - reach), edge, side)
        after = jnp.where((place >= SIDE) & (place < SIDE + reach), edge, side)
        found.append((pltpu.roll(before, reach, 1), pltpu.roll(after, LANES - reach, 1)))
        return found

    def near_rows(field, i, count, reach, chosen=ALL):
        lines = [[field.get(*cell) for cell in cells(i + k, chosen, field.height)] for k in (-1, 0)]
        for k in range(count):
            lines.append([field.get(*cell) for cell in cells(i + k + 1, chosen, field.height)])
            here = lines[k + 1]
            sides = beside(list(zip(chosen, here)), here[-1], reach)
            out = []
            for n, (kind, row) in enumerate(cells(i + k, chosen, field.height)):
                total = lines[k][n] + lines[k + 2][n]
                total = total + (field.get(kind, row, -reach) + field.get(kind, row, reach))
                out.append((kind, row, total + (sides[n][0] + sides[n][1])))
            yield out

    def smooth_setup(i, count):
        for group in near_rows(wet, i, count, 1):
            for kind, row, around in group:
                water = wet.get(kind, row)
                scale = water * (helm.get(kind, row) + around) + (1.0 - water)
                inverse = 0.8 / scale
                start = inverse * rhs.get(kind, row)
                diag.put(kind, row, scale)
                base.put(kind, row, start)
                gain.put(kind, row, inverse * water)
                flow.put(kind, row, water * start)

    rows_loop(0, BLOCK, 4, smooth_setup)
    flow.wrap()

    def smooth_second(i, count):
        for group in near_rows(flow, i, count, 1):
            for kind, row, near in group:
                value = 1.2 * base.get(kind, row) + gain.get(kind, row) * near
                state.put(kind, row, value)
                flow_next.put(kind, row, wet.get(kind, row) * value)

    rows_loop(0, BLOCK, 8, smooth_second)
    flow_next.wrap()

    def pair_sum(value):
        value = value + jnp.where(
            level % 2 == 0, pltpu.roll(value, CZ - 1, 0), pltpu.roll(value, 1, 0)
        )
        return value + jnp.where(
            lane % 2 == 0, pltpu.roll(value, LANES - 1, 1), pltpu.roll(value, 1, 1)
        )

    def coarse_mask(j, count):
        for k in range(count):
            for kind, row in cells(j + k, ALL, BLOCK // 2):
                total = pair_sum(wet.get(kind, 2 * row) + wet.get(kind, 2 * row + 1))
                wet_c.put(kind, row, jnp.where(total >= 3.5, 1.0, 0.0))

    rows_loop(0, BLOCK // 2, 4, coarse_mask)
    wet_c.wrap()

    low, high = eig_ref[0], eig_ref[1]
    centre = 0.5 * (high + low)
    half = 0.5 * (high - low)
    sigma = centre / half
    rho = 1.0 / sigma
    start_scale = 1.0 / centre

    def coarse_setup(j, count):
        fine_near = near_rows(flow_next, 2 * j, 2 * count, 1)
        for group in near_rows(wet_c, j, count, 2):
            sources, shifts = [0.0] * len(group), [0.0] * len(group)
            for _ in range(2):
                for n, (kind, row, near) in enumerate(next(fine_near)):
                    left_over = rhs.get(kind, row) - diag.get(kind, row) * state.get(kind, row)
                    sources[n] = sources[n] + wet.get(kind, row) * (left_over + near)
                    shifts[n] = shifts[n] + helm.get(kind, row)
            for n, (kind, row, count_c) in enumerate(group):
                source, shift = 0.125 * pair_sum(sources[n]), 0.125 * pair_sum(shifts[n])
                water_c = wet_c.get(kind, row)
                scale = water_c * (shift + 0.25 * count_c) + (1.0 - water_c)
                inverse = 1.0 / scale
                first = source * inverse * start_scale
                diag_c.put(kind, row, scale)
                inverse_c.put(kind, row, inverse)
                remain.put(kind, row, source)
                error.put(kind, row, first)
                spread.put(kind, row, first)
                masked.put(kind, row, water_c * first)

    rows_loop(0, BLOCK // 2, 2, coarse_setup)
    masked.wrap()

    direction, now, later = spread, masked, masked_next
    for sweep in range(1, CHEB):
        rho_next = 1.0 / (2.0 * sigma - rho)
        keep = rho_next * rho
        add = 2.0 * rho_next / half

        def chebyshev(j, count, sweep=sweep, keep=keep, add=add, now=now, later=later):
            for group in near_rows(now, j, count, 2):
                for kind, row, near in group:
                    old = direction.get(kind, row)
                    water_c = wet_c.get(kind, row)
                    image = diag_c.get(kind, row) * old - 0.25 * water_c * near
                    left_over = remain.get(kind, row) - image
                    fresh = keep * old + add * (left_over * inverse_c.get(kind, row))
                    error.put(kind, row, error.get(kind, row) + fresh)
                    if sweep + 1 < CHEB:
                        remain.put(kind, row, left_over)
                        direction.put(kind, row, fresh)
                        later.put(kind, row, water_c * fresh)

        rows_loop(0, BLOCK // 2, 8, chebyshev)
        if sweep + 1 < CHEB:
            later.wrap()
        rho = rho_next
        now, later = later, now

    def prolong(j, count):
        for k in range(count):
            group = cells(j + k, ALL, BLOCK // 2)
            values = [error.get(*cell) for cell in group]
            sides = beside(list(zip(ALL, values)), values[-1], 1)
            for value, pair, cell in zip(values, sides, group):
                line = 0.75 * value + 0.25 * jnp.where(lane % 2 == 0, *pair)
                other = jnp.where(
                    level % 2 == 0, pltpu.roll(line, 1, 0), pltpu.roll(line, CZ - 1, 0)
                )
                other = jnp.where((level == 0) | (level == CZ - 1), 0.0, other)
                spread.put(*cell, 0.75 * line + 0.25 * other)

    rows_loop(0, BLOCK // 2, 4, prolong)
    spread.wrap()

    def correct(chosen):
        def step(j, count):
            for k in range(count):
                for kind, row in cells(j + k, chosen, BLOCK // 2):
                    here = 0.75 * spread.get(kind, row)
                    for fine, beyond in ((2 * row, row - 1), (2 * row + 1, row + 1)):
                        water = wet.get(kind, fine)
                        value = here + 0.25 * spread.get(kind, beyond)
                        value = state.get(kind, fine) + water * value
                        state.put(kind, fine, value)
                        flow.put(kind, fine, water * value)

        return step

    rows_loop(0, 5, 5, correct((1, 2, 3)))
    rows_loop(5, BLOCK // 2, 3, correct((0, 1, 2)))
    flow.wrap()

    for now, later in ((flow, flow_next), (flow_next, flow)):

        def smooth(chosen, now=now, later=later):
            def step(i, count):
                for group in near_rows(now, i, count, 1, chosen):
                    for kind, row, near in group:
                        value = 0.2 * state.get(kind, row) + base.get(kind, row)
                        value = value + gain.get(kind, row) * near
                        state.put(kind, row, value)
                        later.put(kind, row, wet.get(kind, row) * value)

            return step

        rows_loop(0, 12, 6, smooth((1, 2)))
        rows_loop(12, BLOCK, 4, smooth((0, 1, 2)))
        later.wrap()

    def finish(chosen):
        def step(i, count):
            for group in near_rows(flow, i, count, 1, chosen):
                for kind, row, near in group[:-1]:
                    value = state.get(0, row)
                    left_over = rhs.get(0, row) - diag.get(0, row) * value
                    left_over = left_over + wet.get(0, row) * near
                    pressure_ref[pl.ds(row - RIM, CZ, stride=ROWS), :] = value
                    residual_ref[pl.ds(row - RIM, CZ, stride=ROWS), :] = left_over

        return step

    rows_loop(0, RIM, 7, finish((1, 2)))
    rows_loop(RIM, BLOCK, 2, finish((0, 1)))
    copies = (
        pltpu.make_async_copy(pressure_ref, pressure_out, out_sem.at[0]),
        pltpu.make_async_copy(residual_ref, residual_out, out_sem.at[1]),
    )
    for copy in copies:
        copy.start()
    for copy in copies:
        copy.wait()


def swapped(array, axis, first):
    pairs = [(i, i + 1) for i in range(first, lax.axis_size(axis) - 1, 2)]
    return lax.ppermute(array, axis, pairs + [(j, i) for i, j in pairs])


def in_hbm(array):
    return pltpu.with_memory_space_constraint(array, pltpu.HBM)


def f32(*shape):
    return jax.ShapeDtypeStruct(shape, jnp.float32)


def body(right_side, wet_mask, helmholtz, eig_low, eig_high):
    flat = (CZ * ROWS, LANES)
    right_flat = right_side.reshape(flat)
    mask_flat = wet_mask.reshape(flat)
    helm_flat = helmholtz.reshape(flat)
    limits = pltpu.CompilerParams(vmem_limit_bytes=24 * 1024 * 1024)

    far, near, own = pl.pallas_call(
        strips_kernel,
        out_shape=(f32(STRIP, CZ, LANES), f32(STRIP, CZ, LANES), f32(3, ROWS, CZ, LANES)),
        in_specs=[HBM] * 3,
        out_specs=(VMEM,) * 3,
        scratch_shapes=[
            pltpu.VMEM(flat, jnp.int32),
            pltpu.VMEM(flat, jnp.float32),
            pltpu.VMEM(flat, jnp.float32),
            pltpu.SemaphoreType.DMA((3,)),
        ],
        compiler_params=limits,
        name="strips",
    )(in_hbm(right_flat), in_hbm(mask_flat), in_hbm(helm_flat))
    far = swapped(far, "wide", 1)
    near = swapped(near, "wide", 0)

    tall, far, near, eigs = pl.pallas_call(
        sides_kernel,
        out_shape=(
            f32(3, TALL, CZ, LANES),
            f32(3 * PACKED, CZ, LANES),
            f32(3 * PACKED, CZ, LANES),
            f32(2, CZ, LANES),
        ),
        in_specs=[SMEM] * 2 + [VMEM] * 3,
        out_specs=(VMEM,) * 4,
        compiler_params=limits,
        name="sides",
    )(eig_low, eig_high, own, far, near)
    far = swapped(far, "narrow", 1)
    near = swapped(near, "narrow", 0)

    padded = [((rows + 3) * PITCH, LANES) for rows in (TALL, BLOCK)]
    plain = [(rows + 2, CZ, LANES) for rows in (TALL, BLOCK)]
    padded_c = [((rows // 2 + 3) * PITCH, LANES) for rows in (TALL, BLOCK)]
    plain_c = [(rows // 2 + 2, CZ, LANES) for rows in (TALL, BLOCK)]
    shapes = padded * 3 + plain * 4 + padded_c * 3 + plain_c * 5 + [plain[1]] * 2 + [flat] * 2
    pressure, residual = pl.pallas_call(
        cycle_kernel,
        out_shape=(f32(*flat),) * 2,
        in_specs=[VMEM] * 4,
        out_specs=(HBM,) * 2,
        scratch_shapes=[pltpu.VMEM(shape, jnp.float32) for shape in shapes]
        + [pltpu.SemaphoreType.DMA((2,))],
        compiler_params=limits,
        name="cycle",
    )(eigs, tall, far, near)
    shape = (CZ, ROWS, LANES)
    return pressure.reshape(shape), residual.reshape(shape)


def solution(mesh):
    field = P(None, "wide", "narrow")
    return jax.shard_map(
        body,
        mesh=mesh,
        in_specs=(field, field, field, P(), P()),
        out_specs=(field, field),
        check_vma=False,
    )
```

time: 61.1 us -> 38.8 us (0.64)
  Pallas kernels: 34.3 us -> 12 us
    pallas_call x1, Pallas kernels: 32.8 us -> 10.5 us  [body(): pl.pallas_call(cycle_kernel, out_shape=(f32(*flat),) * 2, in_specs=[VMEM]...]
where the time goes in v7:
time: 38.8 us; the launch traced here: 38.6 us
  starting transfers between devices  20.2 us (52%)
  Pallas kernels  12 us (31%)
  waiting for transfers between devices  4.42 us (11%)
  between operations  1.97 us (5%)
    ppermute x4, starting transfers between devices, swapped(): return lax.ppermute(array, axis, pairs + [(j, i) for i, j in pairs])  20.2 us
    pallas_call x1, Pallas kernels, body(): pl.pallas_call(cycle_kernel, out_shape=(f32(*flat),) * 2, in_specs=[VMEM]...  10.5 us
    ppermute x4, waiting for transfers between devices, swapped(): return lax.ppermute(array, axis, pairs + [(j, i) for i, j in pairs])  4.42 us
    pallas_call x1, Pallas kernels, body(): pl.pallas_call(strips_kernel, out_shape=(f32(STRIP, CZ, LANES), f32(STRIP...  1.21 us
  transfers between devices with their start and end apart: 4, of which 4 were waited for; matrix products, arithmetic and copies ran while one was open for 0% of the time, Pallas kernels for 0%

profile of v7, /device:TPU:57, one launch (start us, length us, event | category | flops | bytes accessed | tf_op | source)
XLA Modules:
  0.0 38.6 jit_solution(13823288835999281211)
XLA Ops:
  0.6 1.2 %strips.1 = (f32[37,8,128]{2,1,0:T(8,128)S(1)}, f32[37,8,128]{2,1,0:T(8,128)S(1)}, f32[3,32,8,128]{3,2,1,0:T(8,128)S(1)}) custom-call(f32[256,128]{1,0:T(8,128)} %bitcast.5, s32[256,128]{1,0:T(8,128)} %bitcast.6, f32[256,128]{1,0:T(8,128)} %bitcast.7), custom_call_target="tpu_custom_call" | custom-call | tf_op jit(solution)/shard_map/strips/pallas_call | solution.py:424
  1.8 11.5 %collective-permute-start = (f32[37,8,128]{2,1,0:T(8,128)S(1)}, f32[37,8,128]{2,1,0:T(8,128)S(1)}, u32[]{:S(2)}, u32[]{:S(2)}) collective-permute-start(f32[37,8,128]{2,1,0:T(8,128)S(1)} %get-tuple-element.12), channel_id=1, source_target_pairs={{8,16},{24,32},{40,48},{56,64},{72,80},{88,96},{104,112},{120,128}... | collective-permute-start | bytes 454664 | tf_op jit(solution)/shard_map/ppermute | solution.py:406
  13.3 1.9 %collective-permute-start.1 = (f32[37,8,128]{2,1,0:T(8,128)S(1)}, f32[37,8,128]{2,1,0:T(8,128)S(1)}, u32[]{:S(2)}, u32[]{:S(2)}) collective-permute-start(f32[37,8,128]{2,1,0:T(8,128)S(1)} %get-tuple-element.13), channel_id=1, source_target_pairs={{0,8},{16,24},{32,40},{48,56},{64,72},{80,88},{96,104},{112,120},{... | collective-permute-start | bytes 454664 | tf_op jit(solution)/shard_map/ppermute | solution.py:406
  16.5 0.4 %collective-permute-done.far_ref = f32[37,8,128]{2,1,0:T(8,128)S(1)} collective-permute-done((f32[37,8,128]{2,1,0:T(8,128)S(1)}, f32[37,8,128]{2,1,0:T(8,128)S(1)}, u32[]{:S(2)}, u32[]{:S(2)}) %collective-permute-start) | collective-permute-done | bytes 151584 | tf_op jit(solution)/shard_map/ppermute | solution.py:406
  17.0 2.7 %collective-permute-done.1.near_ref = f32[37,8,128]{2,1,0:T(8,128)S(1)} collective-permute-done((f32[37,8,128]{2,1,0:T(8,128)S(1)}, f32[37,8,128]{2,1,0:T(8,128)S(1)}, u32[]{:S(2)}, u32[]{:S(2)}) %collective-permute-start.1) | collective-permute-done | bytes 151584 | tf_op jit(solution)/shard_map/ppermute | solution.py:406
  19.7 0.3 sides.1
  20.0 4.9 %collective-permute-start.2 = (f32[24,8,128]{2,1,0:T(8,128)S(1)}, f32[24,8,128]{2,1,0:T(8,128)S(1)}, u32[]{:S(2)}, u32[]{:S(2)}) collective-permute-start(f32[24,8,128]{2,1,0:T(8,128)S(1)} %get-tuple-element.16), channel_id=1, source_target_pairs={{1,2},{3,4},{5,6},{2,1},{4,3},{6,5},{9,10},{11,12},{13,14},{10,9},... | collective-permute-start | bytes 294920 | tf_op jit(solution)/shard_map/ppermute | solution.py:406
  24.9 1.9 %collective-permute-start.3 = (f32[24,8,128]{2,1,0:T(8,128)S(1)}, f32[24,8,128]{2,1,0:T(8,128)S(1)}, u32[]{:S(2)}, u32[]{:S(2)}) collective-permute-start(f32[24,8,128]{2,1,0:T(8,128)S(1)} %get-tuple-element.17), channel_id=1, source_target_pairs={{0,1},{2,3},{4,5},{6,7},{1,0},{3,2},{5,4},{7,6},{8,9},{10,11},{12,... | collective-permute-start | bytes 294920 | tf_op jit(solution)/shard_map/ppermute | solution.py:406
  26.8 0.4 collective-permute-done.2.far_ref
  27.2 0.9 %collective-permute-done.3.near_ref = f32[24,8,128]{2,1,0:T(8,128)S(1)} collective-permute-done((f32[24,8,128]{2,1,0:T(8,128)S(1)}, f32[24,8,128]{2,1,0:T(8,128)S(1)}, u32[]{:S(2)}, u32[]{:S(2)}) %collective-permute-start.3) | collective-permute-done | bytes 98336 | tf_op jit(solution)/shard_map/ppermute | solution.py:406
  28.1 10.5 %cycle.1 = (f32[256,128]{1,0:T(8,128)}, f32[256,128]{1,0:T(8,128)}) custom-call(f32[2,8,128]{2,1,0:T(8,128)S(1)} %get-tuple-element.14.eig_ref, f32[3,64,8,128]{3,2,1,0:T(8,128)S(1)} %get-tuple-element.15.tall_ref, f32[24,8,128]{2,1,0:T(8,128)S(1)} %collective-permute-done.2.far_ref, f32[24,8,128]{2,1,0:T(8,128)S(1)} %collective-permute-done.3.near_ref), custom_call_target="tpu_custom_call" | custom-call | tf_op jit(solution)/shard_map/cycle/pallas_call | solution.py:462
Async XLA Ops:
  1.8 15.1 %collective-permute-start = (f32[37,8,128]{2,1,0:T(8,128)S(1)}, f32[37,8,128]{2,1,0:T(8,128)S(1)}, u32[]{:S(2)}, u32[]{:S(2)}) collective-permute-start(f32[37,8,128]{2,1,0:T(8,128)S(1)} %get-tuple-element.12), channel_id=1, source_target_pairs={{8,16},{24,32},{40,48},{56,64},{72,80},{88,96},{104,112},{120,128}... | collective-permute-start | bytes 454664 | tf_op jit(solution)/shard_map/ppermute | solution.py:406
  13.3 6.4 %collective-permute-start.1 = (f32[37,8,128]{2,1,0:T(8,128)S(1)}, f32[37,8,128]{2,1,0:T(8,128)S(1)}, u32[]{:S(2)}, u32[]{:S(2)}) collective-permute-start(f32[37,8,128]{2,1,0:T(8,128)S(1)} %get-tuple-element.13), channel_id=1, source_target_pairs={{0,8},{16,24},{32,40},{48,56},{64,72},{80,88},{96,104},{112,120},{... | collective-permute-start | bytes 454664 | tf_op jit(solution)/shard_map/ppermute | solution.py:406
  20.0 7.2 %collective-permute-start.2 = (f32[24,8,128]{2,1,0:T(8,128)S(1)}, f32[24,8,128]{2,1,0:T(8,128)S(1)}, u32[]{:S(2)}, u32[]{:S(2)}) collective-permute-start(f32[24,8,128]{2,1,0:T(8,128)S(1)} %get-tuple-element.16), channel_id=1, source_target_pairs={{1,2},{3,4},{5,6},{2,1},{4,3},{6,5},{9,10},{11,12},{13,14},{10,9},... | collective-permute-start | bytes 294920 | tf_op jit(solution)/shard_map/ppermute | solution.py:406
  24.9 3.2 %collective-permute-start.3 = (f32[24,8,128]{2,1,0:T(8,128)S(1)}, f32[24,8,128]{2,1,0:T(8,128)S(1)}, u32[]{:S(2)}, u32[]{:S(2)}) collective-permute-start(f32[24,8,128]{2,1,0:T(8,128)S(1)} %get-tuple-element.17), channel_id=1, source_target_pairs={{0,1},{2,3},{4,5},{6,7},{1,0},{3,2},{5,4},{7,6},{8,9},{10,11},{12,... | collective-permute-start | bytes 294920 | tf_op jit(solution)/shard_map/ppermute | solution.py:406

commit v8 on v7

--- a/solution.py
+++ b/solution.py
@@ -87,21 +87,24 @@
         for row in range(ROWS):
             tall_ref[field, RIM + row] = own_ref[field, row]
 
-    block, half = lane // SPAN, lane % SPAN < SIDE
-    for field in range(3):
-        for i in range(BLOCK // 2):
+    block, half = lane // SPAN, lane & (SPAN - 1) < SIDE
+
+    def pack(start, count):
+        for i, field in ((start + k, field) for k in range(count) for field in range(3)):
             first, last = zero, zero
-            for b in range(LANES // SPAN):
+            for b in range(BLOCKS):
                 low = tall_ref[field, BLOCK * b + i]
                 low = pltpu.roll(low, SPAN * b + SIDE, 1)
                 high = tall_ref[field, BLOCK * b + i + BLOCK // 2]
-                high = pltpu.roll(high, SPAN * (b + 1), 1) if SPAN * (b + 1) < LANES else high
-                here, after = block == b, block == (b + 1) % (LANES // SPAN)
+                high = pltpu.roll(high, SPAN * (b + 1), 1) if b + 1 < BLOCKS else high
+                here, after = block == b, block == (b + 1) % BLOCKS
                 last = jnp.where(here, jnp.where(half, low, high), last)
                 first = jnp.where(here & ~half, low, jnp.where(after & half, high, first))
             place = field * PACKED + i
             far_out[place] = jnp.where(odd_column, last, first)
             near_out[place] = jnp.where(odd_column, first, last)
+
+    rows_loop(0, PACKED, 4, pack)
 
 
 def rows_loop(start, stop, chunk, step):
@@ -165,8 +168,8 @@
 
     lane = lax.broadcasted_iota(jnp.int32, (CZ, LANES), 1)
     level = lax.broadcasted_iota(jnp.int32, (CZ, LANES), 0)
-    place = lane % SPAN
-    blocks = [lane // SPAN == b for b in range(BLOCKS)]
+    place = lane & (SPAN - 1)
+    spots = {1: place, 2: lax.shift_right_logical(place, 1)}
 
     wet.clear(1)
     flow.clear(1)
@@ -207,9 +210,10 @@
             before = jnp.where(lane >= LANES - reach, inner, main)
             after = jnp.where(lane < reach, inner, main)
             found.append((pltpu.roll(before, reach, 1), pltpu.roll(after, LANES - reach, 1)))
-            edge = jnp.where(blocks[b], pltpu.roll(main, SIDE + SPAN * b, 1), edge)
-        before = jnp.where((place < SIDE) & (place >= SIDE - reach), edge, side)
-        after = jnp.where((place >= SIDE) & (place < SIDE + reach), edge, side)
+            other = pltpu.roll(main, SIDE + SPAN * b, 1)
+            edge = jnp.where(lane >= SPAN * b, other, edge) if b else other
+        before = jnp.where(spots[reach] == SIDE // reach - 1, edge, side)
+        after = jnp.where(spots[reach] == SIDE // reach, edge, side)
         found.append((pltpu.roll(before, reach, 1), pltpu.roll(after, LANES - reach, 1)))
         return found
 
@@ -248,15 +252,15 @@
                 state.put(kind, row, value)
                 flow_next.put(kind, row, wet.get(kind, row) * value)
 
-    rows_loop(0, BLOCK, 8, smooth_second)
+    rows_loop(0, BLOCK, 4, smooth_second)
     flow_next.wrap()
 
     def pair_sum(value):
         value = value + jnp.where(
-            level % 2 == 0, pltpu.roll(value, CZ - 1, 0), pltpu.roll(value, 1, 0)
+            level & 1 == 0, pltpu.roll(value, CZ - 1, 0), pltpu.roll(value, 1, 0)
         )
         return value + jnp.where(
-            lane % 2 == 0, pltpu.roll(value, LANES - 1, 1), pltpu.roll(value, 1, 1)
+            lane & 1 == 0, pltpu.roll(value, LANES - 1, 1), pltpu.roll(value, 1, 1)
         )
 
     def coarse_mask(j, count):
@@ -320,7 +324,7 @@
                         direction.put(kind, row, fresh)
                         later.put(kind, row, water_c * fresh)
 
-        rows_loop(0, BLOCK // 2, 8, chebyshev)
+        rows_loop(0, BLOCK // 2, 4, chebyshev)
         if sweep + 1 < CHEB:
             later.wrap()
         rho = rho_next
@@ -332,9 +336,9 @@
             values = [error.get(*cell) for cell in group]
             sides = beside(list(zip(ALL, values)), values[-1], 1)
             for value, pair, cell in zip(values, sides, group):
-                line = 0.75 * value + 0.25 * jnp.where(lane % 2 == 0, *pair)
+                line = 0.75 * value + 0.25 * jnp.where(lane & 1 == 0, *pair)
                 other = jnp.where(
-                    level % 2 == 0, pltpu.roll(line, 1, 0), pltpu.roll(line, CZ - 1, 0)
+                    level & 1 == 0, pltpu.roll(line, 1, 0), pltpu.roll(line, CZ - 1, 0)
                 )
                 other = jnp.where((level == 0) | (level == CZ - 1), 0.0, other)
                 spread.put(*cell, 0.75 * line + 0.25 * other)

time: 38.8 us -> 36.6 us (0.943)
  Pallas kernels: 12 us -> 9.81 us
    pallas_call x1, Pallas kernels: 10.5 us -> 8.22 us  [body(): pl.pallas_call(cycle_kernel, out_shape=(f32(*flat),) * 2, in_specs=[VMEM]...]
where the time goes in v8:
time: 36.6 us; the launch traced here: 36.4 us
  starting transfers between devices  20.2 us (55%)
  Pallas kernels  9.81 us (27%)
  waiting for transfers between devices  4.42 us (12%)
  between operations  1.97 us (5%)
    ppermute x4, starting transfers between devices, swapped(): return lax.ppermute(array, axis, pairs + [(j, i) for i, j in pairs])  20.2 us
    pallas_call x1, Pallas kernels, body(): pl.pallas_call(cycle_kernel, out_shape=(f32(*flat),) * 2, in_specs=[VMEM]...  8.22 us
    ppermute x4, waiting for transfers between devices, swapped(): return lax.ppermute(array, axis, pairs + [(j, i) for i, j in pairs])  4.42 us
    pallas_call x1, Pallas kernels, body(): pl.pallas_call(strips_kernel, out_shape=(f32(STRIP, CZ, LANES), f32(STRIP...  1.21 us
  transfers between devices with their start and end apart: 4, of which 4 were waited for; matrix products, arithmetic and copies ran while one was open for 0% of the time, Pallas kernels for 0%

profile of v8, /device:TPU:57, one launch (start us, length us, event | category | flops | bytes accessed | tf_op | source)
XLA Modules:
  0.0 36.4 jit_solution(81810996878495374)
XLA Ops:
  0.6 1.2 %strips.1 = (f32[37,8,128]{2,1,0:T(8,128)S(1)}, f32[37,8,128]{2,1,0:T(8,128)S(1)}, f32[3,32,8,128]{3,2,1,0:T(8,128)S(1)}) custom-call(f32[256,128]{1,0:T(8,128)} %bitcast.5, s32[256,128]{1,0:T(8,128)} %bitcast.6, f32[256,128]{1,0:T(8,128)} %bitcast.7), custom_call_target="tpu_custom_call" | custom-call | tf_op jit(solution)/shard_map/strips/pallas_call | solution.py:428
  1.8 11.5 %collective-permute-start = (f32[37,8,128]{2,1,0:T(8,128)S(1)}, f32[37,8,128]{2,1,0:T(8,128)S(1)}, u32[]{:S(2)}, u32[]{:S(2)}) collective-permute-start(f32[37,8,128]{2,1,0:T(8,128)S(1)} %get-tuple-element.12), channel_id=1, source_target_pairs={{8,16},{24,32},{40,48},{56,64},{72,80},{88,96},{104,112},{120,128}... | collective-permute-start | bytes 454664 | tf_op jit(solution)/shard_map/ppermute | solution.py:410
  13.3 1.9 %collective-permute-start.1 = (f32[37,8,128]{2,1,0:T(8,128)S(1)}, f32[37,8,128]{2,1,0:T(8,128)S(1)}, u32[]{:S(2)}, u32[]{:S(2)}) collective-permute-start(f32[37,8,128]{2,1,0:T(8,128)S(1)} %get-tuple-element.13), channel_id=1, source_target_pairs={{0,8},{16,24},{32,40},{48,56},{64,72},{80,88},{96,104},{112,120},{... | collective-permute-start | bytes 454664 | tf_op jit(solution)/shard_map/ppermute | solution.py:410
  16.5 0.4 %collective-permute-done.far_ref = f32[37,8,128]{2,1,0:T(8,128)S(1)} collective-permute-done((f32[37,8,128]{2,1,0:T(8,128)S(1)}, f32[37,8,128]{2,1,0:T(8,128)S(1)}, u32[]{:S(2)}, u32[]{:S(2)}) %collective-permute-start) | collective-permute-done | bytes 151584 | tf_op jit(solution)/shard_map/ppermute | solution.py:410
  17.0 2.7 %collective-permute-done.1.near_ref = f32[37,8,128]{2,1,0:T(8,128)S(1)} collective-permute-done((f32[37,8,128]{2,1,0:T(8,128)S(1)}, f32[37,8,128]{2,1,0:T(8,128)S(1)}, u32[]{:S(2)}, u32[]{:S(2)}) %collective-permute-start.1) | collective-permute-done | bytes 151584 | tf_op jit(solution)/shard_map/ppermute | solution.py:410
  19.7 0.4 %sides.1 = (f32[3,64,8,128]{3,2,1,0:T(8,128)S(1)}, f32[24,8,128]{2,1,0:T(8,128)S(1)}, f32[24,8,128]{2,1,0:T(8,128)S(1)}, f32[2,8,128]{2,1,0:T(8,128)S(1)}) custom-call(f32[1]{0:T(128)S(6)} %copy.7.low_ref, f32[1]{0:T(128)S(6)} %copy.8.high_ref, f32[3,32,8,128]{3,2,1,0:T(8,128)S(1)} %get-tuple-element.11.own_ref, ...), custom_call_target="tpu_custom_call" | custom-call | tf_op jit(solution)/shard_map/sides/pallas_call | solution.py:445
  20.1 4.9 %collective-permute-start.2 = (f32[24,8,128]{2,1,0:T(8,128)S(1)}, f32[24,8,128]{2,1,0:T(8,128)S(1)}, u32[]{:S(2)}, u32[]{:S(2)}) collective-permute-start(f32[24,8,128]{2,1,0:T(8,128)S(1)} %get-tuple-element.16), channel_id=1, source_target_pairs={{1,2},{3,4},{5,6},{2,1},{4,3},{6,5},{9,10},{11,12},{13,14},{10,9},... | collective-permute-start | bytes 294920 | tf_op jit(solution)/shard_map/ppermute | solution.py:410
  25.0 1.9 %collective-permute-start.3 = (f32[24,8,128]{2,1,0:T(8,128)S(1)}, f32[24,8,128]{2,1,0:T(8,128)S(1)}, u32[]{:S(2)}, u32[]{:S(2)}) collective-permute-start(f32[24,8,128]{2,1,0:T(8,128)S(1)} %get-tuple-element.17), channel_id=1, source_target_pairs={{0,1},{2,3},{4,5},{6,7},{1,0},{3,2},{5,4},{7,6},{8,9},{10,11},{12,... | collective-permute-start | bytes 294920 | tf_op jit(solution)/shard_map/ppermute | solution.py:410
  26.9 0.4 collective-permute-done.2.far_ref
  27.2 0.9 %collective-permute-done.3.near_ref = f32[24,8,128]{2,1,0:T(8,128)S(1)} collective-permute-done((f32[24,8,128]{2,1,0:T(8,128)S(1)}, f32[24,8,128]{2,1,0:T(8,128)S(1)}, u32[]{:S(2)}, u32[]{:S(2)}) %collective-permute-start.3) | collective-permute-done | bytes 98336 | tf_op jit(solution)/shard_map/ppermute | solution.py:410
  28.1 8.2 %cycle.1 = (f32[256,128]{1,0:T(8,128)}, f32[256,128]{1,0:T(8,128)}) custom-call(f32[2,8,128]{2,1,0:T(8,128)S(1)} %get-tuple-element.14.eig_ref, f32[3,64,8,128]{3,2,1,0:T(8,128)S(1)} %get-tuple-element.15.tall_ref, f32[24,8,128]{2,1,0:T(8,128)S(1)} %collective-permute-done.2.far_ref, f32[24,8,128]{2,1,0:T(8,128)S(1)} %collective-permute-done.3.near_ref), custom_call_target="tpu_custom_call" | custom-call | tf_op jit(solution)/shard_map/cycle/pallas_call | solution.py:466
Async XLA Ops:
  1.8 15.1 %collective-permute-start = (f32[37,8,128]{2,1,0:T(8,128)S(1)}, f32[37,8,128]{2,1,0:T(8,128)S(1)}, u32[]{:S(2)}, u32[]{:S(2)}) collective-permute-start(f32[37,8,128]{2,1,0:T(8,128)S(1)} %get-tuple-element.12), channel_id=1, source_target_pairs={{8,16},{24,32},{40,48},{56,64},{72,80},{88,96},{104,112},{120,128}... | collective-permute-start | bytes 454664 | tf_op jit(solution)/shard_map/ppermute | solution.py:410
  13.3 6.4 %collective-permute-start.1 = (f32[37,8,128]{2,1,0:T(8,128)S(1)}, f32[37,8,128]{2,1,0:T(8,128)S(1)}, u32[]{:S(2)}, u32[]{:S(2)}) collective-permute-start(f32[37,8,128]{2,1,0:T(8,128)S(1)} %get-tuple-element.13), channel_id=1, source_target_pairs={{0,8},{16,24},{32,40},{48,56},{64,72},{80,88},{96,104},{112,120},{... | collective-permute-start | bytes 454664 | tf_op jit(solution)/shard_map/ppermute | solution.py:410
  20.1 7.2 %collective-permute-start.2 = (f32[24,8,128]{2,1,0:T(8,128)S(1)}, f32[24,8,128]{2,1,0:T(8,128)S(1)}, u32[]{:S(2)}, u32[]{:S(2)}) collective-permute-start(f32[24,8,128]{2,1,0:T(8,128)S(1)} %get-tuple-element.16), channel_id=1, source_target_pairs={{1,2},{3,4},{5,6},{2,1},{4,3},{6,5},{9,10},{11,12},{13,14},{10,9},... | collective-permute-start | bytes 294920 | tf_op jit(solution)/shard_map/ppermute | solution.py:410
  25.0 3.2 %collective-permute-start.3 = (f32[24,8,128]{2,1,0:T(8,128)S(1)}, f32[24,8,128]{2,1,0:T(8,128)S(1)}, u32[]{:S(2)}, u32[]{:S(2)}) collective-permute-start(f32[24,8,128]{2,1,0:T(8,128)S(1)} %get-tuple-element.17), channel_id=1, source_target_pairs={{0,1},{2,3},{4,5},{6,7},{1,0},{3,2},{5,4},{7,6},{8,9},{10,11},{12,... | collective-permute-start | bytes 294920 | tf_op jit(solution)/shard_map/ppermute | solution.py:410

commit v9 on v5

--- a/solution.py
+++ b/solution.py
@@ -13,13 +13,15 @@
 ROWS = 32
 LANES = 128
 RIM = 14
-TALL = ROWS + 2 * RIM
+TALL = ROWS + 2 * RIM + 4
 MASK_RIM = 13
 RIGHT_RIM = 12
 STRIP = MASK_RIM + 2 * RIGHT_RIM
 SIDE = 16
-GROUP = LANES // SIDE
-PACKED = 8
+SPAN = 2 * SIDE
+BLOCK = TALL * SPAN // LANES
+BLOCKS = LANES // SPAN
+PACKED = BLOCK // 2
 PITCH = 2 * CZ
 
 VMEM = pl.BlockSpec(memory_space=pltpu.VMEM)
@@ -74,7 +76,7 @@
         (1, MASK_RIM, RIGHT_RIM),
         (2, MASK_RIM + RIGHT_RIM, RIGHT_RIM),
     ):
-        for row in (0, 1, TALL - 2, TALL - 1):
+        for row in (0, 1) + tuple(range(TALL - 6, TALL)):
             tall_ref[field, row] = zero
         from_far = RIM - rim + (ROWS + rim) * odd
         from_near = RIM - rim + (ROWS + rim) * (1 - odd)
@@ -84,26 +86,24 @@
         for row in range(ROWS):
             tall_ref[field, RIM + row] = own_ref[field, row]
 
-    def pack(first_group, groups):
-        for i in range(groups):
-            group = first_group + i
-            for field in range(3):
-                first, last = [], []
-                for k in range(GROUP):
-                    line = tall_ref[field, jnp.minimum(group * GROUP + k, TALL - 1)]
-                    here = (lane >= SIDE * k) & (lane < SIDE * (k + 1))
-                    one = pltpu.roll(line, SIDE * k, 1) if k else line
-                    two = pltpu.roll(line, SIDE * (k + 1), 1) if k + 1 < GROUP else line
-                    first.append(jnp.where(here, one, 0.0))
-                    last.append(jnp.where(here, two, 0.0))
-                while len(first) > 1:
-                    first = [x + y for x, y in zip(first[::2], first[1::2])]
-                    last = [x + y for x, y in zip(last[::2], last[1::2])]
-                place = field * PACKED + group
-                far_out[place] = jnp.where(odd_column, last[0], first[0])
-                near_out[place] = jnp.where(odd_column, first[0], last[0])
-
-    rows_loop(0, PACKED, 2, pack)
+    block, half = lane // SPAN, lane & (SPAN - 1) < SIDE
+
+    def pack(start, count):
+        for i, field in ((start + k, field) for k in range(count) for field in range(3)):
+            first, last = zero, zero
+            for b in range(BLOCKS):
+                low = tall_ref[field, BLOCK * b + i]
+                low = pltpu.roll(low, SPAN * b + SIDE, 1)
+                high = tall_ref[field, BLOCK * b + i + BLOCK // 2]
+                high = pltpu.roll(high, SPAN * (b + 1), 1) if b + 1 < BLOCKS else high
+                here, after = block == b, block == (b + 1) % BLOCKS
+                last = jnp.where(here, jnp.where(half, low, high), last)
+                first = jnp.where(here & ~half, low, jnp.where(after & half, high, first))
+            place = field * PACKED + i
+            far_out[place] = jnp.where(odd_column, last, first)
+            near_out[place] = jnp.where(odd_column, first, last)
+
+    rows_loop(0, PACKED, 4, pack)
 
 
 def rows_loop(start, stop, chunk, step):
@@ -197,26 +197,25 @@
 
     odd_column = lax.rem(lax.axis_index("narrow"), 2) == 1
 
-    def unpack(first_group, groups):
-        for i in range(groups):
-            group = first_group + i
-            for field in range(3):
-                far, near = far_ref[field * PACKED + group], near_ref[field * PACKED + group]
-                after = jnp.where(odd_column, far, near)
-                ahead = pltpu.roll(jnp.where(odd_column, near, far), LANES - SIDE, 1)
-                for k in range(GROUP):
-                    row = jnp.minimum(group * GROUP + k, TALL - 1)
-                    low, high = SIDE * k, SIDE * (k + 1)
-                    beyond = (low - SIDE) % LANES
-                    both = jnp.where((lane >= beyond) & (lane < beyond + SIDE), ahead, 0.0)
-                    both = jnp.where((lane >= low) & (lane < high), after, both)
-                    if k:
-                        both = pltpu.roll(both, LANES - low, 1)
+    def unpack(start, count):
+        edges = (lane < SIDE) | (lane >= LANES - SIDE)
+        left_half = lane & (SPAN - 1) < SIDE
+        for i, field in ((start + k, field) for k in range(count) for field in range(3)):
+            far, near = far_ref[field * PACKED + i], near_ref[field * PACKED + i]
+            right = jnp.where(odd_column, far, near)
+            left = jnp.where(odd_column, near, far)
+            early = jnp.where(left_half, left, right)
+            late = jnp.where(left_half, right, left)
+            for b in range(BLOCKS):
+                low = pltpu.roll(early, LANES - SPAN * b - SIDE, 1)
+                high = pltpu.roll(late, LANES - SPAN * (b + 1), 1) if b + 1 < BLOCKS else late
+                for row, side in ((BLOCK * b + i, low), (BLOCK * b + i + PACKED, high)):
+                    side = jnp.where(edges, side, 0.0)
                     if field == 0:
                         put(wet, 0, row, tall_ref[0, row])
-                        put(wet, 1, row, both)
+                        put(wet, 1, row, side)
                     else:
-                        (helm_side, rhs_side)[field - 1][row] = both
+                        (helm_side, rhs_side)[field - 1][row] = side
 
     rows_loop(0, PACKED, 4, unpack)
 

time: 34 us -> 33.6 us (0.988)
  Pallas kernels: 7.25 us -> 6.78 us
where the time goes in v9:
time: 33.6 us; the launch traced here: 33.3 us
  starting transfers between devices  20.2 us (60%)
  Pallas kernels  6.78 us (20%)
  waiting for transfers between devices  4.42 us (13%)
  between operations  1.97 us (6%)
    ppermute x4, starting transfers between devices, swapped(): return lax.ppermute(array, axis, pairs + [(j, i) for i, j in pairs])  20.2 us
    pallas_call x1, Pallas kernels, body(): pl.pallas_call(cycle_kernel, out_shape=(f32(*flat),) * 2, in_specs=[VMEM]...  5.19 us
    ppermute x4, waiting for transfers between devices, swapped(): return lax.ppermute(array, axis, pairs + [(j, i) for i, j in pairs])  4.42 us
    pallas_call x1, Pallas kernels, body(): pl.pallas_call(strips_kernel, out_shape=(f32(STRIP, CZ, LANES), f32(STRIP...  1.21 us
  transfers between devices with their start and end apart: 4, of which 4 were waited for; matrix products, arithmetic and copies ran while one was open for 0% of the time, Pallas kernels for 0%

profile of v9, /device:TPU:57, one launch (start us, length us, event | category | flops | bytes accessed | tf_op | source)
XLA Modules:
  0.0 33.3 jit_solution(5187470732826698541)
XLA Ops:
  0.6 1.2 %strips.1 = (f32[37,8,128]{2,1,0:T(8,128)S(1)}, f32[37,8,128]{2,1,0:T(8,128)S(1)}, f32[3,32,8,128]{3,2,1,0:T(8,128)S(1)}) custom-call(f32[256,128]{1,0:T(8,128)} %bitcast.5, s32[256,128]{1,0:T(8,128)} %bitcast.6, f32[256,128]{1,0:T(8,128)} %bitcast.7), custom_call_target="tpu_custom_call" | custom-call | tf_op jit(solution)/shard_map/strips/pallas_call | solution.py:402
  1.8 11.5 %collective-permute-start = (f32[37,8,128]{2,1,0:T(8,128)S(1)}, f32[37,8,128]{2,1,0:T(8,128)S(1)}, u32[]{:S(2)}, u32[]{:S(2)}) collective-permute-start(f32[37,8,128]{2,1,0:T(8,128)S(1)} %get-tuple-element.12), channel_id=1, source_target_pairs={{8,16},{24,32},{40,48},{56,64},{72,80},{88,96},{104,112},{120,128}... | collective-permute-start | bytes 454664 | tf_op jit(solution)/shard_map/ppermute | solution.py:384
  13.3 1.9 %collective-permute-start.1 = (f32[37,8,128]{2,1,0:T(8,128)S(1)}, f32[37,8,128]{2,1,0:T(8,128)S(1)}, u32[]{:S(2)}, u32[]{:S(2)}) collective-permute-start(f32[37,8,128]{2,1,0:T(8,128)S(1)} %get-tuple-element.13), channel_id=1, source_target_pairs={{0,8},{16,24},{32,40},{48,56},{64,72},{80,88},{96,104},{112,120},{... | collective-permute-start | bytes 454664 | tf_op jit(solution)/shard_map/ppermute | solution.py:384
  16.5 0.4 %collective-permute-done.far_ref = f32[37,8,128]{2,1,0:T(8,128)S(1)} collective-permute-done((f32[37,8,128]{2,1,0:T(8,128)S(1)}, f32[37,8,128]{2,1,0:T(8,128)S(1)}, u32[]{:S(2)}, u32[]{:S(2)}) %collective-permute-start) | collective-permute-done | bytes 151584 | tf_op jit(solution)/shard_map/ppermute | solution.py:384
  17.0 2.7 %collective-permute-done.1.near_ref = f32[37,8,128]{2,1,0:T(8,128)S(1)} collective-permute-done((f32[37,8,128]{2,1,0:T(8,128)S(1)}, f32[37,8,128]{2,1,0:T(8,128)S(1)}, u32[]{:S(2)}, u32[]{:S(2)}) %collective-permute-start.1) | collective-permute-done | bytes 151584 | tf_op jit(solution)/shard_map/ppermute | solution.py:384
  19.7 0.4 %sides.1 = (f32[3,64,8,128]{3,2,1,0:T(8,128)S(1)}, f32[24,8,128]{2,1,0:T(8,128)S(1)}, f32[24,8,128]{2,1,0:T(8,128)S(1)}, f32[2,8,128]{2,1,0:T(8,128)S(1)}) custom-call(f32[1]{0:T(128)S(6)} %copy.7.low_ref, f32[1]{0:T(128)S(6)} %copy.8.high_ref, f32[3,32,8,128]{3,2,1,0:T(8,128)S(1)} %get-tuple-element.11.own_ref, ...), custom_call_target="tpu_custom_call" | custom-call | tf_op jit(solution)/shard_map/sides/pallas_call | solution.py:419
  20.1 4.9 %collective-permute-start.2 = (f32[24,8,128]{2,1,0:T(8,128)S(1)}, f32[24,8,128]{2,1,0:T(8,128)S(1)}, u32[]{:S(2)}, u32[]{:S(2)}) collective-permute-start(f32[24,8,128]{2,1,0:T(8,128)S(1)} %get-tuple-element.16), channel_id=1, source_target_pairs={{1,2},{3,4},{5,6},{2,1},{4,3},{6,5},{9,10},{11,12},{13,14},{10,9},... | collective-permute-start | bytes 294920 | tf_op jit(solution)/shard_map/ppermute | solution.py:384
  25.0 1.9 %collective-permute-start.3 = (f32[24,8,128]{2,1,0:T(8,128)S(1)}, f32[24,8,128]{2,1,0:T(8,128)S(1)}, u32[]{:S(2)}, u32[]{:S(2)}) collective-permute-start(f32[24,8,128]{2,1,0:T(8,128)S(1)} %get-tuple-element.17), channel_id=1, source_target_pairs={{0,1},{2,3},{4,5},{6,7},{1,0},{3,2},{5,4},{7,6},{8,9},{10,11},{12,... | collective-permute-start | bytes 294920 | tf_op jit(solution)/shard_map/ppermute | solution.py:384
  26.9 0.4 %collective-permute-done.2.far_ref = f32[24,8,128]{2,1,0:T(8,128)S(1)} collective-permute-done((f32[24,8,128]{2,1,0:T(8,128)S(1)}, f32[24,8,128]{2,1,0:T(8,128)S(1)}, u32[]{:S(2)}, u32[]{:S(2)}) %collective-permute-start.2) | collective-permute-done | bytes 98336 | tf_op jit(solution)/shard_map/ppermute | solution.py:384
  27.2 0.9 %collective-permute-done.3.near_ref = f32[24,8,128]{2,1,0:T(8,128)S(1)} collective-permute-done((f32[24,8,128]{2,1,0:T(8,128)S(1)}, f32[24,8,128]{2,1,0:T(8,128)S(1)}, u32[]{:S(2)}, u32[]{:S(2)}) %collective-permute-start.3) | collective-permute-done | bytes 98336 | tf_op jit(solution)/shard_map/ppermute | solution.py:384
  28.1 5.2 %cycle.1 = (f32[256,128]{1,0:T(8,128)}, f32[256,128]{1,0:T(8,128)}) custom-call(f32[2,8,128]{2,1,0:T(8,128)S(1)} %get-tuple-element.14.eig_ref, f32[3,64,8,128]{3,2,1,0:T(8,128)S(1)} %get-tuple-element.15.tall_ref, f32[24,8,128]{2,1,0:T(8,128)S(1)} %collective-permute-done.2.far_ref, f32[24,8,128]{2,1,0:T(8,128)S(1)} %collective-permute-done.3.near_ref), custom_call_target="tpu_custom_call" | custom-call | tf_op jit(solution)/shard_map/cycle/pallas_call | solution.py:435
Async XLA Ops:
  1.8 15.1 %collective-permute-start = (f32[37,8,128]{2,1,0:T(8,128)S(1)}, f32[37,8,128]{2,1,0:T(8,128)S(1)}, u32[]{:S(2)}, u32[]{:S(2)}) collective-permute-start(f32[37,8,128]{2,1,0:T(8,128)S(1)} %get-tuple-element.12), channel_id=1, source_target_pairs={{8,16},{24,32},{40,48},{56,64},{72,80},{88,96},{104,112},{120,128}... | collective-permute-start | bytes 454664 | tf_op jit(solution)/shard_map/ppermute | solution.py:384
  13.3 6.4 %collective-permute-start.1 = (f32[37,8,128]{2,1,0:T(8,128)S(1)}, f32[37,8,128]{2,1,0:T(8,128)S(1)}, u32[]{:S(2)}, u32[]{:S(2)}) collective-permute-start(f32[37,8,128]{2,1,0:T(8,128)S(1)} %get-tuple-element.13), channel_id=1, source_target_pairs={{0,8},{16,24},{32,40},{48,56},{64,72},{80,88},{96,104},{112,120},{... | collective-permute-start | bytes 454664 | tf_op jit(solution)/shard_map/ppermute | solution.py:384
  20.1 7.2 %collective-permute-start.2 = (f32[24,8,128]{2,1,0:T(8,128)S(1)}, f32[24,8,128]{2,1,0:T(8,128)S(1)}, u32[]{:S(2)}, u32[]{:S(2)}) collective-permute-start(f32[24,8,128]{2,1,0:T(8,128)S(1)} %get-tuple-element.16), channel_id=1, source_target_pairs={{1,2},{3,4},{5,6},{2,1},{4,3},{6,5},{9,10},{11,12},{13,14},{10,9},... | collective-permute-start | bytes 294920 | tf_op jit(solution)/shard_map/ppermute | solution.py:384
  25.0 3.2 %collective-permute-start.3 = (f32[24,8,128]{2,1,0:T(8,128)S(1)}, f32[24,8,128]{2,1,0:T(8,128)S(1)}, u32[]{:S(2)}, u32[]{:S(2)}) collective-permute-start(f32[24,8,128]{2,1,0:T(8,128)S(1)} %get-tuple-element.17), channel_id=1, source_target_pairs={{0,1},{2,3},{4,5},{6,7},{1,0},{3,2},{5,4},{7,6},{8,9},{10,11},{12,... | collective-permute-start | bytes 294920 | tf_op jit(solution)/shard_map/ppermute | solution.py:384

commit v10 on v9

--- a/solution.py
+++ b/solution.py
@@ -103,7 +103,7 @@
             far_out[place] = jnp.where(odd_column, last, first)
             near_out[place] = jnp.where(odd_column, first, last)
 
-    rows_loop(0, PACKED, 4, pack)
+    rows_loop(0, PACKED, 8, pack)
 
 
 def rows_loop(start, stop, chunk, step):
@@ -263,7 +263,7 @@
                 total = pair_sum(get(wet, tile, fine) + get(wet, tile, fine + 1))
                 put(wet_c, tile, row + k, jnp.where(total >= 3.5, 1.0, 0.0))
 
-    rows_loop(1, 29, 28, coarse_mask)
+    rows_loop(1, 29, 14, coarse_mask)
 
     low, high = eig_ref[0], eig_ref[1]
     centre = 0.5 * (high + low)
@@ -360,7 +360,7 @@
 
         return step
 
-    rows_loop(12, 48, 18, smooth(flow, flow_next))
+    rows_loop(12, 48, 36, smooth(flow, flow_next))
     rows_loop(13, 47, 34, smooth(flow_next, flow, True))
 
     pressure_copy = pltpu.make_async_copy(pressure_ref, pressure_out, out_sem.at[0])

time: 33.6 us -> 33.4 us (level)
  no operation moved by 1% of the time
where the time goes in v10:
time: 33.4 us; the launch traced here: 33.1 us
  starting transfers between devices  20.2 us (60%)
  Pallas kernels  6.55 us (20%)
  waiting for transfers between devices  4.42 us (13%)
  between operations  1.97 us (6%)
    ppermute x4, starting transfers between devices, swapped(): return lax.ppermute(array, axis, pairs + [(j, i) for i, j in pairs])  20.2 us
    pallas_call x1, Pallas kernels, body(): pl.pallas_call(cycle_kernel, out_shape=(f32(*flat),) * 2, in_specs=[VMEM]...  5.04 us
    ppermute x4, waiting for transfers between devices, swapped(): return lax.ppermute(array, axis, pairs + [(j, i) for i, j in pairs])  4.42 us
    pallas_call x1, Pallas kernels, body(): pl.pallas_call(strips_kernel, out_shape=(f32(STRIP, CZ, LANES), f32(STRIP...  1.21 us
  transfers between devices with their start and end apart: 4, of which 4 were waited for; matrix products, arithmetic and copies ran while one was open for 0% of the time, Pallas kernels for 0%

profile of v10, /device:TPU:57, one launch (start us, length us, event | category | flops | bytes accessed | tf_op | source)
XLA Modules:
  0.0 33.1 jit_solution(5186577512163589348)
XLA Ops:
  0.6 1.2 %strips.1 = (f32[37,8,128]{2,1,0:T(8,128)S(1)}, f32[37,8,128]{2,1,0:T(8,128)S(1)}, f32[3,32,8,128]{3,2,1,0:T(8,128)S(1)}) custom-call(f32[256,128]{1,0:T(8,128)} %bitcast.5, s32[256,128]{1,0:T(8,128)} %bitcast.6, f32[256,128]{1,0:T(8,128)} %bitcast.7), custom_call_target="tpu_custom_call" | custom-call | tf_op jit(solution)/shard_map/strips/pallas_call | solution.py:402
  1.8 11.5 %collective-permute-start = (f32[37,8,128]{2,1,0:T(8,128)S(1)}, f32[37,8,128]{2,1,0:T(8,128)S(1)}, u32[]{:S(2)}, u32[]{:S(2)}) collective-permute-start(f32[37,8,128]{2,1,0:T(8,128)S(1)} %get-tuple-element.12), channel_id=1, source_target_pairs={{8,16},{24,32},{40,48},{56,64},{72,80},{88,96},{104,112},{120,128}... | collective-permute-start | bytes 454664 | tf_op jit(solution)/shard_map/ppermute | solution.py:384
  13.3 1.9 %collective-permute-start.1 = (f32[37,8,128]{2,1,0:T(8,128)S(1)}, f32[37,8,128]{2,1,0:T(8,128)S(1)}, u32[]{:S(2)}, u32[]{:S(2)}) collective-permute-start(f32[37,8,128]{2,1,0:T(8,128)S(1)} %get-tuple-element.13), channel_id=1, source_target_pairs={{0,8},{16,24},{32,40},{48,56},{64,72},{80,88},{96,104},{112,120},{... | collective-permute-start | bytes 454664 | tf_op jit(solution)/shard_map/ppermute | solution.py:384
  16.5 0.4 %collective-permute-done.far_ref = f32[37,8,128]{2,1,0:T(8,128)S(1)} collective-permute-done((f32[37,8,128]{2,1,0:T(8,128)S(1)}, f32[37,8,128]{2,1,0:T(8,128)S(1)}, u32[]{:S(2)}, u32[]{:S(2)}) %collective-permute-start) | collective-permute-done | bytes 151584 | tf_op jit(solution)/shard_map/ppermute | solution.py:384
  17.0 2.7 %collective-permute-done.1.near_ref = f32[37,8,128]{2,1,0:T(8,128)S(1)} collective-permute-done((f32[37,8,128]{2,1,0:T(8,128)S(1)}, f32[37,8,128]{2,1,0:T(8,128)S(1)}, u32[]{:S(2)}, u32[]{:S(2)}) %collective-permute-start.1) | collective-permute-done | bytes 151584 | tf_op jit(solution)/shard_map/ppermute | solution.py:384
  19.7 0.3 sides.1
  20.0 4.9 %collective-permute-start.2 = (f32[24,8,128]{2,1,0:T(8,128)S(1)}, f32[24,8,128]{2,1,0:T(8,128)S(1)}, u32[]{:S(2)}, u32[]{:S(2)}) collective-permute-start(f32[24,8,128]{2,1,0:T(8,128)S(1)} %get-tuple-element.16), channel_id=1, source_target_pairs={{1,2},{3,4},{5,6},{2,1},{4,3},{6,5},{9,10},{11,12},{13,14},{10,9},... | collective-permute-start | bytes 294920 | tf_op jit(solution)/shard_map/ppermute | solution.py:384
  24.9 1.9 %collective-permute-start.3 = (f32[24,8,128]{2,1,0:T(8,128)S(1)}, f32[24,8,128]{2,1,0:T(8,128)S(1)}, u32[]{:S(2)}, u32[]{:S(2)}) collective-permute-start(f32[24,8,128]{2,1,0:T(8,128)S(1)} %get-tuple-element.17), channel_id=1, source_target_pairs={{0,1},{2,3},{4,5},{6,7},{1,0},{3,2},{5,4},{7,6},{8,9},{10,11},{12,... | collective-permute-start | bytes 294920 | tf_op jit(solution)/shard_map/ppermute | solution.py:384
  26.8 0.4 %collective-permute-done.2.far_ref = f32[24,8,128]{2,1,0:T(8,128)S(1)} collective-permute-done((f32[24,8,128]{2,1,0:T(8,128)S(1)}, f32[24,8,128]{2,1,0:T(8,128)S(1)}, u32[]{:S(2)}, u32[]{:S(2)}) %collective-permute-start.2) | collective-permute-done | bytes 98336 | tf_op jit(solution)/shard_map/ppermute | solution.py:384
  27.2 0.9 %collective-permute-done.3.near_ref = f32[24,8,128]{2,1,0:T(8,128)S(1)} collective-permute-done((f32[24,8,128]{2,1,0:T(8,128)S(1)}, f32[24,8,128]{2,1,0:T(8,128)S(1)}, u32[]{:S(2)}, u32[]{:S(2)}) %collective-permute-start.3) | collective-permute-done | bytes 98336 | tf_op jit(solution)/shard_map/ppermute | solution.py:384
  28.1 5.0 %cycle.1 = (f32[256,128]{1,0:T(8,128)}, f32[256,128]{1,0:T(8,128)}) custom-call(f32[2,8,128]{2,1,0:T(8,128)S(1)} %get-tuple-element.14.eig_ref, f32[3,64,8,128]{3,2,1,0:T(8,128)S(1)} %get-tuple-element.15.tall_ref, f32[24,8,128]{2,1,0:T(8,128)S(1)} %collective-permute-done.2.far_ref, f32[24,8,128]{2,1,0:T(8,128)S(1)} %collective-permute-done.3.near_ref), custom_call_target="tpu_custom_call" | custom-call | tf_op jit(solution)/shard_map/cycle/pallas_call | solution.py:435
Async XLA Ops:
  1.8 15.1 %collective-permute-start = (f32[37,8,128]{2,1,0:T(8,128)S(1)}, f32[37,8,128]{2,1,0:T(8,128)S(1)}, u32[]{:S(2)}, u32[]{:S(2)}) collective-permute-start(f32[37,8,128]{2,1,0:T(8,128)S(1)} %get-tuple-element.12), channel_id=1, source_target_pairs={{8,16},{24,32},{40,48},{56,64},{72,80},{88,96},{104,112},{120,128}... | collective-permute-start | bytes 454664 | tf_op jit(solution)/shard_map/ppermute | solution.py:384
  13.3 6.4 %collective-permute-start.1 = (f32[37,8,128]{2,1,0:T(8,128)S(1)}, f32[37,8,128]{2,1,0:T(8,128)S(1)}, u32[]{:S(2)}, u32[]{:S(2)}) collective-permute-start(f32[37,8,128]{2,1,0:T(8,128)S(1)} %get-tuple-element.13), channel_id=1, source_target_pairs={{0,8},{16,24},{32,40},{48,56},{64,72},{80,88},{96,104},{112,120},{... | collective-permute-start | bytes 454664 | tf_op jit(solution)/shard_map/ppermute | solution.py:384
  20.0 7.2 %collective-permute-start.2 = (f32[24,8,128]{2,1,0:T(8,128)S(1)}, f32[24,8,128]{2,1,0:T(8,128)S(1)}, u32[]{:S(2)}, u32[]{:S(2)}) collective-permute-start(f32[24,8,128]{2,1,0:T(8,128)S(1)} %get-tuple-element.16), channel_id=1, source_target_pairs={{1,2},{3,4},{5,6},{2,1},{4,3},{6,5},{9,10},{11,12},{13,14},{10,9},... | collective-permute-start | bytes 294920 | tf_op jit(solution)/shard_map/ppermute | solution.py:384
  24.9 3.2 %collective-permute-start.3 = (f32[24,8,128]{2,1,0:T(8,128)S(1)}, f32[24,8,128]{2,1,0:T(8,128)S(1)}, u32[]{:S(2)}, u32[]{:S(2)}) collective-permute-start(f32[24,8,128]{2,1,0:T(8,128)S(1)} %get-tuple-element.17), channel_id=1, source_target_pairs={{0,1},{2,3},{4,5},{6,7},{1,0},{3,2},{5,4},{7,6},{8,9},{10,11},{12,... | collective-permute-start | bytes 294920 | tf_op jit(solution)/shard_map/ppermute | solution.py:384
